TPU v7x, 32 devices: a whole 2x2x4 slice. The times are simulated.
32 devices in a mesh: seq: 8 (over z, core), fsdp: 4 (over y, x).
Axes of the slice: x: 2, y: 2, z: 4, core: 2. Of those that a mesh axis runs over, the one named last changes fastest.
Arguments:
- inputs: bfloat16 [2, 2048, 2048], P(None, ('seq', 'fsdp')), may hold values from -6 to 6
- segments: int32 [2, 2048], replicated, may hold values from 0 to 1, as said below
- norm1_gain: float32 [2048], replicated, may hold values from 0.5 to 1.5
- norm1_bias: float32 [2048], replicated, may hold values from -1.75 to 1.75
- qkv_weight: bfloat16 [2048, 6144], P('fsdp'), may hold values from -0.125 to 0.125
- qkv_bias: float32 [6144], replicated, may hold values from -0.625 to 0.625
- out_weight: bfloat16 [2048, 2048], P('fsdp'), may hold values from -1 to 1
- norm2_gain: float32 [2048], replicated, may hold values from 0.5 to 1.5
- norm2_bias: float32 [2048], replicated, may hold values from -1.75 to 1.75
- gate_up_weight: bfloat16 [2048, 11264], P('fsdp'), may hold values from -0.125 to 0.125
- down_weight: bfloat16 [5632, 2048], P('fsdp'), may hold values from -0.078125 to 0.078125
- cotangent: bfloat16 [2, 2048, 2048], P(None, ('seq', 'fsdp')), may hold values from -6 to 6
Outputs:
- result: float32 [2, 2048, 2048], P(None, ('seq', 'fsdp'))
- inputs_grad: float32 [2, 2048, 2048], P(None, ('seq', 'fsdp'))
- norm1_gain_grad: float32 [2048], replicated
- norm1_bias_grad: float32 [2048], replicated
- qkv_weight_grad: float32 [2048, 6144], P('fsdp')
- qkv_bias_grad: float32 [6144], replicated
- out_weight_grad: float32 [2048, 2048], P('fsdp')
- norm2_gain_grad: float32 [2048], replicated
- norm2_bias_grad: float32 [2048], replicated
- gate_up_weight_grad: float32 [2048, 11264], P('fsdp')
- down_weight_grad: float32 [5632, 2048], P('fsdp')
Inputs may be any that keep to these rules, and one draw needn't show every extreme that they name: `segments`: along each row the id is 0 and may change to 1 once, never back. One row, drawn from the seed, is all 0; in every other row the change comes at a position from 512 to 1536.
All inputs are finite; a program needn't handle non-finite values.
Results may differ from a plain program's by a relative error of at most 0.02.
Values may be sent and summed in bfloat16 or wider, within the bound.
No kernel may reach another device: no remote copies, remote signals or barrier semaphores. Data moves between devices by JAX's collectives and lax.ppermute only.
A program may use at most 640 MiB of HBM per device.

v0:
```python
import jax
import jax.numpy as jnp
from jax import lax
from jax.sharding import PartitionSpec as P

HD = 64
ROT = 16


EPSILON = 1e-05
MASKED = -1e30


def layer_norm(values, norm_gain, offset):
    average = jnp.mean(values, axis=-1, keepdims=True)
    centred = values - average
    variance = jnp.mean(centred * centred, axis=-1, keepdims=True)
    return centred * lax.rsqrt(variance + EPSILON) * norm_gain + offset


def rotate(values, positions):
    half_rot = ROT // 2
    exponent = jnp.arange(half_rot, dtype=jnp.float32) * (2.0 / ROT)
    inverse = jnp.power(jnp.float32(10000.0), -exponent)
    angles = positions.astype(jnp.float32)[:, None] * inverse[None, :]
    cosine = jnp.cos(angles)[:, None, :]
    sine = jnp.sin(angles)[:, None, :]
    first = values[:, :, :half_rot]
    second = values[:, :, half_rot:ROT]
    return jnp.concatenate(
        [first * cosine - second * sine, second * cosine + first * sine, values[:, :, ROT:]], axis=2
    )


def fold_rows(left, shard):
    return jnp.dot(
        left, lax.all_gather(shard, "fsdp", axis=0, tiled=True), preferred_element_type=jnp.float32
    )


def map_back(grad_rows, shard):
    return lax.dot_general(
        grad_rows,
        lax.all_gather(shard, "fsdp", axis=0, tiled=True),
        (((1,), (1,)), ((), ())),
        preferred_element_type=jnp.float32,
    )


def grad_joint(left, right_side):
    seq_count = lax.axis_size("seq")
    fsdp_count = lax.axis_size("fsdp")
    token_count, total_rows = left.shape
    share = total_rows // (seq_count * fsdp_count)
    permuted = (
        left.reshape(token_count, fsdp_count, seq_count, share)
        .transpose(0, 2, 1, 3)
        .reshape(token_count, total_rows)
    )
    return lax.psum_scatter(
        lax.dot_general(
            permuted, right_side, (((0,), (0,)), ((), ())), preferred_element_type=jnp.float32
        ),
        ("seq", "fsdp"),
        scatter_dimension=0,
        tiled=True,
    )


def shards(
    inputs,
    segments,
    norm1_gain,
    norm1_bias,
    qkv_weight,
    qkv_bias,
    out_weight,
    norm2_gain,
    norm2_bias,
    gate_up_weight,
    down_weight,
    cotangent,
):
    row_count, local_len, features = inputs.shape
    fsdp_count = lax.axis_size("fsdp")
    fsdp_rank = lax.axis_index("fsdp")
    block_rank = lax.axis_index("seq") * fsdp_count + fsdp_rank
    token_count = row_count * local_len
    head_count = features // HD
    ff_width = gate_up_weight.shape[1] // 2
    scale_factor = HD ** (-0.5)
    flat = inputs.reshape(token_count, features).astype(jnp.float32)
    local_pos = block_rank * local_len + jnp.arange(local_len, dtype=jnp.int32)
    positions = jnp.tile(local_pos, row_count)
    weight_set = (qkv_weight, out_weight, gate_up_weight, down_weight)

    def forward_product(left, slot_index):
        return fold_rows(left, weight_set[slot_index])

    def backward_product(grad_rows, slot_index):
        return map_back(grad_rows, weight_set[slot_index])

    normed_in, norm1_back = jax.vjp(layer_norm, flat, norm1_gain, norm1_bias)
    in_low = normed_in.astype(jnp.bfloat16)
    mixed = forward_product(in_low, 0) + qkv_bias
    turn_input = mixed[:, : 2 * features].reshape(token_count, 2 * head_count, HD)
    turned, turn_back = jax.vjp(lambda values: rotate(values, positions), turn_input)
    turned_low = turned.astype(jnp.bfloat16)
    queries = turned_low[:, :head_count].reshape(row_count, local_len, features)
    keys_loc = turned_low[:, head_count:].reshape(row_count, local_len, features)
    values_loc = (
        mixed[:, 2 * features :].astype(jnp.bfloat16).reshape(row_count, local_len, features)
    )
    head_query, head_key, head_value = (
        lax.all_to_all(queries, "seq", split_axis=2, concat_axis=1, tiled=True),
        lax.all_to_all(keys_loc, "seq", split_axis=2, concat_axis=1, tiled=True),
        lax.all_to_all(values_loc, "seq", split_axis=2, concat_axis=1, tiled=True),
    )
    all_keys, all_values = (
        lax.all_gather(head_key, "fsdp", axis=1, tiled=True),
        lax.all_gather(head_value, "fsdp", axis=1, tiled=True),
    )
    query_len = head_query.shape[1]
    key_len = all_keys.shape[1]
    head_width = head_query.shape[2]
    local_heads = head_width // HD
    query_four = head_query.reshape(row_count, query_len, local_heads, HD)
    keys_four = all_keys.reshape(row_count, key_len, local_heads, HD)
    values_four = all_values.reshape(row_count, key_len, local_heads, HD)
    query_index = jnp.arange(query_len, dtype=jnp.int32)
    query_pos = (
        query_index // local_len * fsdp_count + fsdp_rank
    ) * local_len + query_index % local_len
    key_index = jnp.arange(key_len, dtype=jnp.int32)
    key_pos = (
        key_index % query_len // local_len * fsdp_count + key_index // query_len
    ) * local_len + key_index % local_len
    query_seg = jnp.take(segments, query_pos, axis=1)
    key_seg = jnp.take(segments, key_pos, axis=1)
    span = min(512, key_len)
    block_count = key_len // span

    def block_inputs(block_index):
        first_row = block_index * span
        block_keys = lax.dynamic_slice_in_dim(keys_four, first_row, span, 1)
        block_values = lax.dynamic_slice_in_dim(values_four, first_row, span, 1)
        block_pos = lax.dynamic_slice_in_dim(key_pos, first_row, span, 0)
        block_seg = lax.dynamic_slice_in_dim(key_seg, first_row, span, 1)
        allowed = (query_seg[:, :, None] == block_seg[:, None, :]) & (
            block_pos[None, None, :] <= query_pos[None, :, None]
        )
        scores = (
            jnp.einsum(
                "rqhd,rkhd->rhqk", query_four, block_keys, preferred_element_type=jnp.float32
            )
            * scale_factor
        )
        return (first_row, block_keys, block_values, allowed[:, None], scores)

    def forward_block(carry, block_index):
        row_top, running, weighted = carry
        first_row, block_keys, block_values, allowed, scores = block_inputs(block_index)
        new_top = jnp.maximum(row_top, jnp.max(jnp.where(allowed, scores, MASKED), axis=-1))
        probs = jnp.where(allowed, jnp.exp(scores - new_top[..., None]), 0.0)
        factor = jnp.exp(row_top - new_top)
        running = running * factor + jnp.sum(probs, axis=-1)
        weighted = weighted * factor[..., None] + jnp.einsum(
            "rhqk,rkhd->rhqd",
            probs.astype(jnp.bfloat16),
            block_values,
            preferred_element_type=jnp.float32,
        )
        return ((new_top, running, weighted), None)

    start_top = jnp.full((row_count, local_heads, query_len), MASKED, jnp.float32)
    start_total = jnp.zeros((row_count, local_heads, query_len), jnp.float32)
    start_weighted = jnp.zeros((row_count, local_heads, query_len, HD), jnp.float32)
    (row_top, running, weighted), _ = lax.scan(
        forward_block, (start_top, start_total, start_weighted), jnp.arange(block_count)
    )
    log_total = row_top + jnp.log(running)
    attended_heads = (
        (weighted / running[..., None])
        .transpose(0, 2, 1, 3)
        .reshape(row_count, query_len, head_width)
        .astype(jnp.bfloat16)
    )
    attended_loc = lax.all_to_all(attended_heads, "seq", split_axis=1, concat_axis=2, tiled=True)
    att_flat = attended_loc.reshape(token_count, features)
    middle = flat + forward_product(att_flat, 1)
    normed_mid, norm2_back = jax.vjp(layer_norm, middle, norm2_gain, norm2_bias)
    mid_low = normed_mid.astype(jnp.bfloat16)
    gate_up = forward_product(mid_low, 2)
    act_value, silu_back = jax.vjp(
        lambda gate_part, up_part: jax.nn.silu(gate_part) * up_part,
        gate_up[:, :ff_width],
        gate_up[:, ff_width:],
    )
    act_low = act_value.astype(jnp.bfloat16)
    result = middle + forward_product(act_low, 3)
    d_out = cotangent.reshape(token_count, features)
    d_act = backward_product(d_out, 3)
    d_gate, d_up = silu_back(d_act)
    d_gate_up = jnp.concatenate([d_gate, d_up], axis=1).astype(jnp.bfloat16)
    d_mid_norm = backward_product(d_gate_up, 2)
    d_middle_part, d_gain_two, d_bias_two = norm2_back(d_mid_norm)
    d_middle = d_out.astype(jnp.float32) + d_middle_part
    d_branch = d_middle.astype(jnp.bfloat16)
    d_attended = (
        backward_product(d_branch, 1).astype(jnp.bfloat16).reshape(row_count, local_len, features)
    )
    d_heads = lax.all_to_all(d_attended, "seq", split_axis=2, concat_axis=1, tiled=True)
    d_heads_four = d_heads.reshape(row_count, query_len, local_heads, HD)
    attended_four = attended_heads.reshape(row_count, query_len, local_heads, HD)
    delta = jnp.einsum(
        "rqhd,rqhd->rhq", d_heads_four.astype(jnp.float32), attended_four.astype(jnp.float32)
    )

    def backward_block(carry, block_index):
        d_query, d_keys_all, d_values_all = carry
        first_row, block_keys, block_values, allowed, scores = block_inputs(block_index)
        probs = jnp.where(allowed, jnp.exp(scores - log_total[..., None]), 0.0)
        d_block_values = jnp.einsum(
            "rhqk,rqhd->rkhd",
            probs.astype(jnp.bfloat16),
            d_heads_four,
            preferred_element_type=jnp.float32,
        )
        d_probs = jnp.einsum(
            "rqhd,rkhd->rhqk", d_heads_four, block_values, preferred_element_type=jnp.float32
        )
        d_scores = (probs * (d_probs - delta[..., None])).astype(jnp.bfloat16)
        d_query = (
            d_query
            + jnp.einsum(
                "rhqk,rkhd->rqhd", d_scores, block_keys, preferred_element_type=jnp.float32
            )
            * scale_factor
        )
        d_block_keys = (
            jnp.einsum("rhqk,rqhd->rkhd", d_scores, query_four, preferred_element_type=jnp.float32)
            * scale_factor
        )
        d_keys_all = lax.dynamic_update_slice_in_dim(d_keys_all, d_block_keys, first_row, 1)
        d_values_all = lax.dynamic_update_slice_in_dim(d_values_all, d_block_values, first_row, 1)
        return ((d_query, d_keys_all, d_values_all), None)

    zero_query = jnp.zeros((row_count, query_len, local_heads, HD), jnp.float32)
    zero_keys = jnp.zeros((row_count, key_len, local_heads, HD), jnp.float32)
    (d_query, d_keys_all, d_values_all), _ = lax.scan(
        backward_block, (zero_query, zero_keys, zero_keys), jnp.arange(block_count)
    )
    d_keys_sum, d_values_sum = (
        lax.psum_scatter(
            d_keys_all.reshape(row_count, key_len, head_width).astype(jnp.bfloat16),
            "fsdp",
            scatter_dimension=1,
            tiled=True,
        ).astype(jnp.float32),
        lax.psum_scatter(
            d_values_all.reshape(row_count, key_len, head_width).astype(jnp.bfloat16),
            "fsdp",
            scatter_dimension=1,
            tiled=True,
        ).astype(jnp.float32),
    )
    d_query_low = d_query.reshape(row_count, query_len, head_width).astype(jnp.bfloat16)
    dq_back, dk_back, dv_back = (
        lax.all_to_all(d_query_low, "seq", split_axis=1, concat_axis=2, tiled=True),
        lax.all_to_all(
            d_keys_sum.astype(jnp.bfloat16), "seq", split_axis=1, concat_axis=2, tiled=True
        ),
        lax.all_to_all(
            d_values_sum.astype(jnp.bfloat16), "seq", split_axis=1, concat_axis=2, tiled=True
        ),
    )
    d_turned = jnp.concatenate(
        [
            dq_back.reshape(token_count, head_count, HD),
            dk_back.reshape(token_count, head_count, HD),
        ],
        axis=1,
    ).astype(jnp.float32)
    (d_turn_input,) = turn_back(d_turned)
    d_mixed = jnp.concatenate(
        [
            d_turn_input.reshape(token_count, 2 * features),
            dv_back.reshape(token_count, features).astype(jnp.float32),
        ],
        axis=1,
    ).astype(jnp.bfloat16)
    d_qkv_bias = jnp.sum(d_mixed.astype(jnp.float32), axis=0)
    d_norm_in = backward_product(d_mixed, 0)
    d_flat_part, d_gain_one, d_bias_one = norm1_back(d_norm_in)
    d_inputs = d_middle + d_flat_part
    first_grad = grad_joint(in_low, d_mixed)
    second_grad = grad_joint(att_flat, d_branch)
    third_grad = grad_joint(mid_low, d_gate_up)
    fourth_grad = grad_joint(act_low, d_out)
    qkv_grad, out_grad, gate_up_grad, down_grad = (
        lax.all_gather(first_grad.astype(jnp.bfloat16), "seq", axis=0, tiled=True).astype(
            first_grad.dtype
        ),
        lax.all_gather(second_grad.astype(jnp.bfloat16), "seq", axis=0, tiled=True).astype(
            second_grad.dtype
        ),
        lax.all_gather(third_grad.astype(jnp.bfloat16), "seq", axis=0, tiled=True).astype(
            third_grad.dtype
        ),
        lax.all_gather(fourth_grad.astype(jnp.bfloat16), "seq", axis=0, tiled=True).astype(
            fourth_grad.dtype
        ),
    )
    gain_one, bias_one, bias_qkv, gain_two, bias_two = lax.psum(
        (d_gain_one, d_bias_one, d_qkv_bias, d_gain_two, d_bias_two), ("seq", "fsdp")
    )
    return (
        result.reshape(row_count, local_len, features),
        d_inputs.reshape(row_count, local_len, features),
        gain_one,
        bias_one,
        qkv_grad,
        bias_qkv,
        out_grad,
        gain_two,
        bias_two,
        gate_up_grad,
        down_grad,
    )


def solution(mesh):
    placed = (
        P(None, ("seq", "fsdp"), None),
        P(),
        P(),
        P(),
        P("fsdp", None),
        P(),
        P("fsdp", None),
        P(),
        P(),
        P("fsdp", None),
        P("fsdp", None),
        P(None, ("seq", "fsdp"), None),
    )
    return jax.shard_map(
        shards,
        mesh=mesh,
        in_specs=placed,
        out_specs=(
            P(None, ("seq", "fsdp"), None),
            P(None, ("seq", "fsdp"), None),
            P(),
            P(),
            P("fsdp", None),
            P(),
            P("fsdp", None),
            P(),
            P(),
            P("fsdp", None),
            P("fsdp", None),
        ),
        check_vma=False,
    )
```

profile of v0, /device:TPU:0, one launch (start us, length us, event | category | flops | bytes accessed | tf_op | source)
XLA Modules:
  0.0 5300.9 jit_solution(8290319464417667051)
XLA Ops:
  10.9 229.5 %all-gather.11.cloned.1.call-done = bf16[2048,6144]{1,0:T(8,128)(2,1)} async-done(((bf16[512,6144]{1,0:T(8,128)(2,1)}), bf16[2048,6144]{1,0:T(8,128)(2,1)}) %all-gather.11.cloned.1.call-update) | async-done | bytes 25165840 | tf_op jit(solution)/shard_map/all_gather | solution.py:37
  265.7 20.1 all_to_all.120
  297.0 17.8 all_to_all.121
  346.6 17.6 all-gather.15.cloned.1.call-done
  368.1 70.0 %while.30 = (s32[]{:T(128)}, f32[2,4,512]{2,1,0:T(4,128)S(1)}, f32[2,4,512]{2,1,0:T(4,128)S(1)}, f32[2,4,512,64]{2,3,1,0:T(8,128)}, s32[2,512]{1,0:T(2,128)S(1)}...) while((s32[]{:T(128)}, f32[2,4,512]{2,1,0:T(4,128)S(1)}, ...), condition=%wide.region_5.6_spmd.clone, body=%wide.region_2.5_spmd.clone.sunk | while | flops 562065408 | bytes 65300752 | solution.py:178
  475.3 382.1 %all-gather.19.cloned.1.call-done = bf16[2048,11264]{1,0:T(8,128)(2,1)} async-done(((bf16[512,11264]{1,0:T(8,128)(2,1)}), bf16[2048,11264]{1,0:T(8,128)(2,1)}) %all-gather.19.cloned.1.call-update) | async-done | bytes 46137360 | tf_op jit(solution)/shard_map/all_gather | solution.py:37
  857.4 24.5 fusion.132
  881.9 187.7 %all-gather.21.cloned.1.call-done = bf16[5632,2048]{1,0:T(8,128)(2,1)} async-done(((bf16[1408,2048]{1,0:T(8,128)(2,1)}), bf16[5632,2048]{1,0:T(8,128)(2,1)}) %all-gather.21.cloned.1.call-update) | async-done | bytes 23068688 | tf_op jit(solution)/shard_map/all_gather | solution.py:37
  1069.6 15.5 fusion.71
  1085.0 23.1 multiply_reduce_fusion
  1154.8 83.9 %while.31 = (s32[]{:T(128)}, f32[2,512,4,64]{1,3,2,0:T(8,128)}, bf16[2,2048,4,64]{1,3,2,0:T(8,128)(2,1)}, bf16[2,2048,4,64]{1,3,2,0:T(8,128)(2,1)}, s32[4]{0:T(1...) while((s32[]{:T(128)}, f32[2,512,4,64]{1,3,2,0:T(8,128)}, ...), condition=%wide.region_11.12_spmd.clone, body=%wide.region_10.11_spmd.clone.sunk | while | flops 1365516288 | bytes 137963984 | solution.py:250
  1255.9 16.2 reduce-scatter.9.cloned.1.call-done
  1278.9 31.7 reduce-scatter.7.cloned.1.call-done
  1339.4 19.9 fusion.78
  1363.8 18.0 fusion.134
  1383.2 34.0 fusion.73
  1417.3 253.7 %reduce-scatter.13.cloned.1.call-done = f32[64,2048]{1,0:T(8,128)} async-done(((f32[2048,2048]{1,0:T(8,128)}), f32[64,2048]{1,0:T(8,128)}) %reduce-scatter.13.cloned.1.call-update) | async-done | bytes 524304 | tf_op jit(solution)/shard_map/reduce_scatter | solution.py:60
  1672.9 437.4 %reduce-scatter.11.cloned.1.call-done = f32[64,6144]{1,0:T(8,128)} async-done(((f32[2048,6144]{1,0:T(8,128)}), f32[64,6144]{1,0:T(8,128)}) %reduce-scatter.11.cloned.1.call-update) | async-done | bytes 1572880 | tf_op jit(solution)/shard_map/reduce_scatter | solution.py:60
  2112.7 967.5 %reduce-scatter.17.cloned.1.call-done = f32[176,2048]{1,0:T(8,128)} async-done(((f32[5632,2048]{1,0:T(8,128)}), f32[176,2048]{1,0:T(8,128)}) %reduce-scatter.17.cloned.1.call-update) | async-done | bytes 1441808 | tf_op jit(solution)/shard_map/reduce_scatter | solution.py:60
  3082.9 1928.2 %reduce-scatter.15.cloned.1.call-done = f32[64,11264]{1,0:T(8,128)} async-done(((f32[2048,11264]{1,0:T(8,128)}), f32[64,11264]{1,0:T(8,128)}) %reduce-scatter.15.cloned.1.call-update) | async-done | bytes 2883600 | tf_op jit(solution)/shard_map/reduce_scatter | solution.py:60
  5026.9 17.5 fusion.128
  5046.2 46.0 all-reduce.3
  5121.4 51.1 all-gather.29.cloned.1.call-done
  5181.2 100.1 %all-gather.27.cloned.1.call-done = bf16[512,11264]{1,0:T(8,128)(2,1)} async-done(((bf16[64,11264]{1,0:T(8,128)(2,1)}), bf16[512,11264]{1,0:T(8,128)(2,1)}) %all-gather.27.cloned.1.call-update) | async-done | bytes 11534352 | tf_op jit(solution)/shard_map/all_gather | solution.py:307
  (401 shorter events, 441.0 us)
Async XLA Ops:
  7.2 233.1 %all-gather.11.cloned.1.call-start = ((), (), s32[]{:S(2)}) async-start(), calls=%async_computation.14 | async-start | bytes 31457280 | tf_op jit(solution)/shard_map/all_gather | solution.py:37
  8.0 335.7 %all-gather.13.cloned.1.call-start = ((), (), s32[]{:S(2)}) async-start(), calls=%async_computation.15 | async-start | bytes 2621440 | tf_op jit(solution)/shard_map/all_gather | solution.py:120
  293.0 71.2 %all-gather.15.cloned.1.call-start = ((), (), s32[]{:S(2)}) async-start(), calls=%async_computation.16 | async-start | bytes 2621440 | tf_op jit(solution)/shard_map/all_gather | solution.py:121
  317.3 148.3 %all-gather.17.cloned.1.call-start = ((), (), s32[]{:S(2)}) async-start(), calls=%async_computation.17 | async-start | bytes 10485760 | tf_op jit(solution)/shard_map/all_gather | solution.py:37
  317.9 539.5 %all-gather.19.cloned.1.call-start = ((), (), s32[]{:S(2)}) async-start(), calls=%async_computation.18 | async-start | bytes 57671680 | tf_op jit(solution)/shard_map/all_gather | solution.py:37
  318.5 751.1 %all-gather.21.cloned.1.call-start = ((), (), s32[]{:S(2)}) async-start(), calls=%async_computation.19 | async-start | bytes 28835840 | tf_op jit(solution)/shard_map/all_gather | solution.py:37
  322.9 18.8 all-to-all-start.1
  442.3 20.6 all-to-all-start.3
  475.3 406.6 %copy-start.13 = (bf16[128,2048]{1,0:T(8,128)(2,1)}, bf16[128,2048]{1,0:T(8,128)(2,1)S(1)}, u32[]{:S(2)}) copy-start(bf16[128,2048]{1,0:T(8,128)(2,1)S(1)} %add_convert_fusion.2) | copy-start | bytes 1572868
  1123.6 20.0 all-to-all-start.4
  1128.3 143.9 %reduce-scatter.9.cloned.1.call-start = ((), (), s32[]{:S(2)}) async-start(), calls=%async_computation.21 | async-start | bytes 2621440 | tf_op jit(solution)/shard_map/reduce_scatter | solution.py:260
  1238.8 71.7 %reduce-scatter.7.cloned.1.call-start = ((), (), s32[]{:S(2)}) async-start(), calls=%async_computation.20 | async-start | bytes 2621440 | tf_op jit(solution)/shard_map/reduce_scatter | solution.py:254
  1239.6 431.4 %reduce-scatter.13.cloned.1.call-start = ((), (), s32[]{:S(2)}) async-start(), calls=%async_computation.24 | async-start | bytes 17301504 | tf_op jit(solution)/shard_map/reduce_scatter | solution.py:60
  1252.3 21.8 all-to-all-start.5
  1274.1 38.4 all-to-all-start.7
  1312.5 22.6 all-to-all-start.6
  1317.1 793.1 %reduce-scatter.11.cloned.1.call-start = ((), (), s32[]{:S(2)}) async-start(), calls=%async_computation.22 | async-start | bytes 51904512 | tf_op jit(solution)/shard_map/reduce_scatter | solution.py:60
  1359.2 1721.0 %reduce-scatter.17.cloned.1.call-start = ((), (), s32[]{:S(2)}) async-start(), calls=%async_computation.28 | async-start | bytes 47579136 | tf_op jit(solution)/shard_map/reduce_scatter | solution.py:60
  1381.9 3629.2 %reduce-scatter.15.cloned.1.call-start = ((), (), s32[]{:S(2)}) async-start(), calls=%async_computation.26 | async-start | bytes 95158272 | tf_op jit(solution)/shard_map/reduce_scatter | solution.py:60
  1417.2 3677.8 %all-gather.25.cloned.1.call-start = ((), (), s32[]{:S(2)}) async-start(), calls=%async_computation.25 | async-start | bytes 2359296 | tf_op jit(solution)/shard_map/all_gather | solution.py:304
  1672.8 3439.0 %all-gather.23.cloned.1.call-start = ((), (), s32[]{:S(2)}) async-start(), calls=%async_computation.23 | async-start | bytes 7077888 | tf_op jit(solution)/shard_map/all_gather | solution.py:301
  2112.7 3059.8 %all-gather.29.cloned.1.call-start = ((), (), s32[]{:S(2)}) async-start(), calls=%async_computation.29 | async-start | bytes 6488064 | tf_op jit(solution)/shard_map/all_gather | solution.py:310
  3082.6 1931.5 %copy-start.6 = (f32[128,2048]{1,0:T(8,128)S(1)}, f32[128,2048]{1,0:T(8,128)}, u32[]{:S(2)}) copy-start(f32[128,2048]{1,0:T(8,128)} %copy-done.5) | copy-start | bytes 3145732
  3082.6 2198.6 %all-gather.27.cloned.1.call-start = ((), (), s32[]{:S(2)}) async-start(), calls=%async_computation.27 | async-start | bytes 12976128 | tf_op jit(solution)/shard_map/all_gather | solution.py:307
  (66 other events, 1438.1 us)
Sparse Core Ops, SparseCore 0:
  9.9 230.3 all-gather.10
  293.1 33.2 all-gather.12
  328.8 35.2 all-gather.14
  365.9 87.5 all-gather.16
  455.2 402.0 all-gather.18
  859.1 210.4 all-gather.20
  1238.9 33.1 reduce-scatter.8
  1275.3 35.1 reduce-scatter.6
  1313.4 357.5 reduce-scatter.12
  1677.3 432.9 reduce-scatter.10
  2112.6 967.6 reduce-scatter.16
  3082.5 1928.5 reduce-scatter.14
  5013.3 31.2 all-gather.24
  5046.6 65.1 all-gather.22
  5113.3 59.1 all-gather.28
  5174.5 106.7 all-gather.26
where the time goes:
time: 5310 us; the launch traced here: 5300 us
  waiting for transfers between devices  4660 us (88%)
  matrix products  311 us (6%)
  local copies, waits for them, and re-layouts  104 us (2%)
  other arithmetic  89.9 us (2%)
  blocking collectives  83.8 us (2%)
    reduce_scatter x4, waiting for transfers between devices, grad_joint(): lax.psum_scatter(lax.dot_general(permuted, right_side, (((0,), (0,)), (()...  3590 us
    all_gather x4, waiting for transfers between devices, fold_rows(): lax.all_gather(shard, 'fsdp', axis=0, tiled=True)  799 us
  transfers between devices with their start and end apart: 22, of which 17 were waited for; matrix products, arithmetic and copies ran while one was open for 6% of the time, Pallas kernels for 0%

commit v1 on v0

--- a/solution.py
+++ b/solution.py
@@ -1,6 +1,8 @@
 import jax
 import jax.numpy as jnp
 from jax import lax
+from jax.experimental import pallas as pl
+from jax.experimental.pallas import tpu as pltpu
 from jax.sharding import PartitionSpec as P
 
 HD = 64
@@ -67,7 +69,7 @@
     )
 
 
-def shards(
+def general_plan(
     inputs,
     segments,
     norm1_gain,
@@ -329,6 +331,573 @@
     )
 
 
+BLOCK = 512
+BF = jnp.bfloat16
+F32 = jnp.float32
+
+
+def swap(value, mask):
+    return lax.ppermute(value, ("seq", "fsdp"), [(i, i ^ mask) for i in range(32)])
+
+
+def shift(value, steps):
+    return lax.ppermute(value, ("seq", "fsdp"), [(i, (i + 8 * steps) % 32) for i in range(32)])
+
+
+def pick(stacked, index):
+    return lax.dynamic_index_in_dim(stacked, index, 0, keepdims=False)
+
+
+def unswap(pieces, rank):
+    stacked = jnp.stack(pieces) if isinstance(pieces, (list, tuple)) else pieces
+    return jnp.stack([pick(stacked, j ^ rank) for j in range(stacked.shape[0])])
+
+
+def gather_quad(value):
+    half = value.shape[0] // 2
+    by_x = swap(value, 1)
+    by_y = swap(value, 2)
+    low_part = swap(by_x[:half], 2)
+    high_part = swap(by_y[half:], 1)
+    return jnp.concatenate([value, by_x, by_y, low_part, high_part], axis=0)
+
+
+def gather_plane(value):
+    quad = gather_quad(value)
+    return quad, swap(quad, 4)
+
+
+def sum_quad(blocks):
+    return (
+        blocks[0].astype(F32)
+        + swap(blocks[1].astype(BF), 1).astype(F32)
+        + swap(blocks[2].astype(BF), 2).astype(F32)
+        + swap(blocks[3].astype(BF), 3).astype(F32)
+    )
+
+
+def sum_plane(near, far):
+    arrived = swap(far.astype(BF), 4).astype(F32)
+    total = near.astype(F32) + arrived
+    return sum_quad([total[m] for m in range(4)])
+
+
+def sum_all(value):
+    for mask in (4, 1, 2, 8, 16):
+        value = value + swap(value, mask)
+    return value
+
+
+def dot(left, right):
+    return jnp.dot(left, right, preferred_element_type=F32)
+
+
+def dot_rows(left, right):
+    return lax.dot_general(left, right, (((1,), (1,)), ((), ())), preferred_element_type=F32)
+
+
+def dot_cols(left, right):
+    return lax.dot_general(left, right, (((0,), (0,)), ((), ())), preferred_element_type=F32)
+
+
+def turn_tables(row_len):
+    half_rot = ROT // 2
+    lane = jnp.arange(2 * HD, dtype=jnp.int32) % HD
+    exponent = (lane % half_rot).astype(F32) * (2.0 / ROT)
+    inverse = jnp.power(jnp.float32(10000.0), -exponent)
+    angles = jnp.arange(row_len, dtype=jnp.int32).astype(F32)[:, None] * inverse[None, :]
+    cosine = jnp.where(lane < ROT, jnp.cos(angles), 1.0)
+    sine = jnp.sin(angles)
+    ahead = jnp.where(lane < half_rot, -sine, 0.0)
+    behind = jnp.where((lane >= half_rot) & (lane < ROT), sine, 0.0)
+    return cosine, ahead, behind
+
+
+def attend_kernel(
+    place_ref, split_ref, mixed_ref, cos_ref, ahead_ref, behind_ref,
+    q_ref, k_ref, v_ref, o_ref, log_ref, kz, vz,
+):
+    local_len = mixed_ref.shape[2]
+    row_len = q_ref.shape[0]
+    low = lax.broadcasted_iota(jnp.int32, (local_len, 2 * HD), 1) < HD
+
+    def prepare(i, carry):
+        rows = pl.ds(pl.multiple_of(i * local_len, local_len), local_len)
+        source = place_ref[i]
+        cosine, ahead, behind = cos_ref[rows], ahead_ref[rows], behind_ref[rows]
+
+        def turn(x):
+            return (
+                x * cosine
+                + pltpu.roll(x, 2 * HD - ROT // 2, 1) * ahead
+                + pltpu.roll(x, ROT // 2, 1) * behind
+            )
+
+        first = mixed_ref[source, 0]
+        second = mixed_ref[source, 1]
+        turned0 = turn(first[:, : 2 * HD])
+        turned1 = turn(second[:, : 2 * HD])
+        q = jnp.where(low, turned0, pltpu.roll(turned1, HD, 1))
+        k = jnp.where(low, pltpu.roll(turned0, HD, 1), turned1)
+        v = jnp.where(low, first[:, 2 * HD :], second[:, 2 * HD :])
+        q_ref[rows] = (q * HD**-0.5).astype(BF)
+        k_ref[rows] = k.astype(BF)
+        v_ref[rows] = v.astype(BF)
+        kz[0, rows] = jnp.where(low, k, 0.0).astype(BF)
+        kz[1, rows] = jnp.where(low, 0.0, k).astype(BF)
+        vz[0, rows] = jnp.where(low, v, 0.0).astype(BF)
+        vz[1, rows] = jnp.where(low, 0.0, v).astype(BF)
+        return carry
+
+    lax.fori_loop(0, row_len // local_len, prepare, 0)
+    t_in = lax.broadcasted_iota(jnp.int32, (BLOCK, 1), 0)
+    u_in = lax.broadcasted_iota(jnp.int32, (1, BLOCK), 1)
+    low_q = lax.broadcasted_iota(jnp.int32, (BLOCK, 2 * HD), 1) < HD
+
+    def query_block(qb, carry):
+        rows = pl.ds(pl.multiple_of(qb * BLOCK, BLOCK), BLOCK)
+        q = q_ref[rows]
+        t = t_in + qb * BLOCK
+        outs, logs = [], []
+        for row in range(2):
+            split = split_ref[row]
+            start = jnp.where(t >= split, split, 0)
+
+            def step(kb, state, diagonal, row=row, start=start):
+                top, total, acc = state
+                keys = pl.ds(pl.multiple_of(kb * BLOCK, BLOCK), BLOCK)
+                u = u_in + kb * BLOCK
+                scores = dot_rows(q, kz[row, keys])
+                allowed = u >= start
+                if diagonal:
+                    allowed = allowed & (u <= t)
+                scores = jnp.where(allowed, scores, MASKED)
+                new_top = jnp.maximum(top, jnp.max(scores, axis=1, keepdims=True))
+                probs = jnp.exp(scores - new_top)
+                factor = jnp.exp(top - new_top)
+                total = total * factor + jnp.sum(probs, axis=1, keepdims=True)
+                acc = acc * factor + dot(probs.astype(BF), vz[row, keys])
+                return new_top, total, acc
+
+            state = (
+                jnp.full((BLOCK, 1), MASKED, F32),
+                jnp.zeros((BLOCK, 1), F32),
+                jnp.zeros((BLOCK, 2 * HD), F32),
+            )
+            first_kb = jnp.where(qb * BLOCK >= split, split // BLOCK, 0)
+            state = lax.fori_loop(
+                first_kb, qb, lambda kb, state, step=step: step(kb, state, False), state
+            )
+            top, total, acc = step(qb, state, True)
+            outs.append(acc / total)
+            logs.append(top + jnp.log(total))
+        o_ref[rows] = (outs[0] + outs[1]).astype(BF)
+        log_ref[rows] = jnp.where(low_q, logs[0], logs[1])
+        return carry
+
+    lax.fori_loop(0, row_len // BLOCK, query_block, 0)
+
+
+def attend(place, split, mixed, tables):
+    row_len = tables[0].shape[0]
+    packed = jax.ShapeDtypeStruct((row_len, 2 * HD), BF)
+    smem = pl.BlockSpec(memory_space=pltpu.SMEM)
+    vmem = pl.BlockSpec(memory_space=pltpu.VMEM)
+    pairs = 2 * row_len * row_len // 2
+    return pl.pallas_call(
+        attend_kernel,
+        out_shape=(packed, packed, packed, packed, jax.ShapeDtypeStruct((row_len, 2 * HD), F32)),
+        in_specs=[smem, smem, vmem, vmem, vmem, vmem],
+        out_specs=(vmem,) * 5,
+        scratch_shapes=[pltpu.VMEM((2, row_len, 2 * HD), BF), pltpu.VMEM((2, row_len, 2 * HD), BF)],
+        compiler_params=pltpu.CompilerParams(vmem_limit_bytes=48 * 2**20),
+        cost_estimate=pl.CostEstimate(
+            flops=16 * pairs * HD, bytes_accessed=12 * 2**20, transcendentals=pairs
+        ),
+        name="attend",
+    )(place, split, mixed, *tables)
+
+
+def attend_back_kernel(
+    place_ref, split_ref, q_ref, k_ref, v_ref, kt_ref, o_ref, do_ref, log_ref,
+    cos_ref, ahead_ref, behind_ref,
+    dmix_ref, dpos_ref, kz, vz, qz, dz, ktz, delta, dq_t, dk, dv,
+):
+    row_len = q_ref.shape[0]
+    local_len = dmix_ref.shape[2]
+    low = lax.broadcasted_iota(jnp.int32, (BLOCK, 2 * HD), 1) < HD
+    low_t = lax.broadcasted_iota(jnp.int32, (2 * HD, BLOCK), 0) < HD
+    lane = lax.broadcasted_iota(jnp.int32, (8, 2 * HD), 1)
+    ones = [jnp.where(lane < HD, 1.0, 0.0).astype(BF), jnp.where(lane < HD, 0.0, 1.0).astype(BF)]
+
+    def prepare(b, carry):
+        rows = pl.ds(pl.multiple_of(b * BLOCK, BLOCK), BLOCK)
+        zero = jnp.zeros((BLOCK, 2 * HD), F32)
+        for ref, out in ((k_ref, kz), (v_ref, vz), (q_ref, qz), (do_ref, dz)):
+            value = ref[rows].astype(F32)
+            out[0, rows] = jnp.where(low, value, zero).astype(BF)
+            out[1, rows] = jnp.where(low, zero, value).astype(BF)
+        value = kt_ref[:, rows].astype(F32)
+        ktz[0, :, rows] = jnp.where(low_t, value, 0.0).astype(BF)
+        ktz[1, :, rows] = jnp.where(low_t, 0.0, value).astype(BF)
+        product = do_ref[rows].astype(F32) * o_ref[rows].astype(F32)
+        coarse = product.astype(BF)
+        fine = (product - coarse.astype(F32)).astype(BF)
+        for row in range(2):
+            delta[row, :, rows] = dot_rows(ones[row], coarse) + dot_rows(ones[row], fine)
+        dq_t[:, rows] = jnp.zeros((2 * HD, BLOCK), F32)
+        return carry
+
+    lax.fori_loop(0, row_len // BLOCK, prepare, 0)
+    u_in = lax.broadcasted_iota(jnp.int32, (BLOCK, 1), 0)
+    t_in = lax.broadcasted_iota(jnp.int32, (1, BLOCK), 1)
+
+    def key_block(kb, carry):
+        keys = pl.ds(pl.multiple_of(kb * BLOCK, BLOCK), BLOCK)
+        u = u_in + kb * BLOCK
+        sums_k, sums_v = [], []
+        for row in range(2):
+            split = split_ref[row]
+            k_row = kz[row, keys]
+            v_row = vz[row, keys]
+            kt_row = ktz[row, :, keys]
+
+            def step(qb, state, row=row, split=split, k_row=k_row, v_row=v_row, kt_row=kt_row):
+                d_keys, d_values = state
+                rows = pl.ds(pl.multiple_of(qb * BLOCK, BLOCK), BLOCK)
+                t = t_in + qb * BLOCK
+                start = jnp.where(t >= split, split, 0)
+                allowed = (u >= start) & (u <= t)
+                scores = dot_rows(k_row, q_ref[rows])
+                probs = jnp.where(allowed, jnp.exp(scores - log_ref[pl.ds(row, 1), rows]), 0.0)
+                d_probs = dot_rows(v_row, do_ref[rows])
+                d_scores = (probs * (d_probs - delta[row, pl.ds(0, 1), rows])).astype(BF)
+                d_values = d_values + dot(probs.astype(BF), dz[row, rows])
+                d_keys = d_keys + dot(d_scores, qz[row, rows])
+                dq_t[:, rows] += dot(kt_row, d_scores)
+                return d_keys, d_values
+
+            zero = jnp.zeros((BLOCK, 2 * HD), F32)
+            last = jnp.where(
+                (kb + 1) * BLOCK <= split, (split + BLOCK - 1) // BLOCK, row_len // BLOCK
+            )
+            d_keys, d_values = lax.fori_loop(kb, last, step, (zero, zero))
+            sums_k.append(d_keys)
+            sums_v.append(d_values)
+        dk[keys] = sums_k[0] + sums_k[1]
+        dv[keys] = sums_v[0] + sums_v[1]
+        return carry
+
+    lax.fori_loop(0, row_len // BLOCK, key_block, 0)
+    low_l = lax.broadcasted_iota(jnp.int32, (local_len, 2 * HD), 1) < HD
+    per = 2 * HD // local_len
+
+    def finish(b, carry):
+        both = pl.ds(pl.multiple_of(b * 2 * HD, 2 * HD), 2 * HD)
+        dq = dq_t[:, both].T * HD**-0.5
+        for part in range(per):
+            i = b * per + part
+            rows = pl.ds(pl.multiple_of(i * local_len, local_len), local_len)
+            target = place_ref[i]
+            cosine, ahead, behind = cos_ref[rows], ahead_ref[rows], behind_ref[rows]
+
+            def turn(x, cosine=cosine, ahead=ahead, behind=behind):
+                return (
+                    x * cosine
+                    - pltpu.roll(x, 2 * HD - ROT // 2, 1) * ahead
+                    - pltpu.roll(x, ROT // 2, 1) * behind
+                )
+
+            q_part = turn(dq[part * local_len : (part + 1) * local_len])
+            k_part = turn(dk[rows])
+            v_part = dv[rows]
+            first = jnp.where(low_l, q_part, pltpu.roll(k_part, HD, 1)).astype(BF)
+            second = jnp.where(low_l, pltpu.roll(q_part, HD, 1), k_part).astype(BF)
+            dpos_ref[rows, : 2 * HD] = first
+            dpos_ref[rows, 2 * HD : 4 * HD] = second
+            dpos_ref[rows, 4 * HD :] = v_part.astype(BF)
+            dmix_ref[target, 0, :, : 2 * HD] = first
+            dmix_ref[target, 1, :, : 2 * HD] = second
+            dmix_ref[target, 0, :, 2 * HD :] = jnp.where(low_l, v_part, 0.0).astype(BF)
+            dmix_ref[target, 1, :, 2 * HD :] = jnp.where(
+                low_l, pltpu.roll(v_part, HD, 1), 0.0
+            ).astype(BF)
+        return carry
+
+    lax.fori_loop(0, row_len // (2 * HD), finish, 0)
+
+
+def attend_back(place, split, q, k, v, k_t, out, d_out, logs, tables, local_len):
+    row_len = q.shape[0]
+    smem = pl.BlockSpec(memory_space=pltpu.SMEM)
+    vmem = pl.BlockSpec(memory_space=pltpu.VMEM)
+    masked = pltpu.VMEM((2, row_len, 2 * HD), BF)
+    whole = pltpu.VMEM((row_len, 2 * HD), F32)
+    pairs = 2 * row_len * row_len // 2
+    return pl.pallas_call(
+        attend_back_kernel,
+        out_shape=(
+            jax.ShapeDtypeStruct((row_len // local_len, 2, local_len, 4 * HD), BF),
+            jax.ShapeDtypeStruct((row_len, 6 * HD), BF),
+        ),
+        in_specs=[smem, smem] + [vmem] * 10,
+        out_specs=(vmem, vmem),
+        scratch_shapes=[
+            masked, masked, masked, masked,
+            pltpu.VMEM((2, 2 * HD, row_len), BF),
+            pltpu.VMEM((2, 8, row_len), F32),
+            pltpu.VMEM((2 * HD, row_len), F32),
+            whole, whole,
+        ],
+        compiler_params=pltpu.CompilerParams(vmem_limit_bytes=48 * 2**20),
+        cost_estimate=pl.CostEstimate(
+            flops=40 * pairs * HD, bytes_accessed=12 * 2**20, transcendentals=pairs
+        ),
+        name="attend_back",
+    )(place, split, q, k, v, k_t, out, d_out, logs, *tables)
+
+
+def hidden_layer(mid, d_result, gate_up_pad, down_pad):
+    width = down_pad.shape[0]
+    gate_up = dot(mid, gate_up_pad)
+    gate, up = gate_up[:, :width], gate_up[:, width:]
+    sig = jax.nn.sigmoid(gate)
+    silu = gate * sig
+    act = (silu * up).astype(BF)
+    d_act = dot_rows(d_result, down_pad)
+    d_gate = d_act * up * (sig + silu * (1.0 - sig))
+    d_gate_up = jnp.concatenate([d_gate.astype(BF), (d_act * silu).astype(BF)], axis=1)
+    return act, d_gate_up
+
+
+def plane_plan(
+    inputs,
+    segments,
+    norm1_gain,
+    norm1_bias,
+    qkv_weight,
+    qkv_bias,
+    out_weight,
+    norm2_gain,
+    norm2_bias,
+    gate_up_weight,
+    down_weight,
+    cotangent,
+):
+    row_count, local_len, features = inputs.shape
+    row_len = segments.shape[1]
+    tokens = row_count * local_len
+    seq = lax.axis_index("seq")
+    rank = lax.axis_index("fsdp")
+    core = seq % 2
+    plane = seq // 2
+    own = core * 4 + rank
+    shard = features // 4
+    hidden = gate_up_weight.shape[1] // 2
+    share = hidden // 8
+    padded = -(-share // 128) * 128
+    tables = turn_tables(row_len)
+    split = jnp.sum((segments == 0).astype(jnp.int32), axis=1)
+    canon = jnp.arange(32, dtype=jnp.int32)
+    place = ((plane - canon // 8) % 4) * 8 + ((canon % 8) ^ own)
+
+    def head_columns(m):
+        first = ((rank ^ m) * 8 + seq) * HD
+        parts = [
+            lax.dynamic_slice_in_dim(qkv_weight, first + part * features, HD, 1) for part in (0, 1, 2)
+        ]
+        return jnp.concatenate(parts + parts[2:], axis=1)
+
+    head_weight = unswap(
+        [head_columns(0)] + [swap(head_columns(m), m) for m in (1, 2, 3)], rank
+    ).reshape(features, 4 * HD)
+    head_first = (rank * 8 + seq) * HD
+    bias_parts = [
+        lax.dynamic_slice_in_dim(qkv_bias, head_first + part * features, HD, 0) for part in (0, 1, 2)
+    ]
+    head_bias = jnp.concatenate(bias_parts + bias_parts[2:])
+
+    flat = inputs.reshape(tokens, features).astype(F32)
+    normed_in, norm1_back = jax.vjp(layer_norm, flat, norm1_gain, norm1_bias)
+    chunk = normed_in.astype(BF)
+    in_halves = []
+    for k in range(4):
+        in_halves += list(gather_plane(chunk))
+        if k < 3:
+            chunk = shift(chunk, 1)
+    mixed = jnp.concatenate([dot(half, head_weight) + head_bias for half in in_halves], axis=0)
+    q, k, v, out_heads, logs = attend(
+        place, split, mixed.reshape(row_len // local_len, row_count, local_len, 4 * HD), tables
+    )
+
+    span = row_len // 8
+    sent = [lax.dynamic_slice_in_dim(out_heads, (seq ^ m) * span, span, 0) for m in range(8)]
+    arrived = [sent[0]] + [swap(sent[m], m * 4) for m in range(1, 8)]
+    att = (
+        unswap(arrived, seq)
+        .reshape(8, span, row_count, HD)
+        .transpose(2, 1, 0, 3)
+        .reshape(row_count, 4, local_len, shard)
+    )
+    branch = dot(att.reshape(row_count * span, shard), out_weight).reshape(
+        row_count, 4, local_len, features
+    )
+    branch = branch.transpose(1, 0, 2, 3)
+    middle = flat + sum_quad([pick(branch, rank ^ m).reshape(tokens, features) for m in range(4)])
+    normed_mid, norm2_back = jax.vjp(layer_norm, middle, norm2_gain, norm2_bias)
+    mid_low = normed_mid.astype(BF)
+    mid_near, mid_far = gather_plane(mid_low)
+
+    def hidden_columns(m):
+        first = (rank ^ m) * 2 * share + core * share
+        return jnp.concatenate(
+            [
+                lax.dynamic_slice_in_dim(gate_up_weight, first, share, 1),
+                lax.dynamic_slice_in_dim(gate_up_weight, first + hidden, share, 1),
+            ],
+            axis=1,
+        )
+
+    gate_up_cols = unswap(
+        [hidden_columns(0)] + [swap(hidden_columns(m), m) for m in (1, 2, 3)], rank
+    ).reshape(features, 2, share)
+    gate_up_pad = jnp.pad(gate_up_cols, ((0, 0), (0, 0), (0, padded - share))).reshape(
+        features, 2 * padded
+    )
+    down_pad = jnp.pad(
+        lax.dynamic_slice_in_dim(down_weight, core * share, share, 0),
+        ((0, padded - share), (0, 0)),
+    )
+    d_out = cotangent.reshape(tokens, features)
+    out_near, out_far = gather_plane(d_out)
+
+    act_far, d_gu_far = hidden_layer(mid_far, out_far, gate_up_pad, down_pad)
+    act_near, d_gu_near = hidden_layer(mid_near, out_near, gate_up_pad, down_pad)
+    blocks = (4, tokens, features)
+    d_norm_mid = sum_plane(
+        dot_rows(d_gu_near, gate_up_pad).reshape(blocks),
+        dot_rows(d_gu_far, gate_up_pad).reshape(blocks),
+    )
+    d_middle_part, d_gain_two, d_bias_two = norm2_back(d_norm_mid)
+    d_middle = d_out.astype(F32) + d_middle_part
+    d_branch = gather_quad(d_middle.astype(BF))
+    result = middle + sum_plane(
+        dot(act_near, down_pad).reshape(blocks), dot(act_far, down_pad).reshape(blocks)
+    )
+
+    d_att = dot_rows(d_branch, out_weight).astype(BF)
+    d_att = unswap(d_att.reshape(4, row_count, local_len, 8, HD), rank)
+    d_att = d_att.transpose(3, 0, 2, 1, 4).reshape(8, span, row_count * HD)
+    sent = [pick(d_att, seq ^ m) for m in range(8)]
+    arrived = [sent[0]] + [swap(sent[m], m * 4) for m in range(1, 8)]
+    d_heads = unswap(arrived, seq).reshape(row_len, row_count * HD)
+    log_rows = jnp.stack([logs[:, 0], logs[:, HD]])
+    d_mixed, d_packed = attend_back(
+        place, split, q, k, v, k.T, out_heads, d_heads, log_rows, tables, local_len
+    )
+
+    reach = row_len // 4
+    sent = [lax.dynamic_slice_in_dim(d_packed, (plane + s) % 4 * reach, reach, 0) for s in range(4)]
+    arrived = jnp.stack([sent[0]] + [shift(sent[s], s) for s in (1, 2, 3)])
+    weights = [head_weight]
+    for _ in range(3):
+        weights.append(shift(weights[-1], 1))
+    weights = jnp.stack(weights)
+    near_weight = jnp.concatenate(
+        [
+            weights[:, :, : 2 * HD].transpose(1, 0, 2).reshape(features, 8 * HD),
+            weights[:, :, 2 * HD : 3 * HD].transpose(1, 0, 2).reshape(features, 4 * HD),
+        ],
+        axis=1,
+    )
+    tiles = arrived.reshape(4, reach, 3, 2 * HD)
+    lines = []
+    for row in range(2):
+        lines.append(
+            jnp.concatenate(
+                [
+                    tiles[:, :, row].transpose(1, 0, 2).reshape(reach, 8 * HD),
+                    tiles[:, :, 2, row * HD : (row + 1) * HD].transpose(1, 0, 2).reshape(reach, 4 * HD),
+                ],
+                axis=1,
+            )
+        )
+    d_in = dot_rows(jnp.concatenate(lines, axis=0), near_weight)
+    d_in = d_in.reshape(row_count, 8, local_len, features).transpose(1, 0, 2, 3)
+    near = jnp.stack([pick(d_in, own ^ m).reshape(tokens, features) for m in range(4)])
+    far = jnp.stack([pick(d_in, own ^ (m + 4)).reshape(tokens, features) for m in range(4)])
+    d_norm_in = sum_plane(near, far)
+    d_flat_part, d_gain_one, d_bias_one = norm1_back(d_norm_in)
+    d_inputs = d_middle + d_flat_part
+
+    d_mixed = d_mixed.reshape(row_len * row_count, 4 * HD)
+    head_grad = dot_cols(jnp.concatenate(in_halves, axis=0), d_mixed)[:, : 3 * HD].astype(BF)
+    head_grad = head_grad.reshape(4, shard, 3 * HD)
+    head_rows = unswap(
+        [pick(head_grad, rank)] + [swap(pick(head_grad, rank ^ m), m) for m in (1, 2, 3)], rank
+    )
+    qkv_grad = lax.all_gather(head_rows, "seq", axis=0)
+    qkv_grad = (
+        qkv_grad.reshape(8, 4, shard, 3, HD).transpose(2, 3, 1, 0, 4).reshape(shard, 3 * features)
+    ).astype(F32)
+    bias_sum = jnp.sum(d_mixed.astype(F32), axis=0)
+    bias_own = jnp.zeros((3 * features,), F32)
+    for part in range(3):
+        bias_own = lax.dynamic_update_slice_in_dim(
+            bias_own, bias_sum[part * HD : (part + 1) * HD], head_first + part * features, 0
+        )
+
+    att_order = jnp.stack([pick(att.transpose(1, 0, 2, 3), rank ^ m) for m in range(4)])
+    out_part = dot_cols(att_order.reshape(4 * tokens, shard), d_branch).astype(BF)
+    out_part = lax.psum_scatter(out_part, "seq", scatter_dimension=0, tiled=True)
+    out_grad = lax.all_gather(out_part, "seq", axis=0, tiled=True).astype(F32)
+
+    def gather_rest(value):
+        pieces = [shift(value, 1)]
+        for _ in range(2):
+            pieces.append(shift(pieces[-1], 1))
+        return gather_plane(jnp.concatenate(pieces, axis=0))
+
+    mid_rest = gather_rest(mid_low)
+    out_rest = gather_rest(d_out)
+    rest = [hidden_layer(m, o, gate_up_pad, down_pad) for m, o in zip(mid_rest, out_rest)]
+    mid_all = jnp.concatenate([mid_near, mid_far, *mid_rest], axis=0)
+    out_all = jnp.concatenate([out_near, out_far, *out_rest], axis=0)
+    act_all = jnp.concatenate([act_near, act_far, rest[0][0], rest[1][0]], axis=0)
+    d_gu_all = jnp.concatenate([d_gu_near, d_gu_far, rest[0][1], rest[1][1]], axis=0)
+    down_own = dot_cols(act_all, out_all)[:share].astype(BF)
+    down_other = swap(down_own, 4)
+    down_pair = jnp.stack([down_own, down_other])
+    down_grad = jnp.concatenate([pick(down_pair, core), pick(down_pair, 1 - core)], axis=0).astype(F32)
+    gate_up_own = dot_cols(mid_all, d_gu_all).reshape(features, 2, padded)[:, :, :share].astype(BF)
+    gate_up_own = gate_up_own.reshape(4, shard, 2 * share)
+    gate_up_rows = unswap(
+        [pick(gate_up_own, rank)] + [swap(pick(gate_up_own, rank ^ m), m) for m in (1, 2, 3)], rank
+    )
+    gate_up_pair = jnp.stack([gate_up_rows, swap(gate_up_rows, 4)])
+    gate_up_pair = jnp.stack([pick(gate_up_pair, core), pick(gate_up_pair, 1 - core)])
+    gate_up_grad = (
+        gate_up_pair.reshape(2, 4, shard, 2, share)
+        .transpose(2, 3, 1, 0, 4)
+        .reshape(shard, 2 * hidden)
+        .astype(F32)
+    )
+    sums = sum_all(jnp.concatenate([d_gain_one, d_bias_one, bias_own, d_gain_two, d_bias_two]))
+    return (
+        result.reshape(row_count, local_len, features),
+        d_inputs.reshape(row_count, local_len, features),
+        sums[:features],
+        sums[features : 2 * features],
+        qkv_grad,
+        sums[2 * features : 5 * features],
+        out_grad,
+        sums[5 * features : 6 * features],
+        sums[6 * features :],
+        gate_up_grad,
+        down_grad,
+    )
+
+
 def solution(mesh):
     placed = (
         P(None, ("seq", "fsdp"), None),
@@ -344,8 +913,9 @@
         P("fsdp", None),
         P(None, ("seq", "fsdp"), None),
     )
+    plan = plane_plan if (mesh.shape["seq"], mesh.shape["fsdp"]) == (8, 4) else general_plan
     return jax.shard_map(
-        shards,
+        plan,
         mesh=mesh,
         in_specs=placed,
         out_specs=(

time: 5310 us -> 1220 us (0.23)
  waiting for transfers between devices: 4660 us -> 364 us
  local copies, waits for them, and re-layouts: 104 us -> 381 us
  matrix products: 311 us -> 178 us
  blocking collectives: 83.8 us -> 0 us
  starting transfers between devices: 28 us -> 109 us
    reduce_scatter x6 -> x1, waiting for transfers between devices: 3630 us -> 0.01 us  [plane_plan(): lax.psum_scatter(out_part, 'seq', scatter_dimension=0, tiled=True)]
    all_gather x10 -> x2, waiting for transfers between devices: 981 us -> 0.01 us  [the longest x1 0.01 us: plane_plan(): out_grad = lax.all_gather(out_part, 'seq', axis=0, tiled=True).astype(F32)]
    ppermute x0 -> x107, waiting for transfers between devices: none -> 364 us  [the longest x92 248 us: swap(): lax.ppermute(value, ('seq', 'fsdp'), [(i, i ^ mask) for i in range(32)])]
    dot_general x40 -> x27, matrix products: 311 us -> 178 us  [the longest x4 68.6 us: dot_cols(): lax.dot_general(left, right, (((0,), (0,)), ((), ())), preferred_element_...]
    unnamed x92 -> x268, local copies, waits for them, and re-layouts: 24.2 us -> 145 us
    ppermute x0 -> x107, starting transfers between devices: none -> 109 us  [the longest x92 93.9 us: swap(): lax.ppermute(value, ('seq', 'fsdp'), [(i, i ^ mask) for i in range(32)])]
    dynamic_slice x24 -> x18, local copies, waits for them, and re-layouts: 5.72 us -> 61.9 us  [the longest x11 45.4 us: pick(): return lax.dynamic_index_in_dim(stacked, index, 0, keepdims=False)]
  transfers between devices with their start and end apart: 22 -> 110, of which waited for: 17 -> 40; matrix products, arithmetic and copies ran while one was open for 6% -> 47% of each run, Pallas kernels for 0% -> 4%
where the time goes in v1:
time: 1220 us; the launch traced here: 1210 us
  local copies, waits for them, and re-layouts  381 us (31%)
  waiting for transfers between devices  364 us (30%)
  matrix products  178 us (15%)
  starting transfers between devices  109 us (9%)
  other arithmetic  107 us (9%)
  Pallas kernels  49.5 us (4%)
  between operations  16.2 us (1%)
    ppermute x92, waiting for transfers between devices, swap(): lax.ppermute(value, ('seq', 'fsdp'), [(i, i ^ mask) for i in range(32)])  248 us
    unnamed x268, local copies, waits for them, and re-layouts  145 us
    ppermute x15, waiting for transfers between devices, shift(): lax.ppermute(value, ('seq', 'fsdp'), [(i, (i + 8 * steps) % 32) for i in...  116 us
    ppermute x92, starting transfers between devices, swap(): lax.ppermute(value, ('seq', 'fsdp'), [(i, i ^ mask) for i in range(32)])  93.9 us
    dot_general x4, matrix products, dot_cols(): lax.dot_general(left, right, (((0,), (0,)), ((), ())), preferred_element_...  68.6 us
    dot_general x15, matrix products, dot(): return jnp.dot(left, right, preferred_element_type=F32)  63.4 us
    dot_general x8, matrix products, dot_rows(): lax.dot_general(left, right, (((1,), (1,)), ((), ())), preferred_element_...  46.5 us
    dynamic_slice x11, local copies, waits for them, and re-layouts, pick(): return lax.dynamic_index_in_dim(stacked, index, 0, keepdims=False)  45.4 us
  transfers between devices with their start and end apart: 110, of which 40 were waited for; matrix products, arithmetic and copies ran while one was open for 47% of the time, Pallas kernels for 4%

profile of v1, /device:TPU:0, one launch (start us, length us, event | category | flops | bytes accessed | tf_op | source)
XLA Modules:
  0.0 1205.7 jit_solution(1713732771405829851)
XLA Ops:
  111.9 58.0 %collective-permute-done.12 = bf16[64,2048]{1,0:T(8,128)(2,1)S(1)} collective-permute-done((bf16[64,2048]{1,0:T(8,128)(2,1)S(1)}, bf16[64,2048]{1,0:T(8,128)(2,1)S(1)}, u32[]{:S(2)}, u32[]{:S(2)}) %collective-permute-start.12) | collective-permute-done | bytes 262176 | tf_op jit(solution)/shard_map/ppermute | solution.py:340
  186.7 25.1 %collective-permute-done.95 = bf16[128,2048]{1,0:T(8,128)(2,1)S(1)} collective-permute-done((bf16[128,2048]{1,0:T(8,128)(2,1)}, bf16[128,2048]{1,0:T(8,128)(2,1)S(1)}, u32[]{:S(2)}, u32[]{:S(2)}) %collective-permute-start.95) | collective-permute-done | bytes 524320 | tf_op jit(solution)/shard_map/ppermute | solution.py:344
  221.7 18.0 %collective-permute-done.96 = bf16[128,2048]{1,0:T(8,128)(2,1)S(1)} collective-permute-done((bf16[128,2048]{1,0:T(8,128)(2,1)S(1)}, bf16[128,2048]{1,0:T(8,128)(2,1)S(1)}, u32[]{:S(2)}, u32[]{:S(2)}) %collective-permute-start.96) | collective-permute-done | bytes 524320 | tf_op jit(solution)/shard_map/ppermute | solution.py:344
  243.1 17.3 %collective-permute-done.72 = bf16[2048,256]{0,1:T(8,128)(2,1)} collective-permute-done((bf16[2048,256]{0,1:T(8,128)(2,1)S(1)}, bf16[2048,256]{0,1:T(8,128)(2,1)}, u32[]{:S(2)}, u32[]{:S(2)}) %collective-permute-start.72) | collective-permute-done | bytes 1048608 | tf_op jit(solution)/shard_map/ppermute | solution.py:344
  274.9 14.8 %reshape.334 = bf16[2048,2,704]{2,1,0:T(2,128)(2,1)} reshape(bf16[4,512,1408]{2,1,0:T(8,128)(2,1)} %pad_maximum_fusion.1) | data formatting | bytes 11534336 | tf_op jit(solution)/shard_map/reshape | solution.py:763
  289.7 16.1 %copy.274 = bf16[2048,2,704]{0,2,1:T(8,128)(2,1)} copy(bf16[2048,2,704]{2,1,0:T(2,128)(2,1)} %reshape.334) | data formatting | bytes 11534336 | tf_op jit(solution)/shard_map/reshape | solution.py:763
  358.3 21.4 %attend.1 = (bf16[2048,128]{1,0:T(8,128)(2,1)S(1)}, bf16[2048,128]{1,0:T(8,128)(2,1)S(1)}, bf16[2048,128]{1,0:T(8,128)(2,1)S(1)}, bf16[2048,128]{1,0:T(8,128)(2,1)S(1)}, f32[2048,128]{1,0:T(8,128)S(1)}) custom-call(s32[32]{0:T(128)S(1)} %fusion.92.place_ref, s32[2]{0:T(128)S(1)} %fusion.90.split_ref, f32[32,2,64,256]{3,2,1,0:T(8,128)} %bitcast.406, ...), custom_call_target="tpu_custom_call" | custom-call | flops 4294967296 | bytes 12582912 | tf_op jit(solution)/shard_map/attend/pallas_call | solution.py:507
  577.6 15.0 %collective-permute-done.54 = bf16[128,2048]{1,0:T(8,128)(2,1)S(1)} collective-permute-done((bf16[128,2048]{1,0:T(8,128)(2,1)S(1)}, bf16[128,2048]{1,0:T(8,128)(2,1)S(1)}, u32[]{:S(2)}, u32[]{:S(2)}) %collective-permute-start.54) | collective-permute-done | bytes 524320 | tf_op jit(solution)/shard_map/ppermute | solution.py:340
  628.8 14.1 %fusion.128 = f32[1536,1536]{0,1:T(8,128)} fusion(bf16[1536,2048]{1,0:T(8,128)(2,1)} %get-tuple-element.202, bf16[2048,1536]{0,1:T(8,128)(2,1)S(1)} %bitcast.350), kind=kOutput, calls=%fused_computation.487 | convolution fusion | flops 9663676416 | bytes 22020096 | tf_op jit(solution)/shard_map/dot_general | solution.py:392
  658.2 13.5 %multiply_convert_fusion.5 = (bf16[1536,768]{0,1:T(8,128)(2,1)}, bf16[1536,768]{0,1:T(8,128)(2,1)}, bf16[1536,768]{0,1:T(8,128)(2,1)}) fusion(f32[1536,1536]{0,1:T(8,128)} %fusion.128, bf16[1536,2048]{1,0:T(8,128)(2,1)} %get-tuple-element.199, bf16[704,2048]{1,0:T(8,128)(2,1)} %constant_dynamic-slice_fusion.28), kind=kOutput, calls=%fused_computation.45 | convolution fusion | flops 4848353280 | bytes 25690112 | tf_op jit(solution)/shard_map/dot_general | solution.py:396
  703.3 28.1 %attend_back.1 = (bf16[32,2,64,256]{3,2,1,0:T(8,128)(2,1)}, bf16[2048,384]{1,0:T(8,128)(2,1)}) custom-call(s32[32]{0:T(128)S(1)} %fusion.92.place_ref, s32[2]{0:T(128)S(1)} %fusion.90.split_ref, bf16[2048,128]{1,0:T(8,128)(2,1)S(1)} %copy-done.12, bf16[2048,128]{1,0:T(8,128)(2,1)S(1)} %copy-done.5, bf16[2048,128]{1,0:T(8,128)(2,1)S(1)} %copy-done.14, ...), custom_call_target="tpu_custom_call" | custom-call | flops 10737418240 | bytes 12582912 | tf_op jit(solution)/shard_map/attend_back/pallas_call | solution.py:637
  761.0 47.1 %collective-permute-done.69 = bf16[512,384]{1,0:T(8,128)(2,1)S(1)} collective-permute-done((bf16[512,384]{1,0:T(8,128)(2,1)}, bf16[512,384]{1,0:T(8,128)(2,1)S(1)}, u32[]{:S(2)}, u32[]{:S(2)}) %collective-permute-start.69) | collective-permute-done | bytes 393248 | tf_op jit(solution)/shard_map/ppermute | solution.py:344
  819.2 12.8 %fusion.129 = f32[1536,1536]{0,1:T(8,128)S(1)} fusion(bf16[1536,2048]{1,0:T(8,128)(2,1)} %collective-permute-done.93, bf16[2048,1536]{0,1:T(8,128)(2,1)S(1)} %bitcast.353), kind=kOutput, calls=%fused_computation.488 | convolution fusion | flops 9663676416 | bytes 22020096 | tf_op jit(solution)/shard_map/dot_general | solution.py:392
  838.9 11.4 multiply_convert_fusion.3
  850.3 40.9 %fusion.12 = bf16[2048,1536]{0,1:T(8,128)(2,1)} fusion(bf16[4096,2048]{1,0:T(8,128)(2,1)} %constant_dynamic-update-slice_fusion.112, bf16[1536,768]{0,1:T(8,128)(2,1)} %get-tuple-element.106, bf16[1536,768]{0,1:T(8,128)(2,1)} %get-tuple-element.105, bf16[1536,768]{0,1:T(8,128)(2,1)} %get-tuple-element.104, bf16[1536,768]{0,1:T(8,128)(2,1)} %get-tuple-element.103, ...), kind=kOutput, calls=%fused_computation.18 | convolution fusion | flops 25848446976 | bytes 35651584 | tf_op jit(solution)/shard_map/dot_general | solution.py:400
  907.9 19.6 %constant_dynamic-slice_fusion.7 = (bf16[1,512,1408]{1,0,2:T(2,128)(2,1)}, bf16[1,512,1408]{1,0,2:T(2,128)(2,1)}, bf16[1,512,1408]{1,0,2:T(2,128)(2,1)}, bf16[1,512,1408]{1,0,2:T(2,128)(2,1)}) fusion(bf16[4,512,1408]{1,0,2:T(4,128)(2,1)} %reshape.323, s32[]{:T(128)S(6)} %select_n.344, s32[]{:T(128)S(6)} %select_n.347, s32[]{:T(128)S(6)} %select_n.346, ...), kind=kLoop, calls=%fused_computation.360 | loop fusion | bytes 11534352 | tf_op jit(solution)/shard_map/jit(dynamic_index_in_dim)/dynamic_slice | solution.py:348
  970.8 13.3 %collective-permute-done.102 = bf16[512,1408]{1,0:T(8,128)(2,1)} collective-permute-done((bf16[512,1408]{1,0:T(8,128)(2,1)}, bf16[512,1408]{1,0:T(8,128)(2,1)}, u32[]{:S(2)}, u32[]{:S(2)}) %collective-permute-start.102) | collective-permute-done | bytes 1441824 | tf_op jit(solution)/shard_map/ppermute | solution.py:340
  985.7 29.5 %collective-permute-done.103 = bf16[512,1408]{1,0:T(8,128)(2,1)} collective-permute-done((bf16[512,1408]{1,0:T(8,128)(2,1)}, bf16[512,1408]{1,0:T(8,128)(2,1)}, u32[]{:S(2)}, u32[]{:S(2)}) %collective-permute-start.103) | collective-permute-done | bytes 1441824 | tf_op jit(solution)/shard_map/ppermute | solution.py:340
  1026.3 16.7 %fusion.15 = bf16[768,2048]{1,0:T(8,128)(2,1)S(1)} fusion(bf16[4096,2048]{1,0:T(8,128)(2,1)} %constant_dynamic-update-slice_fusion.126, bf16[1536,768]{0,1:T(8,128)(2,1)S(1)} %copy-done.83, bf16[1536,768]{0,1:T(8,128)(2,1)S(1)} %copy-done.82, bf16[512,768]{0,1:T(8,128)(2,1)S(1)} %copy-done.53, bf16[512,768]{0,1:T(8,128)(2,1)S(1)} %copy-done.52), kind=kOutput, calls=%fused_computation.23 | convolution fusion | flops 12910067712 | bytes 26214400 | tf_op jit(solution)/shard_map/dot_general | solution.py:400
  1094.9 12.2 %copy.253 = f32[512,3,4,8,64]{0,4,3,2,1:T(8,128)} copy(f32[512,3,4,8,64]{0,4,1,2,3:T(8,128)} %convert_bitcast_fusion) | data formatting | bytes 25165824 | tf_op jit(solution)/shard_map/convert_element_type | solution.py:842
  1107.1 12.6 %copy.268 = f32[512,6144]{1,0:T(8,128)} copy(f32[512,6144]{0,1:T(8,128)} %bitcast.330) | data formatting | bytes 25165824
  1135.3 23.4 %copy.264 = f32[2,4,512,1408]{2,3,1,0:T(8,128)} copy(f32[2,4,512,1408]{3,2,1,0:T(8,128)} %maximum_convert_fusion) | data formatting | bytes 46137344 | tf_op jit(solution)/shard_map/convert_element_type | solution.py:883
  1158.8 16.3 %copy.265 = f32[512,2,4,2,704]{0,4,3,2,1:T(8,128)} copy(f32[512,2,4,2,704]{0,4,1,2,3:T(8,128)} %bitcast.328) | data formatting | bytes 46137344 | tf_op jit(solution)/shard_map/convert_element_type | solution.py:883
  1175.0 23.6 %copy.269 = f32[512,11264]{1,0:T(8,128)} copy(f32[512,11264]{0,1:T(8,128)} %bitcast.329) | data formatting | bytes 46137344
  (662 shorter events, 668.8 us)
Async XLA Ops:
  7.2 690.8 %reduce-scatter.2.cloned.1.call-start = ((), (), s32[]{:S(2)}) async-start(), calls=%async_computation.1 | async-start | bytes 2359296 | tf_op jit(solution)/shard_map/reduce_scatter | solution.py:852
  17.6 60.3 %collective-permute-start.49 = (bf16[128,2048]{1,0:T(8,128)(2,1)}, bf16[128,2048]{1,0:T(8,128)(2,1)}, u32[]{:S(2)}, u32[]{:S(2)}) collective-permute-start(bf16[128,2048]{1,0:T(8,128)(2,1)} %bitcast.35), channel_id=1, source_target_pairs={{0,2},{1,3},{2,0},{3,1},{4,6},{5,7},{6,4},{7,5},{8,10},{9,11},{10,... | collective-permute-start | bytes 1572872 | tf_op jit(solution)/shard_map/ppermute | solution.py:340
  99.8 73.9 %collective-permute-start.42 = (bf16[512,1408]{1,0:T(8,128)(2,1)S(1)}, bf16[512,1408]{1,0:T(8,128)(2,1)S(1)}, u32[]{:S(2)}, u32[]{:S(2)}) collective-permute-start(bf16[512,1408]{1,0:T(8,128)(2,1)S(1)} %copy-done.49), channel_id=1, source_target_pairs={{0,3},{1,2},{2,1},{3,0},{4,7},{5,6},{6,5},{7,4},{8,11},{9,10},{10,... | collective-permute-start | bytes 4325384 | tf_op jit(solution)/shard_map/ppermute | solution.py:340
  102.5 72.8 %collective-permute-start.40 = (bf16[512,1408]{1,0:T(8,128)(2,1)S(1)}, bf16[512,1408]{1,0:T(8,128)(2,1)S(1)}, u32[]{:S(2)}, u32[]{:S(2)}) collective-permute-start(bf16[512,1408]{1,0:T(8,128)(2,1)S(1)} %copy-done.48), channel_id=1, source_target_pairs={{0,1},{1,0},{2,3},{3,2},{4,5},{5,4},{6,7},{7,6},{8,9},{9,8},{10,11... | collective-permute-start | bytes 4325384 | tf_op jit(solution)/shard_map/ppermute | solution.py:340
  103.2 73.3 %collective-permute-start.41 = (bf16[512,1408]{1,0:T(8,128)(2,1)S(1)}, bf16[512,1408]{1,0:T(8,128)(2,1)S(1)}, u32[]{:S(2)}, u32[]{:S(2)}) collective-permute-start(bf16[512,1408]{1,0:T(8,128)(2,1)S(1)} %copy-done.47), channel_id=1, source_target_pairs={{0,2},{1,3},{2,0},{3,1},{4,6},{5,7},{6,4},{7,5},{8,10},{9,11},{10,... | collective-permute-start | bytes 4325384 | tf_op jit(solution)/shard_map/ppermute | solution.py:340
  103.6 66.3 %collective-permute-start.12 = (bf16[64,2048]{1,0:T(8,128)(2,1)S(1)}, bf16[64,2048]{1,0:T(8,128)(2,1)S(1)}, u32[]{:S(2)}, u32[]{:S(2)}) collective-permute-start(bf16[64,2048]{1,0:T(8,128)(2,1)S(1)} %slice.243), channel_id=1, source_target_pairs={{0,1},{1,0},{2,3},{3,2},{4,5},{5,4},{6,7},{7,6},{8,9},{9,8},{10,11... | collective-permute-start | bytes 786440 | tf_op jit(solution)/shard_map/ppermute | solution.py:340
  108.4 62.4 %collective-permute-start.11 = (bf16[64,2048]{1,0:T(8,128)(2,1)S(1)}, bf16[64,2048]{1,0:T(8,128)(2,1)S(1)}, u32[]{:S(2)}, u32[]{:S(2)}) collective-permute-start(bf16[64,2048]{1,0:T(8,128)(2,1)S(1)} %slice.242), channel_id=1, source_target_pairs={{0,2},{1,3},{2,0},{3,1},{4,6},{5,7},{6,4},{7,5},{8,10},{9,11},{10,... | collective-permute-start | bytes 786440 | tf_op jit(solution)/shard_map/ppermute | solution.py:340
  185.1 77.1 %collective-permute-start.13 = (bf16[512,2048]{1,0:T(8,128)(2,1)S(1)}, bf16[512,2048]{1,0:T(8,128)(2,1)S(1)}, u32[]{:S(2)}, u32[]{:S(2)}) collective-permute-start(bf16[512,2048]{1,0:T(8,128)(2,1)S(1)} %get-tuple-element.302), channel_id=1, source_target_pairs={{0,4},{1,5},{2,6},{3,7},{4,0},{5,1},{6,2},{7,3},{8,12},{9,13},{10,... | collective-permute-start | bytes 6291464 | tf_op jit(solution)/shard_map/ppermute | solution.py:340
  214.6 55.1 %collective-permute-start.18 = (bf16[64,2048]{1,0:T(8,128)(2,1)S(1)}, bf16[64,2048]{1,0:T(8,128)(2,1)S(1)}, u32[]{:S(2)}, u32[]{:S(2)}) collective-permute-start(bf16[64,2048]{1,0:T(8,128)(2,1)S(1)} %slice.245), channel_id=1, source_target_pairs={{0,1},{1,0},{2,3},{3,2},{4,5},{5,4},{6,7},{7,6},{8,9},{9,8},{10,11... | collective-permute-start | bytes 786440 | tf_op jit(solution)/shard_map/ppermute | solution.py:340
  262.2 56.9 %collective-permute-start.73 = (bf16[2048,256]{0,1:T(8,128)(2,1)}, bf16[2048,256]{0,1:T(8,128)(2,1)}, u32[]{:S(2)}, u32[]{:S(2)}) collective-permute-start(bf16[2048,256]{0,1:T(8,128)(2,1)} %collective-permute-done.72), channel_id=1, source_target_pairs={{0,8},{1,9},{2,10},{3,11},{4,12},{5,13},{6,14},{7,15},{8,16},{9,17... | collective-permute-start | bytes 3145736 | tf_op jit(solution)/shard_map/ppermute | solution.py:344
  267.3 56.6 %collective-permute-start.98 = (bf16[384,2048]{1,0:T(8,128)(2,1)}, bf16[384,2048]{1,0:T(8,128)(2,1)}, u32[]{:S(2)}, u32[]{:S(2)}) collective-permute-start(bf16[384,2048]{1,0:T(8,128)(2,1)} %get-tuple-element.216), channel_id=1, source_target_pairs={{0,2},{1,3},{2,0},{3,1},{4,6},{5,7},{6,4},{7,5},{8,10},{9,11},{10,... | collective-permute-start | bytes 4718600 | tf_op jit(solution)/shard_map/ppermute | solution.py:340
  269.7 55.7 %collective-permute-start.97 = (bf16[384,2048]{1,0:T(8,128)(2,1)}, bf16[384,2048]{1,0:T(8,128)(2,1)}, u32[]{:S(2)}, u32[]{:S(2)}) collective-permute-start(bf16[384,2048]{1,0:T(8,128)(2,1)} %get-tuple-element.216), channel_id=1, source_target_pairs={{0,1},{1,0},{2,3},{3,2},{4,5},{5,4},{6,7},{7,6},{8,9},{9,8},{10,11... | collective-permute-start | bytes 4718600 | tf_op jit(solution)/shard_map/ppermute | solution.py:340
  271.3 60.9 %collective-permute-start.19 = (bf16[512,2048]{1,0:T(8,128)(2,1)}, bf16[512,2048]{1,0:T(8,128)(2,1)}, u32[]{:S(2)}, u32[]{:S(2)}) collective-permute-start(bf16[512,2048]{1,0:T(8,128)(2,1)} %get-tuple-element.298), channel_id=1, source_target_pairs={{0,4},{1,5},{2,6},{3,7},{4,0},{5,1},{6,2},{7,3},{8,12},{9,13},{10,... | collective-permute-start | bytes 6291464 | tf_op jit(solution)/shard_map/ppermute | solution.py:340
  352.0 177.8 %collective-permute-start.101 = (bf16[1536,2048]{1,0:T(8,128)(2,1)}, bf16[1536,2048]{1,0:T(8,128)(2,1)}, u32[]{:S(2)}, u32[]{:S(2)}) collective-permute-start(bf16[1536,2048]{1,0:T(8,128)(2,1)} %get-tuple-element.199), channel_id=1, source_target_pairs={{0,4},{1,5},{2,6},{3,7},{4,0},{5,1},{6,2},{7,3},{8,12},{9,13},{10,... | collective-permute-start | bytes 18874376 | tf_op jit(solution)/shard_map/ppermute | solution.py:340
  603.9 215.3 %collective-permute-start.93 = (bf16[1536,2048]{1,0:T(8,128)(2,1)}, bf16[1536,2048]{1,0:T(8,128)(2,1)}, u32[]{:S(2)}, u32[]{:S(2)}) collective-permute-start(bf16[1536,2048]{1,0:T(8,128)(2,1)} %get-tuple-element.202), channel_id=1, source_target_pairs={{0,4},{1,5},{2,6},{3,7},{4,0},{5,1},{6,2},{7,3},{8,12},{9,13},{10,... | collective-permute-start | bytes 18874376 | tf_op jit(solution)/shard_map/ppermute | solution.py:340
  655.5 415.9 %all-gather.4.cloned.1.call-start = ((), (), s32[]{:S(2)}) async-start(), calls=%async_computation.2 | async-start | bytes 2359296 | tf_op jit(solution)/shard_map/all_gather | solution.py:853
  698.0 387.4 %all-gather.6.cloned.1.call-start = ((), (), s32[]{:S(2)}) async-start(), calls=%async_computation.3 | async-start | bytes 7077888 | tf_op jit(solution)/shard_map/all_gather | solution.py:839
  819.2 136.1 %collective-permute-start.74 = (bf16[4,128,2048]{2,1,0:T(8,128)(2,1)S(1)}, bf16[4,128,2048]{2,1,0:T(8,128)(2,1)}, u32[]{:S(2)}, u32[]{:S(2)}) collective-permute-start(bf16[4,128,2048]{2,1,0:T(8,128)(2,1)S(1)} %pad_maximum_fusion.5), channel_id=1, source_target_pairs={{0,4},{1,5},{2,6},{3,7},{4,0},{5,1},{6,2},{7,3},{8,12},{9,13},{10,... | collective-permute-start | bytes 6291464 | tf_op jit(solution)/shard_map/ppermute | solution.py:340
  950.6 64.5 %collective-permute-start.103 = (bf16[512,1408]{1,0:T(8,128)(2,1)}, bf16[512,1408]{1,0:T(8,128)(2,1)}, u32[]{:S(2)}, u32[]{:S(2)}) collective-permute-start(bf16[512,1408]{1,0:T(8,128)(2,1)} %bitcast.382), channel_id=1, source_target_pairs={{0,2},{1,3},{2,0},{3,1},{4,6},{5,7},{6,4},{7,5},{8,10},{9,11},{10,... | collective-permute-start | bytes 4325384 | tf_op jit(solution)/shard_map/ppermute | solution.py:340
  952.0 64.1 %collective-permute-start.104 = (bf16[512,1408]{1,0:T(8,128)(2,1)S(1)}, bf16[512,1408]{1,0:T(8,128)(2,1)}, u32[]{:S(2)}, u32[]{:S(2)}) collective-permute-start(bf16[512,1408]{1,0:T(8,128)(2,1)S(1)} %bitcast.381), channel_id=1, source_target_pairs={{0,3},{1,2},{2,1},{3,0},{4,7},{5,6},{6,5},{7,4},{8,11},{9,10},{10,... | collective-permute-start | bytes 4325384 | tf_op jit(solution)/shard_map/ppermute | solution.py:340
  961.1 84.2 %collective-permute-start.75 = (bf16[128,2048]{1,0:T(8,128)(2,1)}, bf16[128,2048]{1,0:T(8,128)(2,1)S(1)}, u32[]{:S(2)}, u32[]{:S(2)}) collective-permute-start(bf16[128,2048]{1,0:T(8,128)(2,1)} %get-tuple-element.164), channel_id=1, source_target_pairs={{0,1},{1,0},{2,3},{3,2},{4,5},{5,4},{6,7},{7,6},{8,9},{9,8},{10,11... | collective-permute-start | bytes 1572872 | tf_op jit(solution)/shard_map/ppermute | solution.py:340
  962.3 82.9 %collective-permute-start.77 = (bf16[128,2048]{1,0:T(8,128)(2,1)}, bf16[128,2048]{1,0:T(8,128)(2,1)}, u32[]{:S(2)}, u32[]{:S(2)}) collective-permute-start(bf16[128,2048]{1,0:T(8,128)(2,1)} %get-tuple-element.165), channel_id=1, source_target_pairs={{0,3},{1,2},{2,1},{3,0},{4,7},{5,6},{6,5},{7,4},{8,11},{9,10},{10,... | collective-permute-start | bytes 1572872 | tf_op jit(solution)/shard_map/ppermute | solution.py:340
  984.1 61.1 %collective-permute-start.76 = (bf16[128,2048]{1,0:T(8,128)(2,1)}, bf16[128,2048]{1,0:T(8,128)(2,1)S(1)}, u32[]{:S(2)}, u32[]{:S(2)}) collective-permute-start(bf16[128,2048]{1,0:T(8,128)(2,1)} %get-tuple-element.166), channel_id=1, source_target_pairs={{0,2},{1,3},{2,0},{3,1},{4,6},{5,7},{6,4},{7,5},{8,10},{9,11},{10,... | collective-permute-start | bytes 1572872 | tf_op jit(solution)/shard_map/ppermute | solution.py:340
  1025.9 93.8 %collective-permute-start.105 = (bf16[4,512,1408]{2,1,0:T(8,128)(2,1)}, bf16[4,512,1408]{2,1,0:T(8,128)(2,1)}, u32[]{:S(2)}, u32[]{:S(2)}) collective-permute-start(bf16[4,512,1408]{2,1,0:T(8,128)(2,1)} %get-tuple-element.141), channel_id=1, source_target_pairs={{0,4},{1,5},{2,6},{3,7},{4,0},{5,1},{6,2},{7,3},{8,12},{9,13},{10,... | collective-permute-start | bytes 17301512 | tf_op jit(solution)/shard_map/ppermute | solution.py:340
  (177 other events, 3177.5 us)
Sparse Core Ops, SparseCore 0:
  655.6 37.6 reduce-scatter.1
  698.1 28.5 all-gather.3
  760.9 74.1 all-gather.5

commit v2 on v1

--- a/solution.py
+++ b/solution.py
@@ -1,3 +1,5 @@
+import functools
+
 import jax
 import jax.numpy as jnp
 from jax import lax
@@ -334,58 +336,47 @@
 BLOCK = 512
 BF = jnp.bfloat16
 F32 = jnp.float32
+SMALL = pl.CostEstimate(flops=1000, bytes_accessed=1000, transcendentals=0)
 
 
 def swap(value, mask):
-    return lax.ppermute(value, ("seq", "fsdp"), [(i, i ^ mask) for i in range(32)])
+    return lax.ppermute(value, ("z", "core", "fsdp"), [(i, i ^ mask) for i in range(32)])
 
 
 def shift(value, steps):
-    return lax.ppermute(value, ("seq", "fsdp"), [(i, (i + 8 * steps) % 32) for i in range(32)])
+    return lax.ppermute(value, ("z", "core", "fsdp"), [(i, (i + 8 * steps) % 32) for i in range(32)])
 
 
 def pick(stacked, index):
     return lax.dynamic_index_in_dim(stacked, index, 0, keepdims=False)
 
 
-def unswap(pieces, rank):
-    stacked = jnp.stack(pieces) if isinstance(pieces, (list, tuple)) else pieces
-    return jnp.stack([pick(stacked, j ^ rank) for j in range(stacked.shape[0])])
-
-
-def gather_quad(value):
+def exchange(value, axis="fsdp"):
+    return lax.all_to_all(value, axis, split_axis=0, concat_axis=0, tiled=True)
+
+
+def gather_near(value):
     half = value.shape[0] // 2
     by_x = swap(value, 1)
     by_y = swap(value, 2)
-    low_part = swap(by_x[:half], 2)
-    high_part = swap(by_y[half:], 1)
-    return jnp.concatenate([value, by_x, by_y, low_part, high_part], axis=0)
-
-
-def gather_plane(value):
-    quad = gather_quad(value)
-    return quad, swap(quad, 4)
-
-
-def sum_quad(blocks):
-    return (
-        blocks[0].astype(F32)
-        + swap(blocks[1].astype(BF), 1).astype(F32)
-        + swap(blocks[2].astype(BF), 2).astype(F32)
-        + swap(blocks[3].astype(BF), 3).astype(F32)
-    )
+    return [value, by_x, by_y, swap(by_x[:half], 2), swap(by_y[half:], 1)]
+
+
+def both_cores(near):
+    return near + [swap(piece, 4) for piece in near]
+
+
+def gather_pieces(value):
+    return both_cores(gather_near(value))
+
+
+def sum_quad(terms):
+    return terms[0].astype(F32) + sum(swap(terms[m].astype(BF), m).astype(F32) for m in (1, 2, 3))
 
 
 def sum_plane(near, far):
-    arrived = swap(far.astype(BF), 4).astype(F32)
-    total = near.astype(F32) + arrived
-    return sum_quad([total[m] for m in range(4)])
-
-
-def sum_all(value):
-    for mask in (4, 1, 2, 8, 16):
-        value = value + swap(value, mask)
-    return value
+    arrived = swap(far.astype(BF), 4)
+    return sum_quad([near[m].astype(F32) + arrived[m].astype(F32) for m in range(4)])
 
 
 def dot(left, right):
@@ -414,8 +405,8 @@
 
 
 def attend_kernel(
-    place_ref, split_ref, mixed_ref, cos_ref, ahead_ref, behind_ref,
-    q_ref, k_ref, v_ref, o_ref, log_ref, kz, vz,
+    split_ref, where_ref, mixed_ref, cos_ref, ahead_ref, behind_ref,
+    q_ref, k_ref, v_ref, o_ref, log_ref, mine_ref, theirs_ref, kz, vz,
 ):
     local_len = mixed_ref.shape[2]
     row_len = q_ref.shape[0]
@@ -423,7 +414,6 @@
 
     def prepare(i, carry):
         rows = pl.ds(pl.multiple_of(i * local_len, local_len), local_len)
-        source = place_ref[i]
         cosine, ahead, behind = cos_ref[rows], ahead_ref[rows], behind_ref[rows]
 
         def turn(x):
@@ -433,8 +423,8 @@
                 + pltpu.roll(x, ROT // 2, 1) * behind
             )
 
-        first = mixed_ref[source, 0]
-        second = mixed_ref[source, 1]
+        first = mixed_ref[i, 0]
+        second = mixed_ref[i, 1]
         turned0 = turn(first[:, : 2 * HD])
         turned1 = turn(second[:, : 2 * HD])
         q = jnp.where(low, turned0, pltpu.roll(turned1, HD, 1))
@@ -493,12 +483,17 @@
             logs.append(top + jnp.log(total))
         o_ref[rows] = (outs[0] + outs[1]).astype(BF)
         log_ref[rows] = jnp.where(low_q, logs[0], logs[1])
+        step = lax.rem(qb - where_ref[0] + 4, 4)
+        core = where_ref[1] // 4
+        half = BLOCK // 2
+        for ref, which in ((mine_ref, core), (theirs_ref, 1 - core)):
+            ref[step] = o_ref[pl.ds(pl.multiple_of(qb * BLOCK + which * half, half), half)]
         return carry
 
     lax.fori_loop(0, row_len // BLOCK, query_block, 0)
 
 
-def attend(place, split, mixed, tables):
+def attend(split, where, mixed, tables):
     row_len = tables[0].shape[0]
     packed = jax.ShapeDtypeStruct((row_len, 2 * HD), BF)
     smem = pl.BlockSpec(memory_space=pltpu.SMEM)
@@ -506,20 +501,19 @@
     pairs = 2 * row_len * row_len // 2
     return pl.pallas_call(
         attend_kernel,
-        out_shape=(packed, packed, packed, packed, jax.ShapeDtypeStruct((row_len, 2 * HD), F32)),
+        out_shape=(packed, packed, packed, packed, jax.ShapeDtypeStruct((row_len, 2 * HD), F32))
+        + (jax.ShapeDtypeStruct((4, row_len // 8, 2 * HD), BF),) * 2,
         in_specs=[smem, smem, vmem, vmem, vmem, vmem],
-        out_specs=(vmem,) * 5,
+        out_specs=(vmem,) * 7,
         scratch_shapes=[pltpu.VMEM((2, row_len, 2 * HD), BF), pltpu.VMEM((2, row_len, 2 * HD), BF)],
         compiler_params=pltpu.CompilerParams(vmem_limit_bytes=48 * 2**20),
-        cost_estimate=pl.CostEstimate(
-            flops=16 * pairs * HD, bytes_accessed=12 * 2**20, transcendentals=pairs
-        ),
+        cost_estimate=SMALL,
         name="attend",
-    )(place, split, mixed, *tables)
+    )(split, where, mixed, *tables)
 
 
 def attend_back_kernel(
-    place_ref, split_ref, q_ref, k_ref, v_ref, kt_ref, o_ref, do_ref, log_ref,
+    split_ref, q_ref, k_ref, v_ref, kt_ref, o_ref, do_ref, log_ref,
     cos_ref, ahead_ref, behind_ref,
     dmix_ref, dpos_ref, kz, vz, qz, dz, ktz, delta, dq_t, dk, dv,
 ):
@@ -592,13 +586,13 @@
     low_l = lax.broadcasted_iota(jnp.int32, (local_len, 2 * HD), 1) < HD
     per = 2 * HD // local_len
 
+
     def finish(b, carry):
-        both = pl.ds(pl.multiple_of(b * 2 * HD, 2 * HD), 2 * HD)
-        dq = dq_t[:, both].T * HD**-0.5
+        start = pl.multiple_of(b * 2 * HD, 2 * HD)
+        dq = dq_t[:, pl.ds(start, 2 * HD)].T * HD**-0.5
         for part in range(per):
             i = b * per + part
             rows = pl.ds(pl.multiple_of(i * local_len, local_len), local_len)
-            target = place_ref[i]
             cosine, ahead, behind = cos_ref[rows], ahead_ref[rows], behind_ref[rows]
 
             def turn(x, cosine=cosine, ahead=ahead, behind=behind):
@@ -616,18 +610,16 @@
             dpos_ref[rows, : 2 * HD] = first
             dpos_ref[rows, 2 * HD : 4 * HD] = second
             dpos_ref[rows, 4 * HD :] = v_part.astype(BF)
-            dmix_ref[target, 0, :, : 2 * HD] = first
-            dmix_ref[target, 1, :, : 2 * HD] = second
-            dmix_ref[target, 0, :, 2 * HD :] = jnp.where(low_l, v_part, 0.0).astype(BF)
-            dmix_ref[target, 1, :, 2 * HD :] = jnp.where(
-                low_l, pltpu.roll(v_part, HD, 1), 0.0
-            ).astype(BF)
+            dmix_ref[i, 0, :, : 2 * HD] = first
+            dmix_ref[i, 1, :, : 2 * HD] = second
+            dmix_ref[i, 0, :, 2 * HD :] = jnp.where(low_l, v_part, 0.0).astype(BF)
+            dmix_ref[i, 1, :, 2 * HD :] = jnp.where(low_l, pltpu.roll(v_part, HD, 1), 0.0).astype(BF)
         return carry
 
     lax.fori_loop(0, row_len // (2 * HD), finish, 0)
 
 
-def attend_back(place, split, q, k, v, k_t, out, d_out, logs, tables, local_len):
+def attend_back(split, q, k, v, k_t, out, d_out, logs, tables, local_len):
     row_len = q.shape[0]
     smem = pl.BlockSpec(memory_space=pltpu.SMEM)
     vmem = pl.BlockSpec(memory_space=pltpu.VMEM)
@@ -638,10 +630,10 @@
         attend_back_kernel,
         out_shape=(
             jax.ShapeDtypeStruct((row_len // local_len, 2, local_len, 4 * HD), BF),
-            jax.ShapeDtypeStruct((row_len, 6 * HD), BF),
-        ),
-        in_specs=[smem, smem] + [vmem] * 10,
-        out_specs=(vmem, vmem),
+        )
+        + (jax.ShapeDtypeStruct((row_len, 6 * HD), BF),),
+        in_specs=[smem] + [vmem] * 10,
+        out_specs=(vmem,) * 2,
         scratch_shapes=[
             masked, masked, masked, masked,
             pltpu.VMEM((2, 2 * HD, row_len), BF),
@@ -650,24 +642,451 @@
             whole, whole,
         ],
         compiler_params=pltpu.CompilerParams(vmem_limit_bytes=48 * 2**20),
-        cost_estimate=pl.CostEstimate(
-            flops=40 * pairs * HD, bytes_accessed=12 * 2**20, transcendentals=pairs
+        cost_estimate=SMALL,
+        name="attend_back",
+    )(split, q, k, v, k_t, out, d_out, logs, *tables)
+
+
+def pick_heads_kernel(where_ref, q_ref, k_ref, v_ref, out_ref):
+    wide = 2 * HD
+    low = lax.broadcasted_iota(jnp.int32, (q_ref.shape[0], wide), 1) < HD
+    for core in (0, 1):
+
+        @pl.when(where_ref[1] // 4 == core)
+        def _(core=core):
+            def join(left, right):
+                if core == 0:
+                    return jnp.where(low, left, pltpu.roll(right, HD, 1)).astype(BF)
+                return jnp.where(low, pltpu.roll(left, HD, 1), right).astype(BF)
+
+            for z in range(4):
+                cols = slice(z * wide, (z + 1) * wide)
+                out_ref[:, cols] = join(q_ref[:, cols].astype(F32), k_ref[:, cols].astype(F32))
+            for pair in range(2):
+                left, right = (
+                    v_ref[:, (2 * pair + n) * wide : (2 * pair + n + 1) * wide].astype(F32) for n in (0, 1)
+                )
+                out_ref[:, (4 + pair) * wide : (5 + pair) * wide] = join(left, right)
+
+
+def pick_heads(where, weight):
+    rows, columns = weight.shape
+    wide = columns // 12
+    blocks = [
+        pl.BlockSpec((rows, wide), lambda chip, where, part=part: (0, part * 4 + chip)) for part in range(3)
+    ]
+    return pl.pallas_call(
+        pick_heads_kernel,
+        grid_spec=pltpu.PrefetchScalarGridSpec(
+            num_scalar_prefetch=1,
+            grid=(4,),
+            in_specs=blocks,
+            out_specs=pl.BlockSpec((None, rows, 12 * HD), lambda chip, where: (chip, 0, 0)),
         ),
-        name="attend_back",
-    )(place, split, q, k, v, k_t, out, d_out, logs, *tables)
-
-
-def hidden_layer(mid, d_result, gate_up_pad, down_pad):
-    width = down_pad.shape[0]
-    gate_up = dot(mid, gate_up_pad)
-    gate, up = gate_up[:, :width], gate_up[:, width:]
-    sig = jax.nn.sigmoid(gate)
-    silu = gate * sig
-    act = (silu * up).astype(BF)
-    d_act = dot_rows(d_result, down_pad)
-    d_gate = d_act * up * (sig + silu * (1.0 - sig))
-    d_gate_up = jnp.concatenate([d_gate.astype(BF), (d_act * silu).astype(BF)], axis=1)
-    return act, d_gate_up
+        out_shape=jax.ShapeDtypeStruct((4, rows, 12 * HD), BF),
+        compiler_params=pltpu.CompilerParams(vmem_limit_bytes=32 * 2**20),
+        cost_estimate=SMALL,
+        name="pick_heads",
+    )(where, weight, weight, weight)
+
+
+def small_call(kernel, name, out_shape, where, *arrays, flops=0, scratch=(), limit=32):
+    size = sum(x.size * x.dtype.itemsize for x in arrays)
+    vmem = pl.BlockSpec(memory_space=pltpu.VMEM)
+    return pl.pallas_call(
+        kernel,
+        out_shape=out_shape,
+        in_specs=[pl.BlockSpec(memory_space=pltpu.SMEM)] + [vmem] * len(arrays),
+        out_specs=[vmem] * len(out_shape),
+        scratch_shapes=scratch,
+        compiler_params=pltpu.CompilerParams(vmem_limit_bytes=limit * 2**20),
+        cost_estimate=SMALL,
+        name=name,
+    )(where, *arrays)
+
+
+def pair_kernel(where_ref, mine_ref, theirs_ref, *outs):
+    low = lax.broadcasted_iota(jnp.int32, mine_ref.shape[1:], 1) < HD
+    for step, out in enumerate(outs):
+        for core, (ref0, ref1) in enumerate(((mine_ref, theirs_ref), (theirs_ref, mine_ref))):
+
+            @pl.when(where_ref[1] // 4 == core)
+            def _(ref0=ref0, ref1=ref1):
+                even, uneven = ref0[step].astype(F32), ref1[step].astype(F32)
+                out[:, : 2 * HD] = jnp.where(low, even, pltpu.roll(uneven, HD, 1)).astype(BF)
+                out[:, 2 * HD :] = jnp.where(low, pltpu.roll(even, HD, 1), uneven).astype(BF)
+
+
+def out_project_kernel(where_ref, a0, a1, a2, a3, weight_ref, att_ref, o0, o1, o2, o3, sum_v):
+    plane, rank = where_ref[0], where_ref[1] % 4
+    span = a0.shape[0]
+    for step, ref in enumerate((a0, a1, a2, a3)):
+        lanes = pl.ds(pl.multiple_of(lax.rem(plane - step + 4, 4) * 2 * HD, 2 * HD), 2 * HD)
+        for row in range(2):
+            att_ref[row * span : (row + 1) * span, lanes] = ref[:, row * 2 * HD : (row + 1) * 2 * HD]
+    sum_v[...] = dot(att_ref[...], weight_ref[...])
+    part = span // 4
+    for m, out in enumerate((o0, o1, o2, o3)):
+        for row in range(2):
+            rows = pl.ds(pl.multiple_of(row * span + (rank ^ m) * part, part), part)
+            out[row * part : (row + 1) * part] = sum_v[rows].astype(out.dtype)
+
+
+def d_att_kernel(where_ref, p0, p1, p2, p3_low, p3_high, weight_ref, branch_ref, heads_ref):
+    rank = where_ref[1] % 4
+    span = heads_ref.shape[1]
+    part = span // 4
+    for m, pieces in enumerate(((p0,), (p1,), (p2,), (p3_low, p3_high))):
+        for row in range(2):
+            rows = pl.ds(pl.multiple_of(row * span + (rank ^ m) * part, part), part)
+            if len(pieces) == 2:
+                branch_ref[rows] = pieces[row][...]
+            else:
+                branch_ref[rows] = pieces[0][row * part : (row + 1) * part]
+    d_att = dot_rows(branch_ref[...], weight_ref[...])
+    low = lax.broadcasted_iota(jnp.int32, heads_ref.shape[1:], 1) < HD
+    for z in range(4):
+        lanes = slice(z * 2 * HD, (z + 1) * 2 * HD)
+        row0, row1 = d_att[:span, lanes], d_att[span:, lanes]
+        heads_ref[2 * z] = jnp.where(low, row0, pltpu.roll(row1, HD, 1)).astype(BF)
+        heads_ref[2 * z + 1] = jnp.where(low, pltpu.roll(row0, HD, 1), row1).astype(BF)
+
+
+def d_in_kernel(where_ref, in_ref, weight_ref, near_ref, far_ref, x_v, d_v):
+    core, rank = where_ref[1] // 4, where_ref[1] % 4
+    reach, wide = in_ref.shape[1], 2 * HD
+    features = weight_ref.shape[0]
+    low = lax.broadcasted_iota(jnp.int32, (reach, wide), 1) < HD
+    for z in range(4):
+        for row in range(2):
+            x_v[row * reach : (row + 1) * reach, z * wide : (z + 1) * wide] = in_ref[
+                z, :, row * wide : (row + 1) * wide
+            ]
+    for pair in range(2):
+        cols = slice((4 + pair) * wide, (5 + pair) * wide)
+        one, two = (in_ref[2 * pair + n, :, 2 * wide :].astype(F32) for n in (0, 1))
+        x_v[:reach, cols] = jnp.where(low, one, pltpu.roll(two, HD, 1)).astype(BF)
+        x_v[reach:, cols] = jnp.where(low, pltpu.roll(one, HD, 1), two).astype(BF)
+    part = reach // 8
+    span = d_v.shape[1]
+
+    def columns(n, carry):
+        cols = pl.ds(pl.multiple_of(n * span, span), span)
+        d_v[...] = dot_rows(x_v[...], weight_ref[cols])
+        for ref, which in ((near_ref, core), (far_ref, 1 - core)):
+            for m in range(4):
+                for row in range(2):
+                    first = row * reach + which * 4 * part + (rank ^ m) * part
+                    rows = pl.ds(pl.multiple_of(first, part), part)
+                    ref[m, row * part : (row + 1) * part, cols] = d_v[rows].astype(BF)
+        return carry
+
+    lax.fori_loop(0, features // span, columns, 0)
+
+
+def hidden_kernel(where_ref, *refs, steps, own):
+    n_mid, n_out = (10, 2) if own else (1, 4 * len(steps))
+    mids, outs, refs = refs[:n_mid], refs[n_mid : n_mid + n_out], refs[n_mid + n_out :]
+    gate_ref, up_ref, down_ref = refs[:3]
+    refs = refs[3:] if own else refs[7:]
+    alls, refs = refs[:4], refs[4:]
+    d_mids, acts, refs = (refs[:2], refs[2:4], refs[4:]) if own else ((), (), refs)
+    mid_v, out_v, gate_up_v, down_v, act_v, d_gate_v, d_up_v, sem_in, sem_w, sem_out = refs[:10]
+    rows, features = mid_v.shape[1:]
+    width, tile = down_v.shape[0], 256
+    tiles = width // tile
+    plane, mine = where_ref[0], where_ref[1]
+    core = mine // 4
+    shard = gate_ref.shape[1]
+    step = rows // 4
+    halves = 2 * len(steps)
+
+    def blocks(h):
+        base = lax.rem(plane + 4 - steps[h // 2], 4) * (2 * rows)
+        return [
+            pl.ds(pl.multiple_of(base + (mine ^ (4 * (h % 2) + m)) * step, step), step) for m in range(4)
+        ]
+
+    def loads(h):
+        slot = h % 2
+        if own:
+            pieces, out_pieces = mids[5 * h : 5 * h + 5], outs[h : h + 1]
+        else:
+            pieces = [mids[0].at[block] for block in blocks(h)]
+            out_pieces = outs[2 * h : 2 * h + 2]
+        found = []
+        for held, sources in ((mid_v, pieces), (out_v, out_pieces)):
+            at = 0
+            for source in sources:
+                size = source.shape[0]
+                found.append((source, held.at[slot, pl.ds(at, size)]))
+                at += size
+        return [pltpu.make_async_copy(x, y, sem_in.at[slot, n]) for n, (x, y) in enumerate(found)]
+
+    def stores(h):
+        slot = h % 2
+        return [
+            pltpu.make_async_copy(
+                held.at[slot, pl.ds(m * step, step)], target.at[block], sem_out.at[slot, n, m]
+            )
+            for n, (held, target) in enumerate(zip((act_v, d_gate_v, d_up_v, out_v), alls))
+            for m, block in enumerate(blocks(h))
+        ]
+
+    def tile_copies(j):
+        cols = pl.ds(j * tile, tile)
+        found = [
+            (ref.at[m, :, cols], gate_up_v.at[g, pl.ds(m * shard, shard), cols])
+            for g, ref in enumerate((gate_ref, up_ref))
+            for m in range(4)
+        ]
+        first = pl.multiple_of(core * (down_ref.shape[0] - width) + j * tile, 128)
+        found.append((down_ref.at[pl.ds(first, tile)], down_v.at[cols]))
+        return [pltpu.make_async_copy(x, y, sem_w.at[j, n]) for n, (x, y) in enumerate(found)]
+
+    def wait_tile(j):
+        for copy in weight_copies[j]:
+            copy.wait()
+        if j == 0:
+
+            @pl.when(core == 1)
+            def _():
+                gate_up_v[:, :, : 2 * width - down_ref.shape[0]] = jnp.zeros(
+                    (2, features, 2 * width - down_ref.shape[0]), BF
+                )
+
+    def compute(slot, cols):
+        gate = dot(mid_v[slot], gate_up_v[0, :, cols])
+        up = dot(mid_v[slot], gate_up_v[1, :, cols])
+        d_act = dot_rows(out_v[slot], down_v[cols])
+        sig = 1.0 / (1.0 + jnp.exp(-gate))
+        silu = gate * sig
+        act_v[slot, :, cols] = (silu * up).astype(BF)
+        d_gate_v[slot, :, cols] = (d_act * up * (sig + silu * (1.0 - sig))).astype(BF)
+        d_up_v[slot, :, cols] = (d_act * silu).astype(BF)
+
+    weight_copies = [tile_copies(j) for j in range(tiles)]
+    for copies in [weight_copies[0], loads(0)] + weight_copies[1:] + [loads(1)]:
+        for copy in copies:
+            copy.start()
+    for h in range(halves):
+        slot = h % 2
+        for copy in loads(h):
+            copy.wait()
+        if h == 0:
+            for j in range(tiles):
+                wait_tile(j)
+                compute(0, pl.ds(j * tile, tile))
+        else:
+            compute(slot, pl.ds(0, tile))
+            if h + 1 < halves:
+                for copy in stores(h - 1):
+                    copy.wait()
+                for copy in loads(h + 1):
+                    copy.start()
+
+            def part(j, carry, slot=slot):
+                compute(slot, pl.ds(pl.multiple_of(j * tile, tile), tile))
+                return carry
+
+            lax.fori_loop(1, tiles, part, 0)
+        for copy in stores(h):
+            copy.start()
+    left = []
+    if own:
+        sum_v = refs[10]
+        span = 512
+        for i in (1, 0):
+            for m in range(4):
+                part = pl.ds(m * step, step)
+                left.append(
+                    pltpu.make_async_copy(act_v.at[i, part], acts[i].at[m], sem_out.at[i, 4, m])
+                )
+                left[-1].start()
+
+            def term(n, carry, i=i):
+                cols = pl.ds(pl.multiple_of(n * span, span), span)
+                sum_v[i, :, cols] = (
+                    dot_rows(d_gate_v[i], gate_up_v[0, cols]) + dot_rows(d_up_v[i], gate_up_v[1, cols])
+                ).astype(BF)
+                return carry
+
+            lax.fori_loop(0, features // span, term, 0)
+            for m in range(4):
+                part = pl.ds(m * step, step)
+                left.append(
+                    pltpu.make_async_copy(sum_v.at[i, part], d_mids[i].at[m], sem_out.at[i, 5, m])
+                )
+                left[-1].start()
+    for h in (halves - 2, halves - 1):
+        left += stores(h)
+    for copy in left:
+        copy.wait()
+
+
+def hidden_layer(where, mids, outs, weights, total, steps=(0,), before=None):
+    own = before is None
+    features = outs[0].shape[1]
+    rows, width = total // 8, weights[0].shape[2]
+    narrow = jax.ShapeDtypeStruct((total, width), BF)
+    wide = jax.ShapeDtypeStruct((total, features), BF)
+    term = jax.ShapeDtypeStruct((4, rows // 4, features), BF)
+    act = jax.ShapeDtypeStruct((4, rows // 4, width), BF)
+    held = pltpu.VMEM((2, rows, features), BF)
+    small = pltpu.VMEM((2, rows, width), BF)
+    dma = pltpu.SemaphoreType.DMA
+    count = len(mids) + len(outs)
+    kept = [] if own else list(before)
+    hbm = pl.BlockSpec(memory_space=pl.ANY)
+    found = pl.pallas_call(
+        functools.partial(hidden_kernel, steps=steps, own=own),
+        in_specs=[pl.BlockSpec(memory_space=pltpu.SMEM)] + [hbm] * (count + 3 + len(kept)),
+        out_specs=[hbm] * (8 if own else 4),
+        out_shape=[narrow, narrow, narrow, wide] + ([term, term, act, act] if own else []),
+        input_output_aliases={count + 4 + n: n for n in range(len(kept))},
+        scratch_shapes=[
+            held, held,
+            pltpu.VMEM((2, features, width), BF),
+            pltpu.VMEM((width, features), BF),
+            small, small, small,
+            dma((2, 9)), dma((width // 256, 9)), dma((2, 6, 4)),
+        ]
+        + ([held] if own else []),
+        compiler_params=pltpu.CompilerParams(vmem_limit_bytes=48 * 2**20),
+        cost_estimate=SMALL,
+        name="hidden",
+    )(where, *mids, *outs, *weights, *kept)
+    return list(found[:4]), list(found[4:])
+
+
+def weight_grad_kernel(left_ref, right_ref, out_ref):
+    out_ref[...] = dot_cols(left_ref[...], right_ref[...]).astype(BF)
+
+
+def weight_grad(left, right):
+    tokens, features = left.shape
+    width = right.shape[1]
+    step = 256
+    return pl.pallas_call(
+        weight_grad_kernel,
+        grid=(features // step,),
+        in_specs=[
+            pl.BlockSpec((tokens, step), lambda i: (0, i)),
+            pl.BlockSpec((tokens, width), lambda i: (0, 0), pipeline_mode=pl.Buffered(1)),
+        ],
+        out_specs=pl.BlockSpec((step, width), lambda i: (i, 0)),
+        out_shape=jax.ShapeDtypeStruct((features, width), BF),
+        compiler_params=pltpu.CompilerParams(vmem_limit_bytes=48 * 2**20),
+        cost_estimate=SMALL,
+        name="weight_grad",
+    )(left, right)
+
+
+def place_columns_kernel(where_ref, own_ref, other_ref, *rest):
+    out_ref = rest[-1]
+    wide = own_ref.shape[-1]
+    extra = out_ref.shape[-1] - wide
+
+    @pl.when(where_ref[0] == 0)
+    def _():
+        out_ref[:, :wide] = own_ref[...].astype(F32)
+        out_ref[:, wide:] = other_ref[:, wide - extra :].astype(F32)
+
+    @pl.when(where_ref[0] == 1)
+    def _():
+        out_ref[:, :wide] = other_ref[...].astype(F32)
+        out_ref[:, wide:] = own_ref[:, wide - extra :].astype(F32)
+
+
+def place_columns(core, own, other, before, chip_width, kind):
+    chips, rows, wide = own.shape
+    cut = rows // 2
+    half = pl.BlockSpec((None, cut, wide), lambda chip, b, core: (chip, b, 0))
+    return pl.pallas_call(
+        place_columns_kernel,
+        grid_spec=pltpu.PrefetchScalarGridSpec(
+            num_scalar_prefetch=1,
+            grid=(chips, rows // cut),
+            in_specs=[half, half] + ([] if before is None else [pl.BlockSpec(memory_space=pl.ANY)]),
+            out_specs=pl.BlockSpec((cut, chip_width), lambda chip, b, core: (b, kind * chips + chip)),
+        ),
+        out_shape=jax.ShapeDtypeStruct((rows, 2 * chips * chip_width), F32),
+        input_output_aliases={} if before is None else {3: 0},
+        compiler_params=pltpu.CompilerParams(vmem_limit_bytes=32 * 2**20),
+        cost_estimate=SMALL,
+        name="place_columns",
+    )(core, own, other, *([] if before is None else [before]))
+
+
+def place_down_kernel(core_ref, own_ref, other_ref, out_ref, *, lead):
+    first = pl.program_id(0) < lead
+    mine = first == (core_ref[0] == 0)
+
+    @pl.when(mine)
+    def _():
+        out_ref[...] = own_ref[...].astype(F32)
+
+    @pl.when(jnp.logical_not(mine))
+    def _():
+        out_ref[...] = other_ref[...].astype(F32)
+
+
+def place_down(core, own, other, total):
+    width, features = own.shape
+    step = 128
+    count, lead = total // step, width // step
+    skip = 2 * lead - count
+
+    def block(of_core):
+        def index(i, core):
+            which = core[0] if of_core else 1 - core[0]
+            return (jnp.where(which == 0, jnp.minimum(i, lead - 1), jnp.maximum(i - lead + skip, 0)), 0)
+
+        return pl.BlockSpec((step, features), index)
+
+    return pl.pallas_call(
+        functools.partial(place_down_kernel, lead=lead),
+        grid_spec=pltpu.PrefetchScalarGridSpec(
+            num_scalar_prefetch=1,
+            grid=(count,),
+            in_specs=[block(True), block(False)],
+            out_specs=pl.BlockSpec((step, features), lambda i, core: (i, 0)),
+        ),
+        out_shape=jax.ShapeDtypeStruct((total, features), F32),
+        cost_estimate=SMALL,
+        name="place_down",
+    )(core, own, other)
+
+
+def place_qkv_kernel(where_ref, own_ref, other_ref, out_ref):
+    cut = own_ref.shape[2]
+    core = where_ref[0]
+    for ref, half in ((own_ref, core), (other_ref, 1 - core)):
+        rows = pl.ds(pl.multiple_of(half * cut, cut), cut)
+        for z in range(4):
+            out_ref[rows, z * 2 * HD : (z + 1) * 2 * HD] = ref[z, 0].astype(F32)
+
+
+def place_qkv(where, own, other):
+    _, _, cut, wide = own.shape
+    parts = wide // (2 * HD)
+    piece = pl.BlockSpec((4, 1, cut, 2 * HD), lambda part, chip, where: (0, chip, 0, part))
+    return pl.pallas_call(
+        place_qkv_kernel,
+        grid_spec=pltpu.PrefetchScalarGridSpec(
+            num_scalar_prefetch=1,
+            grid=(parts, 4),
+            in_specs=[piece, piece],
+            out_specs=pl.BlockSpec((2 * cut, 8 * HD), lambda part, chip, where: (0, part * 4 + chip)),
+        ),
+        out_shape=jax.ShapeDtypeStruct((2 * cut, parts * 32 * HD), F32),
+        cost_estimate=SMALL,
+        name="place_qkv",
+    )(where, own, other)
+
+
+def tie(*values):
+    return lax.optimization_barrier(values)
 
 
 def plane_plan(
@@ -687,202 +1106,203 @@
     row_count, local_len, features = inputs.shape
     row_len = segments.shape[1]
     tokens = row_count * local_len
-    seq = lax.axis_index("seq")
-    rank = lax.axis_index("fsdp")
-    core = seq % 2
-    plane = seq // 2
+    plane, core, rank = lax.axis_index("z"), lax.axis_index("core"), lax.axis_index("fsdp")
+    seq = plane * 2 + core
     own = core * 4 + rank
     shard = features // 4
     hidden = gate_up_weight.shape[1] // 2
-    share = hidden // 8
-    padded = -(-share // 128) * 128
+    chip_width = hidden // 4
+    width = -(-chip_width // 256) * 128
     tables = turn_tables(row_len)
     split = jnp.sum((segments == 0).astype(jnp.int32), axis=1)
-    canon = jnp.arange(32, dtype=jnp.int32)
-    place = ((plane - canon // 8) % 4) * 8 + ((canon % 8) ^ own)
-
-    def head_columns(m):
-        first = ((rank ^ m) * 8 + seq) * HD
-        parts = [
-            lax.dynamic_slice_in_dim(qkv_weight, first + part * features, HD, 1) for part in (0, 1, 2)
-        ]
-        return jnp.concatenate(parts + parts[2:], axis=1)
-
-    head_weight = unswap(
-        [head_columns(0)] + [swap(head_columns(m), m) for m in (1, 2, 3)], rank
-    ).reshape(features, 4 * HD)
+    where = jnp.stack([plane, own]).astype(jnp.int32)
+
+    head_all = exchange(pick_heads(where, qkv_weight)).reshape(features, 12 * HD)
+    value = lax.dynamic_slice_in_dim(head_all, 8 * HD + plane * HD, HD, 1)
+    head_weight = jnp.concatenate(
+        [lax.dynamic_slice_in_dim(head_all, plane * 2 * HD, 2 * HD, 1), value, value], axis=1
+    )
     head_first = (rank * 8 + seq) * HD
     bias_parts = [
         lax.dynamic_slice_in_dim(qkv_bias, head_first + part * features, HD, 0) for part in (0, 1, 2)
     ]
     head_bias = jnp.concatenate(bias_parts + bias_parts[2:])
+    hidden_first = core * (chip_width - width)
+
+    def hidden_columns(kind):
+        firsts = [hidden_first + chip * chip_width + kind * hidden for chip in range(4)]
+        return jnp.stack([lax.dynamic_slice_in_dim(gate_up_weight, first, width, 1) for first in firsts])
+
+    gate_weight, up_weight = hidden_columns(0), hidden_columns(1)
 
     flat = inputs.reshape(tokens, features).astype(F32)
     normed_in, norm1_back = jax.vjp(layer_norm, flat, norm1_gain, norm1_bias)
-    chunk = normed_in.astype(BF)
-    in_halves = []
-    for k in range(4):
-        in_halves += list(gather_plane(chunk))
-        if k < 3:
-            chunk = shift(chunk, 1)
-    mixed = jnp.concatenate([dot(half, head_weight) + head_bias for half in in_halves], axis=0)
-    q, k, v, out_heads, logs = attend(
-        place, split, mixed.reshape(row_len // local_len, row_count, local_len, 4 * HD), tables
-    )
-
+    everywhere = ("z", "core", "fsdp")
+    in_all = lax.all_gather(normed_in.astype(BF), everywhere, axis=0, tiled=True)
+    d_out = cotangent.reshape(tokens, features)
+    out_near = jnp.concatenate(gather_near(d_out), axis=0)
+    out_far = swap(out_near, 4)
+    in_all, out_near, out_far, gate_weight, up_weight, head_weight, head_all, *tables = tie(
+        in_all, out_near, out_far, gate_weight, up_weight, head_weight, head_all, *tables
+    )
+    lows, highs = [out_near[: 2 * tokens]], [out_near[2 * tokens :]]
+
+    mixed = (dot(in_all, head_weight) + head_bias).reshape(
+        row_len // local_len, row_count, local_len, 4 * HD
+    )
+    q, k, v, out_heads, logs, mine, theirs, gate_weight, low, up_weight = tie(
+        *attend(split, where, mixed, tables), exchange(gate_weight), shift(lows[0], 1), up_weight
+    )
+    lows.append(low)
     span = row_len // 8
-    sent = [lax.dynamic_slice_in_dim(out_heads, (seq ^ m) * span, span, 0) for m in range(8)]
-    arrived = [sent[0]] + [swap(sent[m], m * 4) for m in range(1, 8)]
-    att = (
-        unswap(arrived, seq)
-        .reshape(8, span, row_count, HD)
-        .transpose(2, 1, 0, 3)
-        .reshape(row_count, 4, local_len, shard)
-    )
-    branch = dot(att.reshape(row_count * span, shard), out_weight).reshape(
-        row_count, 4, local_len, features
-    )
-    branch = branch.transpose(1, 0, 2, 3)
-    middle = flat + sum_quad([pick(branch, rank ^ m).reshape(tokens, features) for m in range(4)])
+    pair = jax.ShapeDtypeStruct((span, 4 * HD), BF)
+    pairs = small_call(pair_kernel, "pair", [pair] * 4, where, mine, swap(theirs, 4))
+    arrived = [pairs[0]] + [shift(pairs[n], n) for n in (1, 2, 3)]
+    square = row_count * span
+    block = jax.ShapeDtypeStruct((tokens, features), BF)
+    blocks = jax.ShapeDtypeStruct((4, tokens, features), BF)
+    att, *branch = small_call(
+        out_project_kernel,
+        "out_project",
+        [jax.ShapeDtypeStruct((square, shard), BF), jax.ShapeDtypeStruct((tokens, features), F32)]
+        + [block] * 3,
+        where,
+        *arrived,
+        out_weight,
+        scratch=[pltpu.VMEM((square, features), F32)],
+    )
+    branch_sum, up_weight, high = tie(sum_quad(branch), exchange(up_weight), shift(highs[0], 1))
+    highs.append(high)
+    hidden_weights = [gate_weight, up_weight, down_weight]
+    middle = flat + branch_sum
     normed_mid, norm2_back = jax.vjp(layer_norm, middle, norm2_gain, norm2_bias)
     mid_low = normed_mid.astype(BF)
-    mid_near, mid_far = gather_plane(mid_low)
-
-    def hidden_columns(m):
-        first = (rank ^ m) * 2 * share + core * share
-        return jnp.concatenate(
-            [
-                lax.dynamic_slice_in_dim(gate_up_weight, first, share, 1),
-                lax.dynamic_slice_in_dim(gate_up_weight, first + hidden, share, 1),
-            ],
-            axis=1,
-        )
-
-    gate_up_cols = unswap(
-        [hidden_columns(0)] + [swap(hidden_columns(m), m) for m in (1, 2, 3)], rank
-    ).reshape(features, 2, share)
-    gate_up_pad = jnp.pad(gate_up_cols, ((0, 0), (0, 0), (0, padded - share))).reshape(
-        features, 2 * padded
-    )
-    down_pad = jnp.pad(
-        lax.dynamic_slice_in_dim(down_weight, core * share, share, 0),
-        ((0, padded - share), (0, 0)),
-    )
-    d_out = cotangent.reshape(tokens, features)
-    out_near, out_far = gather_plane(d_out)
-
-    act_far, d_gu_far = hidden_layer(mid_far, out_far, gate_up_pad, down_pad)
-    act_near, d_gu_near = hidden_layer(mid_near, out_near, gate_up_pad, down_pad)
-    blocks = (4, tokens, features)
-    d_norm_mid = sum_plane(
-        dot_rows(d_gu_near, gate_up_pad).reshape(blocks),
-        dot_rows(d_gu_far, gate_up_pad).reshape(blocks),
-    )
+
+    mid_pieces = gather_pieces(mid_low)
+    *mid_pieces, mid_own, low = tie(*mid_pieces, mid_low, shift(lows[1], 1))
+    lows.append(low)
+    mid_all = lax.all_gather(mid_own, everywhere, axis=0, tiled=True)
+    total = row_count * row_len
+    hidden_all, (d_near, d_far, act_near, act_far) = hidden_layer(
+        where, mid_pieces, [out_near, out_far], hidden_weights, total
+    )
+    d_near, d_far, high = tie(d_near, d_far, shift(highs[1], 1))
+    highs.append(high)
+    d_norm_mid, low = tie(sum_plane(d_near, d_far), shift(lows[2], 1))
+    lows.append(low)
     d_middle_part, d_gain_two, d_bias_two = norm2_back(d_norm_mid)
     d_middle = d_out.astype(F32) + d_middle_part
-    d_branch = gather_quad(d_middle.astype(BF))
-    result = middle + sum_plane(
-        dot(act_near, down_pad).reshape(blocks), dot(act_far, down_pad).reshape(blocks)
-    )
-
-    d_att = dot_rows(d_branch, out_weight).astype(BF)
-    d_att = unswap(d_att.reshape(4, row_count, local_len, 8, HD), rank)
-    d_att = d_att.transpose(3, 0, 2, 1, 4).reshape(8, span, row_count * HD)
-    sent = [pick(d_att, seq ^ m) for m in range(8)]
-    arrived = [sent[0]] + [swap(sent[m], m * 4) for m in range(1, 8)]
-    d_heads = unswap(arrived, seq).reshape(row_len, row_count * HD)
+
+    d_pieces = gather_near(d_middle.astype(BF))
+    d_pieces[4], high = tie(d_pieces[4], shift(highs[2], 1))
+    highs.append(high)
+    d_branch, d_heads = small_call(
+        d_att_kernel,
+        "d_att",
+        [
+            jax.ShapeDtypeStruct((square, features), BF),
+            jax.ShapeDtypeStruct((8, span, 2 * HD), BF),
+        ],
+        where,
+        *d_pieces,
+        out_weight,
+    )
+    d_heads = exchange(d_heads, ("z", "core")).reshape(row_len, 2 * HD)
     log_rows = jnp.stack([logs[:, 0], logs[:, HD]])
     d_mixed, d_packed = attend_back(
-        place, split, q, k, v, k.T, out_heads, d_heads, log_rows, tables, local_len
-    )
-
-    reach = row_len // 4
-    sent = [lax.dynamic_slice_in_dim(d_packed, (plane + s) % 4 * reach, reach, 0) for s in range(4)]
-    arrived = jnp.stack([sent[0]] + [shift(sent[s], s) for s in (1, 2, 3)])
-    weights = [head_weight]
-    for _ in range(3):
-        weights.append(shift(weights[-1], 1))
-    weights = jnp.stack(weights)
-    near_weight = jnp.concatenate(
-        [
-            weights[:, :, : 2 * HD].transpose(1, 0, 2).reshape(features, 8 * HD),
-            weights[:, :, 2 * HD : 3 * HD].transpose(1, 0, 2).reshape(features, 4 * HD),
+        split, q, k, v, k.T, out_heads, d_heads, log_rows, tables, local_len
+    )
+    d_packed, d_mixed, mid_all = tie(d_packed, d_mixed, mid_all)
+
+    arrived = exchange(d_packed.reshape(4, row_len // 4, 6 * HD), "z")
+    d_mixed = d_mixed.reshape(row_len * row_count, 4 * HD)
+    head_grad = dot_cols(in_all, d_mixed)[:, : 3 * HD].astype(BF)
+    down = lax.dynamic_slice_in_dim(down_weight, hidden_first, width, 0)
+    result_sum = sum_plane(
+        dot(act_near.reshape(4 * tokens, width), down).reshape(4, tokens, features),
+        dot(act_far.reshape(4 * tokens, width), down).astype(BF).reshape(4, tokens, features),
+    )
+
+    def rest(steps, before):
+        outs = [
+            piece for n in steps for piece in (lows[n], highs[n], swap(lows[n], 4), swap(highs[n], 4))
+        ]
+        return hidden_layer(where, [mid_all], outs, hidden_weights, total, steps, before)[0]
+
+    hidden_all = rest((1, 2), hidden_all)
+    arrived, result_sum, head_grad, att, d_branch, *hidden_all = tie(
+        arrived, result_sum, head_grad, att, d_branch, *hidden_all
+    )
+    result = middle + result_sum
+    near, far = small_call(
+        d_in_kernel,
+        "d_in",
+        [blocks] * 2,
+        where,
+        arrived,
+        head_all,
+        scratch=[
+            pltpu.VMEM((8 * tokens, 12 * HD), BF),
+            pltpu.VMEM((8 * tokens, 512), F32),
         ],
-        axis=1,
-    )
-    tiles = arrived.reshape(4, reach, 3, 2 * HD)
-    lines = []
-    for row in range(2):
-        lines.append(
-            jnp.concatenate(
-                [
-                    tiles[:, :, row].transpose(1, 0, 2).reshape(reach, 8 * HD),
-                    tiles[:, :, 2, row * HD : (row + 1) * HD].transpose(1, 0, 2).reshape(reach, 4 * HD),
-                ],
-                axis=1,
-            )
-        )
-    d_in = dot_rows(jnp.concatenate(lines, axis=0), near_weight)
-    d_in = d_in.reshape(row_count, 8, local_len, features).transpose(1, 0, 2, 3)
-    near = jnp.stack([pick(d_in, own ^ m).reshape(tokens, features) for m in range(4)])
-    far = jnp.stack([pick(d_in, own ^ (m + 4)).reshape(tokens, features) for m in range(4)])
-    d_norm_in = sum_plane(near, far)
+        limit=48,
+    )
+    cut = shard // 2
+    head_grad = head_grad.reshape(4, 2, cut, 3 * HD)
+    mine = lax.dynamic_index_in_dim(head_grad, core, 1, keepdims=False)
+    theirs = swap(lax.dynamic_index_in_dim(head_grad, 1 - core, 1, keepdims=False), 4)
+    first, second = jnp.where(core == 0, mine, theirs), jnp.where(core == 0, theirs, mine)
+    pairs = jnp.concatenate(
+        [half[:, :, p * HD : (p + 1) * HD] for p in range(3) for half in (first, second)], axis=2
+    )
+    heads = lax.all_gather(exchange(pairs), "z", axis=0)
+
+    out_part = dot_cols(att, d_branch).astype(BF)
+    out_part = lax.psum_scatter(out_part, ("z", "core"), scatter_dimension=0, tiled=True)
+    out_rows = lax.all_gather(out_part, ("z", "core"), axis=0, tiled=True)
+
+    far, near, *hidden_all = tie(swap(far, 4), near, *hidden_all)
+    hidden_all = rest((3,), hidden_all)
+    act_all, d_gate_all, d_up_all, out_all = hidden_all
+    d_norm_in, d_gate_all = tie(
+        sum_quad([near[m].astype(F32) + far[m].astype(F32) for m in range(4)]), d_gate_all
+    )
     d_flat_part, d_gain_one, d_bias_one = norm1_back(d_norm_in)
     d_inputs = d_middle + d_flat_part
 
-    d_mixed = d_mixed.reshape(row_len * row_count, 4 * HD)
-    head_grad = dot_cols(jnp.concatenate(in_halves, axis=0), d_mixed)[:, : 3 * HD].astype(BF)
-    head_grad = head_grad.reshape(4, shard, 3 * HD)
-    head_rows = unswap(
-        [pick(head_grad, rank)] + [swap(pick(head_grad, rank ^ m), m) for m in (1, 2, 3)], rank
-    )
-    qkv_grad = lax.all_gather(head_rows, "seq", axis=0)
-    qkv_grad = (
-        qkv_grad.reshape(8, 4, shard, 3, HD).transpose(2, 3, 1, 0, 4).reshape(shard, 3 * features)
-    ).astype(F32)
     bias_sum = jnp.sum(d_mixed.astype(F32), axis=0)
     bias_own = jnp.zeros((3 * features,), F32)
     for part in range(3):
         bias_own = lax.dynamic_update_slice_in_dim(
             bias_own, bias_sum[part * HD : (part + 1) * HD], head_first + part * features, 0
         )
-
-    att_order = jnp.stack([pick(att.transpose(1, 0, 2, 3), rank ^ m) for m in range(4)])
-    out_part = dot_cols(att_order.reshape(4 * tokens, shard), d_branch).astype(BF)
-    out_part = lax.psum_scatter(out_part, "seq", scatter_dimension=0, tiled=True)
-    out_grad = lax.all_gather(out_part, "seq", axis=0, tiled=True).astype(F32)
-
-    def gather_rest(value):
-        pieces = [shift(value, 1)]
-        for _ in range(2):
-            pieces.append(shift(pieces[-1], 1))
-        return gather_plane(jnp.concatenate(pieces, axis=0))
-
-    mid_rest = gather_rest(mid_low)
-    out_rest = gather_rest(d_out)
-    rest = [hidden_layer(m, o, gate_up_pad, down_pad) for m, o in zip(mid_rest, out_rest)]
-    mid_all = jnp.concatenate([mid_near, mid_far, *mid_rest], axis=0)
-    out_all = jnp.concatenate([out_near, out_far, *out_rest], axis=0)
-    act_all = jnp.concatenate([act_near, act_far, rest[0][0], rest[1][0]], axis=0)
-    d_gu_all = jnp.concatenate([d_gu_near, d_gu_far, rest[0][1], rest[1][1]], axis=0)
-    down_own = dot_cols(act_all, out_all)[:share].astype(BF)
-    down_other = swap(down_own, 4)
-    down_pair = jnp.stack([down_own, down_other])
-    down_grad = jnp.concatenate([pick(down_pair, core), pick(down_pair, 1 - core)], axis=0).astype(F32)
-    gate_up_own = dot_cols(mid_all, d_gu_all).reshape(features, 2, padded)[:, :, :share].astype(BF)
-    gate_up_own = gate_up_own.reshape(4, shard, 2 * share)
-    gate_up_rows = unswap(
-        [pick(gate_up_own, rank)] + [swap(pick(gate_up_own, rank ^ m), m) for m in (1, 2, 3)], rank
-    )
-    gate_up_pair = jnp.stack([gate_up_rows, swap(gate_up_rows, 4)])
-    gate_up_pair = jnp.stack([pick(gate_up_pair, core), pick(gate_up_pair, 1 - core)])
-    gate_up_grad = (
-        gate_up_pair.reshape(2, 4, shard, 2, share)
-        .transpose(2, 3, 1, 0, 4)
-        .reshape(shard, 2 * hidden)
-        .astype(F32)
-    )
-    sums = sum_all(jnp.concatenate([d_gain_one, d_bias_one, bias_own, d_gain_two, d_bias_two]))
+    sums = jnp.concatenate([d_gain_one, d_bias_one, bias_own, d_gain_two, d_bias_two])
+    sums = sums + swap(sums, 4)
+    sums = sums + sum(swap(sums, m) for m in (1, 2, 3))
+
+    d_gate_grad, sums, d_up_all = tie(
+        weight_grad(mid_all, d_gate_all), sums + sum(shift(sums, n) for n in (1, 2, 3)), d_up_all
+    )
+    by_chip = (4, shard, width)
+    gate_parts, d_up_grad, act_all, out_rows, heads = tie(
+        exchange(d_gate_grad.reshape(by_chip)),
+        weight_grad(mid_all, d_up_all),
+        act_all,
+        out_rows,
+        heads,
+    )
+    core_index = core.reshape(1).astype(jnp.int32)
+    up_parts, down_own, gate_up_grad = tie(
+        exchange(d_up_grad.reshape(by_chip)),
+        weight_grad(act_all, out_all),
+        place_columns(core_index, gate_parts, swap(gate_parts, 4), None, chip_width, 0),
+    )
+    down_grad = place_down(core_index, down_own, swap(down_own, 4), chip_width)
+    qkv_grad = place_qkv(core_index, heads, swap(heads, 4))
+    out_grad = out_rows.astype(F32)
+    gate_up_grad = place_columns(
+        core_index, up_parts, swap(up_parts, 4), gate_up_grad, chip_width, 1
+    )
     return (
         result.reshape(row_count, local_len, features),
         d_inputs.reshape(row_count, local_len, features),
@@ -899,8 +1319,13 @@
 
 
 def solution(mesh):
+    planes = (mesh.shape["seq"], mesh.shape["fsdp"]) == (8, 4)
+    plan = plane_plan if planes else general_plan
+    if planes:
+        mesh = jax.sharding.Mesh(mesh.devices.reshape(4, 2, 4), ("z", "core", "fsdp"))
+    spread = P(None, (*mesh.axis_names,), None)
     placed = (
-        P(None, ("seq", "fsdp"), None),
+        spread,
         P(),
         P(),
         P(),
@@ -911,16 +1336,15 @@
         P(),
         P("fsdp", None),
         P("fsdp", None),
-        P(None, ("seq", "fsdp"), None),
-    )
-    plan = plane_plan if (mesh.shape["seq"], mesh.shape["fsdp"]) == (8, 4) else general_plan
+        spread,
+    )
     return jax.shard_map(
         plan,
         mesh=mesh,
         in_specs=placed,
         out_specs=(
-            P(None, ("seq", "fsdp"), None),
-            P(None, ("seq", "fsdp"), None),
+            spread,
+            spread,
             P(),
             P(),
             P("fsdp", None),

time: 1220 us -> 794 us (0.65)
  local copies, waits for them, and re-layouts: 381 us -> 59.6 us
  Pallas kernels: 49.5 us -> 247 us
  matrix products: 178 us -> 32.2 us
  waiting for transfers between devices: 364 us -> 283 us
  other arithmetic: 107 us -> 41.1 us
  starting transfers between devices: 109 us -> 88.3 us
  blocking collectives: 0 us -> 15 us
    pallas_call x0 -> x15, Pallas kernels: none -> 198 us  [the longest x3 84.4 us: hidden_layer(): pl.pallas_call(functools.partial(hidden_kernel, steps=steps, own=own), in...]
    ppermute x107 -> x61, waiting for transfers between devices: 364 us -> 173 us  [the longest x49 156 us: swap(): lax.ppermute(value, ('z', 'core', 'fsdp'), [(i, i ^ mask) for i in range(...]
    unnamed x268 -> x140, local copies, waits for them, and re-layouts: 145 us -> 33.2 us
    all_gather x2 -> x4, waiting for transfers between devices: 0.01 us -> 66 us  [the longest x1 61 us: plane_plan(): lax.all_gather(normed_in.astype(BF), everywhere, axis=0, tiled=True)]
    convert_element_type x9 -> x0, local copies, waits for them, and re-layouts: 58.3 us -> none  [the longest x2 39.7 us: plane_plan(): gate_up_grad = gate_up_pair.reshape(2, 4, shard, 2, share).transpose(2, 3...]
    dot_general x4 -> x2, matrix products: 68.6 us -> 12.6 us  [dot_cols(): lax.dot_general(left, right, (((0,), (0,)), ((), ())), preferred_element_...]
    ppermute x107 -> x61, starting transfers between devices: 109 us -> 56.2 us  [the longest x49 38.6 us: swap(): lax.ppermute(value, ('z', 'core', 'fsdp'), [(i, i ^ mask) for i in range(...]
    dynamic_slice x17 -> x5, local copies, waits for them, and re-layouts: 61.1 us -> 9.09 us  [the longest x1 3.44 us: plane_plan(): lax.dynamic_index_in_dim(head_grad, 1 - core, 1, keepdims=False)]
  transfers between devices with their start and end apart: 110 -> 73, of which waited for: 40 -> 33; matrix products, arithmetic and copies ran while one was open for 47% -> 12% of each run, Pallas kernels for 4% -> 31%
where the time goes in v2:
time: 794 us; the launch traced here: 782 us
  waiting for transfers between devices  283 us (36%)
  Pallas kernels  247 us (31%)
  starting transfers between devices  88.3 us (11%)
  local copies, waits for them, and re-layouts  59.6 us (8%)
  other arithmetic  41.1 us (5%)
  matrix products  32.2 us (4%)
  blocking collectives  15 us (2%)
  between operations  14.9 us (2%)
    ppermute x49, waiting for transfers between devices, swap(): lax.ppermute(value, ('z', 'core', 'fsdp'), [(i, i ^ mask) for i in range(...  156 us
    pallas_call x3, Pallas kernels, hidden_layer(): pl.pallas_call(functools.partial(hidden_kernel, steps=steps, own=own), in...  84.4 us
    all_gather x1, waiting for transfers between devices, plane_plan(): lax.all_gather(normed_in.astype(BF), everywhere, axis=0, tiled=True)  61 us
    pallas_call x3, Pallas kernels, weight_grad(): pl.pallas_call(weight_grad_kernel, grid=(features // step,), in_specs=[pl...  58 us
    all_to_all x7, waiting for transfers between devices, exchange(): return lax.all_to_all(value, axis, split_axis=0, concat_axis=0, tiled=True)  44.4 us
    ppermute x49, starting transfers between devices, swap(): lax.ppermute(value, ('z', 'core', 'fsdp'), [(i, i ^ mask) for i in range(...  38.6 us
    unnamed x140, local copies, waits for them, and re-layouts  33.2 us
    all_to_all x7, starting transfers between devices, exchange(): return lax.all_to_all(value, axis, split_axis=0, concat_axis=0, tiled=True)  31.5 us
  transfers between devices with their start and end apart: 73, of which 33 were waited for; matrix products, arithmetic and copies ran while one was open for 12% of the time, Pallas kernels for 31%

profile of v2, /device:TPU:0, one launch (start us, length us, event | category | flops | bytes accessed | tf_op | source)
XLA Modules:
  0.0 781.7 jit_solution(3334421960959474651)
XLA Ops:
  32.1 17.9 %collective-permute-done.1 = bf16[128,2048]{1,0:T(8,128)(2,1)S(1)} collective-permute-done((bf16[128,2048]{1,0:T(8,128)(2,1)}, bf16[128,2048]{1,0:T(8,128)(2,1)S(1)}, u32[]{:S(2)}, u32[]{:S(2)}) %collective-permute-start.1) | collective-permute-done | bytes 524320 | tf_op jit(solution)/shard_map/ppermute | solution.py:343
  51.8 27.3 %collective-permute-done.2 = bf16[64,2048]{1,0:T(8,128)(2,1)S(1)} collective-permute-done((bf16[64,2048]{1,0:T(8,128)(2,1)S(1)}, bf16[64,2048]{1,0:T(8,128)(2,1)S(1)}, u32[]{:S(2)}, u32[]{:S(2)}) %collective-permute-start.2) | collective-permute-done | bytes 262176 | tf_op jit(solution)/shard_map/ppermute | solution.py:343
  94.7 61.0 %all-gather.6.cloned.1.call-done = bf16[4096,2048]{1,0:T(8,128)(2,1)} async-done(((bf16[128,2048]{1,0:T(8,128)(2,1)}), bf16[4096,2048]{1,0:T(8,128)(2,1)}) %all-gather.6.cloned.1.call-update) | async-done | bytes 16777232 | tf_op jit(solution)/shard_map/all_gather | solution.py:1141
  164.7 10.4 %convolution_add_fusion = f32[4096,256]{1,0:T(8,128)} fusion(bf16[4096,2048]{1,0:T(8,128)(2,1)} %all-gather.6.cloned.1.call-done, bf16[2048,256]{1,0:T(8,128)(2,1)S(1)} %pad_maximum_fusion.2, f32[256]{0:T(256)S(1)} %pad_maximum_fusion.4), kind=kOutput, calls=%fused_computation | convolution fusion | flops 4296015872 | bytes 22021120 | tf_op jit(solution)/shard_map/dot_general | solution.py:383
  175.1 21.3 %attend.1 = (bf16[2048,128]{1,0:T(8,128)(2,1)S(1)}, bf16[2048,128]{1,0:T(8,128)(2,1)S(1)}, bf16[2048,128]{1,0:T(8,128)(2,1)S(1)}, bf16[2048,128]{1,0:T(8,128)(2,...) custom-call(s32[2]{0:T(128)S(1)} %fusion.29.split_ref, ...), custom_call_target="tpu_custom_call" | custom-call | flops 1000 | bytes 1000 | tf_op jit(solution)/shard_map/attend/pallas_call | solution.py:502
  232.1 22.8 %collective-permute-done.12 = bf16[128,2048]{1,0:T(8,128)(2,1)S(1)} collective-permute-done((bf16[128,2048]{1,0:T(8,128)(2,1)S(1)}, bf16[128,2048]{1,0:T(8,128)(2,1)S(1)}, u32[]{:S(2)}, u32[]{:S(2)}) %collective-permute-start.12) | collective-permute-done | bytes 524320 | tf_op jit(solution)/shard_map/ppermute | solution.py:343
  254.9 9.3 %collective-permute-done.11 = bf16[128,2048]{1,0:T(8,128)(2,1)S(1)} collective-permute-done((bf16[128,2048]{1,0:T(8,128)(2,1)S(1)}, bf16[128,2048]{1,0:T(8,128)(2,1)S(1)}, u32[]{:S(2)}, u32[]{:S(2)}) %collective-permute-start.11) | collective-permute-done | bytes 524320 | tf_op jit(solution)/shard_map/ppermute | solution.py:343
  270.3 11.6 %collective-permute-done.14.refs_1_ = bf16[128,2048]{1,0:T(8,128)(2,1)S(1)} collective-permute-done((bf16[128,2048]{1,0:T(8,128)(2,1)S(1)}, bf16[128,2048]{1,0:T(8,128)(2,1)S(1)}, u32[]{:S(2)}, u32[]{:S(2)}) %collective-permute-start.14) | collective-permute-done | bytes 524320 | tf_op jit(solution)/shard_map/ppermute | solution.py:343
  306.6 30.7 %hidden.3 = (bf16[4096,768]{1,0:T(8,128)(2,1)}, bf16[4096,768]{1,0:T(8,128)(2,1)}, bf16[4096,768]{1,0:T(8,128)(2,1)}, bf16[4096,2048]{1,0:T(8,128)(2,1)}, bf16[4...) custom-call(s32[2]{0:T(128)S(1)} %pad_add_fusion.where_ref, ...), custom_call_target="tpu_custom_call" | custom-call | flops 1000 | bytes 1000 | tf_op jit(solution)/shard_map/hidden/pallas_call | solution.py:941
  357.6 9.7 %collective-permute-done.28 = bf16[128,2048]{1,0:T(8,128)(2,1)} collective-permute-done((bf16[128,2048]{1,0:T(8,128)(2,1)}, bf16[128,2048]{1,0:T(8,128)(2,1)}, u32[]{:S(2)}, u32[]{:S(2)}) %collective-permute-start.28) | collective-permute-done | bytes 524320 | tf_op jit(solution)/shard_map/ppermute | solution.py:343
  391.3 10.1 %collective-permute-done.30.p1 = bf16[128,2048]{1,0:T(8,128)(2,1)S(1)} collective-permute-done((bf16[128,2048]{1,0:T(8,128)(2,1)S(1)}, bf16[128,2048]{1,0:T(8,128)(2,1)S(1)}, u32[]{:S(2)}, u32[]{:S(2)}) %collective-permute-start.30) | collective-permute-done | bytes 524320 | tf_op jit(solution)/shard_map/ppermute | solution.py:343
  427.4 20.9 %all-to-all-done.3 = bf16[8,256,128]{2,1,0:T(8,128)(2,1)} async-done(((bf16[8,256,128]{2,1,0:T(8,128)(2,1)}), bf16[8,256,128]{2,1,0:T(8,128)(2,1)}, u32[]{:S(2)}, u32[]{:S(2)}) %all-to-all-start.3) | async-done | bytes 524320 | tf_op jit(solution)/shard_map/all_to_all | solution.py:355
  453.6 28.1 %attend_back.1 = (bf16[32,2,64,256]{3,2,1,0:T(8,128)(2,1)}, bf16[2048,384]{1,0:T(8,128)(2,1)}) custom-call(s32[2]{0:T(128)S(1)} %fusion.29.split_ref, bf16[2048,128]{1,0:T(8,128)(2,1)S(1)} %copy-done.16, bf16[2048,128]{1,0:T(8,128)(2,1)S(1)} %copy-done.9, bf16[2048,128]{1,0:T(8,128)(2,1)S(1)} %copy-done.18, bf16[128,2048]{1,0:T(8,128)(2,1)S(1)} %bitcast.116, ...), custom_call_target="tpu_custom_call" | custom-call | flops 1000 | bytes 1000 | tf_op jit(solution)/shard_map/attend_back/pallas_call | solution.py:629
  492.9 11.6 %collective-permute-done.36 = bf16[128,2048]{1,0:T(8,128)(2,1)S(1)} collective-permute-done((bf16[128,2048]{1,0:T(8,128)(2,1)S(1)}, bf16[128,2048]{1,0:T(8,128)(2,1)S(1)}, u32[]{:S(2)}, u32[]{:S(2)}) %collective-permute-start.36) | collective-permute-done | bytes 524320 | tf_op jit(solution)/shard_map/ppermute | solution.py:343
  508.8 32.8 %hidden.4 = (bf16[4096,768]{1,0:T(8,128)(2,1)}, bf16[4096,768]{1,0:T(8,128)(2,1)}, bf16[4096,768]{1,0:T(8,128)(2,1)}, bf16[4096,2048]{1,0:T(8,128)(2,1)}) custom-call(s32[2]{0:T(128)S(1)} %pad_add_fusion.where_ref, ...), custom_call_target="tpu_custom_call", output_to_operand_aliasing={{0}: (13, {}), {1}: (14, {}), {2}: (15, {}), {3}: (16, {})} | custom-call | flops 1000 | bytes 1000 | tf_op jit(solution)/shard_map/hidden/pallas_call | solution.py:941
  569.1 15.0 %all_to_all.40 = bf16[4,256,384]{2,1,0:T(8,128)(2,1)} all-to-all(bf16[4,256,384]{2,1,0:T(8,128)(2,1)S(1)} %concatenate.19), channel_id=1, replica_groups=mesh['z'=4,'core'=2,'fsdp'=4] {'fsdp'}, dimensions={0} | all-to-all | bytes 1572864 | tf_op jit(solution)/shard_map/all_to_all | solution.py:355
  600.0 20.9 %hidden.5 = (bf16[4096,768]{1,0:T(8,128)(2,1)}, bf16[4096,768]{1,0:T(8,128)(2,1)}, bf16[4096,768]{1,0:T(8,128)(2,1)}, bf16[4096,2048]{1,0:T(8,128)(2,1)}) custom-call(s32[2]{0:T(128)S(1)} %pad_add_fusion.where_ref, ...), custom_call_target="tpu_custom_call", output_to_operand_aliasing={{0}: (9, {}), {1}: (10, {}), {2}: (11, {}), {3}: (12, {})} | custom-call | flops 1000 | bytes 1000 | tf_op jit(solution)/shard_map/hidden/pallas_call | solution.py:941
  636.2 19.0 %weight_grad.3 = bf16[2048,768]{1,0:T(8,128)(2,1)} custom-call(bf16[4096,2048]{1,0:T(8,128)(2,1)} %all-gather.8.cloned.1.call-done.refs_0_.left_ref, bf16[4096,768]{1,0:T(8,128)(2,1)} %get-tuple-element.215.right_ref), custom_call_target="tpu_custom_call" | custom-call | flops 1000 | bytes 1000 | tf_op jit(solution)/shard_map/weight_grad/pallas_call | solution.py:970
  660.1 19.0 %weight_grad.4 = bf16[2048,768]{1,0:T(8,128)(2,1)} custom-call(bf16[4096,2048]{1,0:T(8,128)(2,1)} %all-gather.8.cloned.1.call-done.refs_0_.left_ref, bf16[4096,768]{1,0:T(8,128)(2,1)} %get-tuple-element.219.right_ref), custom_call_target="tpu_custom_call" | custom-call | flops 1000 | bytes 1000 | tf_op jit(solution)/shard_map/weight_grad/pallas_call | solution.py:970
  679.1 16.0 %all-to-all-done.5.own_ref = bf16[4,512,768]{2,1,0:T(8,128)(2,1)} async-done(((bf16[4,512,768]{2,1,0:T(8,128)(2,1)}), bf16[4,512,768]{2,1,0:T(8,128)(2,1)}, u32[]{:S(2)}, u32[]{:S(2)}) %all-to-all-start.5) | async-done | bytes 3145760 | tf_op jit(solution)/shard_map/all_to_all | solution.py:355
  700.3 20.0 %weight_grad.5.own_ref = bf16[768,2048]{1,0:T(8,128)(2,1)S(1)} custom-call(bf16[4096,768]{1,0:T(8,128)(2,1)} %get-tuple-element.227.left_ref, bf16[4096,2048]{1,0:T(8,128)(2,1)} %get-tuple-element.228.right_ref), custom_call_target="tpu_custom_call" | custom-call | flops 1000 | bytes 1000 | tf_op jit(solution)/shard_map/weight_grad/pallas_call | solution.py:970
  720.4 9.0 %place_columns.2.rest_0_ = f32[512,11264]{1,0:T(8,128)} custom-call(s32[1]{0:T(128)} %bitcast.35.where_ref.core_ref, bf16[4,512,768]{2,1,0:T(8,128)(2,1)} %all-to-all-done.5.own_ref, bf16[4,512,768]{2,1,0:T(8,128)(2,1)} %collective-permute-done.58.other_ref), custom_call_target="tpu_custom_call" | custom-call | flops 1000 | bytes 1000 | tf_op jit(solution)/shard_map/place_columns/pallas_call | solution.py:1005
  745.7 10.6 %place_qkv.1 = f32[512,6144]{1,0:T(8,128)} custom-call(s32[1]{0:T(128)} %bitcast.35.where_ref.core_ref, bf16[4,4,256,384]{3,2,1,0:T(8,128)(2,1)} %bitcast.39.own_ref, bf16[4,4,256,384]{3,2,1,0:T(8,128)(2,1)} %collective-permute-done.57.other_ref), custom_call_target="tpu_custom_call" | custom-call | flops 1000 | bytes 1000 | tf_op jit(solution)/shard_map/place_qkv/pallas_call | solution.py:1074
  756.4 10.0 %place_down.1 = f32[1408,2048]{1,0:T(8,128)} custom-call(s32[1]{0:T(128)} %bitcast.35.where_ref.core_ref, bf16[768,2048]{1,0:T(8,128)(2,1)} %copy-done.1, bf16[768,2048]{1,0:T(8,128)(2,1)} %collective-permute-done.60.other_ref), custom_call_target="tpu_custom_call" | custom-call | flops 1000 | bytes 1000 | tf_op jit(solution)/shard_map/place_down/pallas_call | solution.py:1047
  (368 shorter events, 301.9 us)
Async XLA Ops:
  7.2 148.5 %all-gather.6.cloned.1.call-start = ((), (), s32[]{:S(2)}) async-start(), calls=%async_computation.9 | async-start | bytes 17301504 | tf_op jit(solution)/shard_map/all_gather | solution.py:1141
  23.4 68.7 %all-to-all-start = ((bf16[4,512,768]{2,1,0:T(8,128)(2,1)}), bf16[4,512,768]{2,1,0:T(8,128)(2,1)}, u32[]{:S(2)}, u32[]{:S(2)}) async-start(bf16[4,512,768]{2,1,0:T(8,128)(2,1)} %pick_heads.1), calls=%async_computation | async-start | bytes 6291456 | tf_op jit(solution)/shard_map/all_to_all | solution.py:355
  30.8 48.3 %collective-permute-start.2 = (bf16[64,2048]{1,0:T(8,128)(2,1)S(1)}, bf16[64,2048]{1,0:T(8,128)(2,1)S(1)}, u32[]{:S(2)}, u32[]{:S(2)}) collective-permute-start(bf16[64,2048]{1,0:T(8,128)(2,1)S(1)} %slice.201), channel_id=1, source_target_pairs={{0,2},{1,3},{2,0},{3,1},{4,6},{5,7},{6,4},{7,5},{8,10},{9,11},{10,... | collective-permute-start | bytes 786440 | tf_op jit(solution)/shard_map/ppermute | solution.py:343
  155.7 44.9 %all-to-all-start.1 = ((bf16[4,512,768]{2,1,0:T(8,128)(2,1)}), bf16[4,512,768]{2,1,0:T(8,128)(2,1)}, u32[]{:S(2)}, u32[]{:S(2)}) async-start(bf16[4,512,768]{2,1,0:T(8,128)(2,1)} %get-tuple-element.134), calls=%async_computation.1 | async-start | bytes 6291456 | tf_op jit(solution)/shard_map/all_to_all | solution.py:355
  164.3 36.3 %collective-permute-start.5 = (bf16[256,2048]{1,0:T(8,128)(2,1)S(1)}, bf16[256,2048]{1,0:T(8,128)(2,1)}, u32[]{:S(2)}, u32[]{:S(2)}) collective-permute-start(bf16[256,2048]{1,0:T(8,128)(2,1)S(1)} %get-tuple-element.264), channel_id=1, source_target_pairs={{0,8},{1,9},{2,10},{3,11},{4,12},{5,13},{6,14},{7,15},{8,16},{9,17... | collective-permute-start | bytes 3145736 | tf_op jit(solution)/shard_map/ppermute | solution.py:347
  200.6 65.0 %all-to-all-start.2 = ((bf16[4,512,768]{2,1,0:T(8,128)(2,1)}), bf16[4,512,768]{2,1,0:T(8,128)(2,1)}, u32[]{:S(2)}, u32[]{:S(2)}) async-start(bf16[4,512,768]{2,1,0:T(8,128)(2,1)} %get-tuple-element.147), calls=%async_computation.2 | async-start | bytes 6291456 | tf_op jit(solution)/shard_map/all_to_all | solution.py:355
  205.3 281.4 %all-gather.8.cloned.1.call-start = ((), (), s32[]{:S(2)}) async-start(), calls=%async_computation.10 | async-start | bytes 17301504 | tf_op jit(solution)/shard_map/all_gather | solution.py:1184
  228.1 36.1 %collective-permute-start.11 = (bf16[128,2048]{1,0:T(8,128)(2,1)S(1)}, bf16[128,2048]{1,0:T(8,128)(2,1)S(1)}, u32[]{:S(2)}, u32[]{:S(2)}) collective-permute-start(bf16[128,2048]{1,0:T(8,128)(2,1)S(1)} %get-tuple-element.145), channel_id=1, source_target_pairs={{0,2},{1,3},{2,0},{3,1},{4,6},{5,7},{6,4},{7,5},{8,10},{9,11},{10,... | collective-permute-start | bytes 1572872 | tf_op jit(solution)/shard_map/ppermute | solution.py:343
  228.7 35.6 %collective-permute-start.10 = (bf16[128,2048]{1,0:T(8,128)(2,1)S(1)}, bf16[128,2048]{1,0:T(8,128)(2,1)S(1)}, u32[]{:S(2)}, u32[]{:S(2)}) collective-permute-start(bf16[128,2048]{1,0:T(8,128)(2,1)S(1)} %get-tuple-element.144), channel_id=1, source_target_pairs={{0,1},{1,0},{2,3},{3,2},{4,5},{5,4},{6,7},{7,6},{8,9},{9,8},{10,11... | collective-permute-start | bytes 1572872 | tf_op jit(solution)/shard_map/ppermute | solution.py:343
  228.8 36.8 %collective-permute-start.13 = (bf16[256,2048]{1,0:T(8,128)(2,1)}, bf16[256,2048]{1,0:T(8,128)(2,1)}, u32[]{:S(2)}, u32[]{:S(2)}) collective-permute-start(bf16[256,2048]{1,0:T(8,128)(2,1)} %get-tuple-element.263), channel_id=1, source_target_pairs={{0,8},{1,9},{2,10},{3,11},{4,12},{5,13},{6,14},{7,15},{8,16},{9,17... | collective-permute-start | bytes 3145736 | tf_op jit(solution)/shard_map/ppermute | solution.py:347
  232.1 51.5 %collective-permute-start.23 = (bf16[256,2048]{1,0:T(8,128)(2,1)}, bf16[256,2048]{1,0:T(8,128)(2,1)}, u32[]{:S(2)}, u32[]{:S(2)}) collective-permute-start(bf16[256,2048]{1,0:T(8,128)(2,1)} %collective-permute-done.5.refs_1_), channel_id=1, source_target_pairs={{0,8},{1,9},{2,10},{3,11},{4,12},{5,13},{6,14},{7,15},{8,16},{9,17... | collective-permute-start | bytes 3145736 | tf_op jit(solution)/shard_map/ppermute | solution.py:347
  296.8 40.5 %collective-permute-start.24 = (bf16[256,2048]{1,0:T(8,128)(2,1)}, bf16[256,2048]{1,0:T(8,128)(2,1)S(1)}, u32[]{:S(2)}, u32[]{:S(2)}) collective-permute-start(bf16[256,2048]{1,0:T(8,128)(2,1)} %collective-permute-done.13.refs_2_), channel_id=1, source_target_pairs={{0,8},{1,9},{2,10},{3,11},{4,12},{5,13},{6,14},{7,15},{8,16},{9,17... | collective-permute-start | bytes 3145736 | tf_op jit(solution)/shard_map/ppermute | solution.py:347
  349.0 38.2 %collective-permute-start.29 = (bf16[256,2048]{1,0:T(8,128)(2,1)}, bf16[256,2048]{1,0:T(8,128)(2,1)S(1)}, u32[]{:S(2)}, u32[]{:S(2)}) collective-permute-start(bf16[256,2048]{1,0:T(8,128)(2,1)} %collective-permute-done.23.refs_5_), channel_id=1, source_target_pairs={{0,8},{1,9},{2,10},{3,11},{4,12},{5,13},{6,14},{7,15},{8,16},{9,17... | collective-permute-start | bytes 3145736 | tf_op jit(solution)/shard_map/ppermute | solution.py:347
  349.7 59.6 %collective-permute-start.34 = (bf16[256,2048]{1,0:T(8,128)(2,1)}, bf16[256,2048]{1,0:T(8,128)(2,1)}, u32[]{:S(2)}, u32[]{:S(2)}) collective-permute-start(bf16[256,2048]{1,0:T(8,128)(2,1)} %copy-done.55), channel_id=1, source_target_pairs={{0,8},{1,9},{2,10},{3,11},{4,12},{5,13},{6,14},{7,15},{8,16},{9,17... | collective-permute-start | bytes 3145736 | tf_op jit(solution)/shard_map/ppermute | solution.py:347
  367.3 50.4 %collective-permute-start.35 = (bf16[4,128,2048]{2,1,0:T(8,128)(2,1)}, bf16[4,128,2048]{2,1,0:T(8,128)(2,1)}, u32[]{:S(2)}, u32[]{:S(2)}) collective-permute-start(bf16[4,128,2048]{2,1,0:T(8,128)(2,1)} %bitcast.23), channel_id=1, source_target_pairs={{0,4},{1,5},{2,6},{3,7},{4,0},{5,1},{6,2},{7,3},{8,12},{9,13},{10,... | collective-permute-start | bytes 6291464 | tf_op jit(solution)/shard_map/ppermute | solution.py:343
  421.5 70.9 %collective-permute-start.38 = (bf16[128,2048]{1,0:T(8,128)(2,1)}, bf16[128,2048]{1,0:T(8,128)(2,1)}, u32[]{:S(2)}, u32[]{:S(2)}) collective-permute-start(bf16[128,2048]{1,0:T(8,128)(2,1)} %get-tuple-element.255), channel_id=1, source_target_pairs={{0,3},{1,2},{2,1},{3,0},{4,7},{5,6},{6,5},{7,4},{8,11},{9,10},{10,... | collective-permute-start | bytes 1572872 | tf_op jit(solution)/shard_map/ppermute | solution.py:343
  423.9 68.5 %collective-permute-start.37 = (bf16[128,2048]{1,0:T(8,128)(2,1)}, bf16[128,2048]{1,0:T(8,128)(2,1)}, u32[]{:S(2)}, u32[]{:S(2)}) collective-permute-start(bf16[128,2048]{1,0:T(8,128)(2,1)} %get-tuple-element.256), channel_id=1, source_target_pairs={{0,2},{1,3},{2,0},{3,1},{4,6},{5,7},{6,4},{7,5},{8,10},{9,11},{10,... | collective-permute-start | bytes 1572872 | tf_op jit(solution)/shard_map/ppermute | solution.py:343
  486.7 63.5 %all-to-all-start.4 = ((bf16[4,512,384]{2,1,0:T(8,128)(2,1)}), bf16[4,512,384]{2,1,0:T(8,128)(2,1)S(1)}, u32[]{:S(2)}, u32[]{:S(2)}) async-start(bf16[4,512,384]{2,1,0:T(8,128)(2,1)} %bitcast.126), calls=%async_computation.4 | async-start | bytes 3145728 | tf_op jit(solution)/shard_map/all_to_all | solution.py:355
  490.3 133.1 %reduce-scatter.2.cloned.1.call-start = ((), (), s32[]{:S(2)}) async-start(), calls=%async_computation.11 | async-start | bytes 2359296 | tf_op jit(solution)/shard_map/reduce_scatter | solution.py:1261
  554.4 140.7 %all-gather.12.cloned.1.call-start = ((), (), s32[]{:S(2)}) async-start(), calls=%async_computation.13 | async-start | bytes 3932160 | tf_op jit(solution)/shard_map/all_gather | solution.py:1258
  584.2 110.9 %all-gather.10.cloned.1.call-start = ((), (), s32[]{:S(2)}) async-start(), calls=%async_computation.12 | async-start | bytes 2359296 | tf_op jit(solution)/shard_map/all_gather | solution.py:1262
  655.2 39.9 %all-to-all-start.5 = ((bf16[4,512,768]{2,1,0:T(8,128)(2,1)}), bf16[4,512,768]{2,1,0:T(8,128)(2,1)}, u32[]{:S(2)}, u32[]{:S(2)}) async-start(bf16[4,512,768]{2,1,0:T(8,128)(2,1)} %bitcast.36), calls=%async_computation.5 | async-start | bytes 6291456 | tf_op jit(solution)/shard_map/all_to_all | solution.py:355
  695.1 41.7 %all-to-all-start.7 = ((bf16[4,512,768]{2,1,0:T(8,128)(2,1)}), bf16[4,512,768]{2,1,0:T(8,128)(2,1)}, u32[]{:S(2)}, u32[]{:S(2)}) async-start(bf16[4,512,768]{2,1,0:T(8,128)(2,1)} %bitcast.40), calls=%async_computation.8 | async-start | bytes 6291456 | tf_op jit(solution)/shard_map/all_to_all | solution.py:355
  699.8 46.0 %collective-permute-start.57 = (bf16[4,4,256,384]{3,2,1,0:T(8,128)(2,1)}, bf16[4,4,256,384]{3,2,1,0:T(8,128)(2,1)}, u32[]{:S(2)}, u32[]{:S(2)}) collective-permute-start(bf16[4,4,256,384]{3,2,1,0:T(8,128)(2,1)} %bitcast.39.own_ref), channel_id=1, source_target_pairs={{0,4},{1,5},{2,6},{3,7},{4,0},{5,1},{6,2},{7,3},{8,12},{9,13},{10,... | collective-permute-start | bytes 9437192 | tf_op jit(solution)/shard_map/ppermute | solution.py:343
  (115 other events, 1240.9 us)
Sparse Core Ops, SparseCore 0:
  12.3 143.3 all-gather.5
  296.9 189.7 all-gather.7
  554.5 35.9 reduce-scatter.1
  591.9 66.7 all-gather.11
  660.2 27.7 all-gather.9

commit v3 on v2

--- a/solution.py
+++ b/solution.py
@@ -482,7 +482,9 @@
             outs.append(acc / total)
             logs.append(top + jnp.log(total))
         o_ref[rows] = (outs[0] + outs[1]).astype(BF)
-        log_ref[rows] = jnp.where(low_q, logs[0], logs[1])
+        turned = jnp.where(low_q, logs[0], logs[1]).T
+        log_ref[0:1, rows] = turned[0:1]
+        log_ref[1:2, rows] = turned[HD : HD + 1]
         step = lax.rem(qb - where_ref[0] + 4, 4)
         core = where_ref[1] // 4
         half = BLOCK // 2
@@ -501,7 +503,7 @@
     pairs = 2 * row_len * row_len // 2
     return pl.pallas_call(
         attend_kernel,
-        out_shape=(packed, packed, packed, packed, jax.ShapeDtypeStruct((row_len, 2 * HD), F32))
+        out_shape=(packed, packed, packed, packed, jax.ShapeDtypeStruct((2, row_len), F32))
         + (jax.ShapeDtypeStruct((4, row_len // 8, 2 * HD), BF),) * 2,
         in_specs=[smem, smem, vmem, vmem, vmem, vmem],
         out_specs=(vmem,) * 7,
@@ -513,10 +515,21 @@
 
 
 def attend_back_kernel(
-    split_ref, q_ref, k_ref, v_ref, kt_ref, o_ref, do_ref, log_ref,
+    split_ref, q_hbm, k_hbm, v_hbm, o_hbm, do_hbm, log_ref,
     cos_ref, ahead_ref, behind_ref,
     dmix_ref, dpos_ref, kz, vz, qz, dz, ktz, delta, dq_t, dk, dv,
+    q_ref, k_ref, v_ref, o_ref, do_ref, sem,
 ):
+    loads = [
+        pltpu.make_async_copy(source, target, sem.at[n])
+        for n, (source, target) in enumerate(
+            ((k_hbm, k_ref), (v_hbm, v_ref), (q_hbm, q_ref), (do_hbm, do_ref), (o_hbm, o_ref))
+        )
+    ]
+    for copy in loads:
+        copy.start()
+    for copy in loads:
+        copy.wait()
     row_len = q_ref.shape[0]
     local_len = dmix_ref.shape[2]
     low = lax.broadcasted_iota(jnp.int32, (BLOCK, 2 * HD), 1) < HD
@@ -531,7 +544,7 @@
             value = ref[rows].astype(F32)
             out[0, rows] = jnp.where(low, value, zero).astype(BF)
             out[1, rows] = jnp.where(low, zero, value).astype(BF)
-        value = kt_ref[:, rows].astype(F32)
+        value = k_ref[rows].astype(F32).T
         ktz[0, :, rows] = jnp.where(low_t, value, 0.0).astype(BF)
         ktz[1, :, rows] = jnp.where(low_t, 0.0, value).astype(BF)
         product = do_ref[rows].astype(F32) * o_ref[rows].astype(F32)
@@ -619,7 +632,7 @@
     lax.fori_loop(0, row_len // (2 * HD), finish, 0)
 
 
-def attend_back(split, q, k, v, k_t, out, d_out, logs, tables, local_len):
+def attend_back(split, q, k, v, out, d_out, logs, tables, local_len):
     row_len = q.shape[0]
     smem = pl.BlockSpec(memory_space=pltpu.SMEM)
     vmem = pl.BlockSpec(memory_space=pltpu.VMEM)
@@ -632,7 +645,7 @@
             jax.ShapeDtypeStruct((row_len // local_len, 2, local_len, 4 * HD), BF),
         )
         + (jax.ShapeDtypeStruct((row_len, 6 * HD), BF),),
-        in_specs=[smem] + [vmem] * 10,
+        in_specs=[smem] + [pl.BlockSpec(memory_space=pltpu.HBM)] * 5 + [vmem] * 4,
         out_specs=(vmem,) * 2,
         scratch_shapes=[
             masked, masked, masked, masked,
@@ -640,11 +653,13 @@
             pltpu.VMEM((2, 8, row_len), F32),
             pltpu.VMEM((2 * HD, row_len), F32),
             whole, whole,
-        ],
+        ]
+        + [pltpu.VMEM((row_len, 2 * HD), BF)] * 5
+        + [pltpu.SemaphoreType.DMA((5,))],
         compiler_params=pltpu.CompilerParams(vmem_limit_bytes=48 * 2**20),
         cost_estimate=SMALL,
         name="attend_back",
-    )(split, q, k, v, k_t, out, d_out, logs, *tables)
+    )(split, q, k, v, out, d_out, logs, *tables)
 
 
 def pick_heads_kernel(where_ref, q_ref, k_ref, v_ref, out_ref):
@@ -937,7 +952,7 @@
     dma = pltpu.SemaphoreType.DMA
     count = len(mids) + len(outs)
     kept = [] if own else list(before)
-    hbm = pl.BlockSpec(memory_space=pl.ANY)
+    hbm = pl.BlockSpec(memory_space=pltpu.HBM)
     found = pl.pallas_call(
         functools.partial(hidden_kernel, steps=steps, own=own),
         in_specs=[pl.BlockSpec(memory_space=pltpu.SMEM)] + [hbm] * (count + 3 + len(kept)),
@@ -1070,7 +1085,7 @@
 def place_qkv(where, own, other):
     _, _, cut, wide = own.shape
     parts = wide // (2 * HD)
-    piece = pl.BlockSpec((4, 1, cut, 2 * HD), lambda part, chip, where: (0, chip, 0, part))
+    piece = pl.BlockSpec((4, 1, cut, 2 * HD), lambda part, chip, where: (0, chip ^ where[1], 0, part))
     return pl.pallas_call(
         place_qkv_kernel,
         grid_spec=pltpu.PrefetchScalarGridSpec(
@@ -1117,11 +1132,15 @@
     split = jnp.sum((segments == 0).astype(jnp.int32), axis=1)
     where = jnp.stack([plane, own]).astype(jnp.int32)
 
-    head_all = exchange(pick_heads(where, qkv_weight)).reshape(features, 12 * HD)
-    value = lax.dynamic_slice_in_dim(head_all, 8 * HD + plane * HD, HD, 1)
-    head_weight = jnp.concatenate(
-        [lax.dynamic_slice_in_dim(head_all, plane * 2 * HD, 2 * HD, 1), value, value], axis=1
-    )
+    def head_columns(chip):
+        parts = [
+            lax.dynamic_slice_in_dim(qkv_weight, (chip * 8 + seq) * HD + part * features, HD, 1)
+            for part in (0, 1, 2)
+        ]
+        return jnp.concatenate(parts + parts[2:], axis=1)
+
+    head_weight = exchange(jnp.stack([head_columns(chip) for chip in range(4)])).reshape(features, 4 * HD)
+    picked = pick_heads(where, qkv_weight)
     head_first = (rank * 8 + seq) * HD
     bias_parts = [
         lax.dynamic_slice_in_dim(qkv_bias, head_first + part * features, HD, 0) for part in (0, 1, 2)
@@ -1142,8 +1161,8 @@
     d_out = cotangent.reshape(tokens, features)
     out_near = jnp.concatenate(gather_near(d_out), axis=0)
     out_far = swap(out_near, 4)
-    in_all, out_near, out_far, gate_weight, up_weight, head_weight, head_all, *tables = tie(
-        in_all, out_near, out_far, gate_weight, up_weight, head_weight, head_all, *tables
+    in_all, out_near, out_far, gate_weight, up_weight, head_weight, picked, *tables = tie(
+        in_all, out_near, out_far, gate_weight, up_weight, head_weight, picked, *tables
     )
     lows, highs = [out_near[: 2 * tokens]], [out_near[2 * tokens :]]
 
@@ -1194,8 +1213,6 @@
     d_middle = d_out.astype(F32) + d_middle_part
 
     d_pieces = gather_near(d_middle.astype(BF))
-    d_pieces[4], high = tie(d_pieces[4], shift(highs[2], 1))
-    highs.append(high)
     d_branch, d_heads = small_call(
         d_att_kernel,
         "d_att",
@@ -1208,15 +1225,25 @@
         out_weight,
     )
     d_heads = exchange(d_heads, ("z", "core")).reshape(row_len, 2 * HD)
-    log_rows = jnp.stack([logs[:, 0], logs[:, HD]])
-    d_mixed, d_packed = attend_back(
-        split, q, k, v, k.T, out_heads, d_heads, log_rows, tables, local_len
-    )
-    d_packed, d_mixed, mid_all = tie(d_packed, d_mixed, mid_all)
+    d_heads, high_own = tie(d_heads, highs[2])
+    d_packed, d_mixed, mid_all, high = tie(
+        *attend_back(split, q, k, v, out_heads, d_heads, logs, tables, local_len)[::-1],
+        mid_all,
+        shift(high_own, 1),
+    )
+    highs.append(high)
 
     arrived = exchange(d_packed.reshape(4, row_len // 4, 6 * HD), "z")
     d_mixed = d_mixed.reshape(row_len * row_count, 4 * HD)
     head_grad = dot_cols(in_all, d_mixed)[:, : 3 * HD].astype(BF)
+    cut = shard // 2
+    head_grad = head_grad.reshape(4, 2, cut, 3 * HD)
+    mine = lax.dynamic_index_in_dim(head_grad, core, 1, keepdims=False)
+    theirs = swap(lax.dynamic_index_in_dim(head_grad, 1 - core, 1, keepdims=False), 4)
+    first, second = jnp.where(core == 0, mine, theirs), jnp.where(core == 0, theirs, mine)
+    pairs = jnp.concatenate(
+        [half[:, :, p * HD : (p + 1) * HD] for p in range(3) for half in (first, second)], axis=2
+    )
     down = lax.dynamic_slice_in_dim(down_weight, hidden_first, width, 0)
     result_sum = sum_plane(
         dot(act_near.reshape(4 * tokens, width), down).reshape(4, tokens, features),
@@ -1230,10 +1257,22 @@
         return hidden_layer(where, [mid_all], outs, hidden_weights, total, steps, before)[0]
 
     hidden_all = rest((1, 2), hidden_all)
-    arrived, result_sum, head_grad, att, d_branch, *hidden_all = tie(
-        arrived, result_sum, head_grad, att, d_branch, *hidden_all
+    arrived, result_sum, pairs, att, d_branch, picked, *hidden_all = tie(
+        arrived, result_sum, pairs, att, d_branch, picked, *hidden_all
     )
     result = middle + result_sum
+
+    pairs = [pick(pairs, rank ^ m) for m in range(4)]
+    pairs = [pairs[0]] + [swap(pairs[m], m) for m in (1, 2, 3)]
+    head_all = exchange(picked).reshape(features, 12 * HD)
+    out_part = dot_cols(att, d_branch).astype(BF)
+    out_part = lax.psum_scatter(out_part, ("z", "core"), scatter_dimension=0, tiled=True)
+    act_all, d_gate_all, d_up_all, out_all = rest((3,), hidden_all)
+    head_all, d_gate_grad, d_up_all, act_all, arrived, out_part, *pairs = tie(
+        head_all, weight_grad(mid_all, d_gate_all), d_up_all, act_all, arrived, out_part, *pairs
+    )
+
+    by_chip = (4, shard, width)
     near, far = small_call(
         d_in_kernel,
         "d_in",
@@ -1247,29 +1286,27 @@
         ],
         limit=48,
     )
-    cut = shard // 2
-    head_grad = head_grad.reshape(4, 2, cut, 3 * HD)
-    mine = lax.dynamic_index_in_dim(head_grad, core, 1, keepdims=False)
-    theirs = swap(lax.dynamic_index_in_dim(head_grad, 1 - core, 1, keepdims=False), 4)
-    first, second = jnp.where(core == 0, mine, theirs), jnp.where(core == 0, theirs, mine)
-    pairs = jnp.concatenate(
-        [half[:, :, p * HD : (p + 1) * HD] for p in range(3) for half in (first, second)], axis=2
-    )
-    heads = lax.all_gather(exchange(pairs), "z", axis=0)
-
-    out_part = dot_cols(att, d_branch).astype(BF)
-    out_part = lax.psum_scatter(out_part, ("z", "core"), scatter_dimension=0, tiled=True)
+    heads = lax.all_gather(jnp.stack(pairs), "z", axis=0)
+    gate_parts, d_up_grad, near, far, act_all = tie(
+        exchange(d_gate_grad.reshape(by_chip)),
+        weight_grad(mid_all, d_up_all),
+        near,
+        swap(far, 4),
+        act_all,
+    )
+    d_norm_in, down_own, d_up_grad = tie(
+        sum_quad([near[m].astype(F32) + far[m].astype(F32) for m in range(4)]),
+        weight_grad(act_all, out_all),
+        d_up_grad,
+    )
+
+    core_index = core.reshape(1).astype(jnp.int32)
+    up_parts = exchange(d_up_grad.reshape(by_chip))
     out_rows = lax.all_gather(out_part, ("z", "core"), axis=0, tiled=True)
-
-    far, near, *hidden_all = tie(swap(far, 4), near, *hidden_all)
-    hidden_all = rest((3,), hidden_all)
-    act_all, d_gate_all, d_up_all, out_all = hidden_all
-    d_norm_in, d_gate_all = tie(
-        sum_quad([near[m].astype(F32) + far[m].astype(F32) for m in range(4)]), d_gate_all
-    )
+    gate_up_grad = place_columns(core_index, gate_parts, swap(gate_parts, 4), None, chip_width, 0)
+    down_grad = place_down(core_index, down_own, swap(down_own, 4), chip_width)
     d_flat_part, d_gain_one, d_bias_one = norm1_back(d_norm_in)
     d_inputs = d_middle + d_flat_part
-
     bias_sum = jnp.sum(d_mixed.astype(F32), axis=0)
     bias_own = jnp.zeros((3 * features,), F32)
     for part in range(3):
@@ -1278,27 +1315,12 @@
         )
     sums = jnp.concatenate([d_gain_one, d_bias_one, bias_own, d_gain_two, d_bias_two])
     sums = sums + swap(sums, 4)
+    sums = sums + sum(shift(sums, n) for n in (1, 2, 3))
+    qkv_grad = place_qkv(jnp.stack([core, rank]).astype(jnp.int32), heads, swap(heads, 4))
+    up_parts, sums, gate_up_grad, down_grad, qkv_grad = tie(
+        up_parts, sums, gate_up_grad, down_grad, qkv_grad
+    )
     sums = sums + sum(swap(sums, m) for m in (1, 2, 3))
-
-    d_gate_grad, sums, d_up_all = tie(
-        weight_grad(mid_all, d_gate_all), sums + sum(shift(sums, n) for n in (1, 2, 3)), d_up_all
-    )
-    by_chip = (4, shard, width)
-    gate_parts, d_up_grad, act_all, out_rows, heads = tie(
-        exchange(d_gate_grad.reshape(by_chip)),
-        weight_grad(mid_all, d_up_all),
-        act_all,
-        out_rows,
-        heads,
-    )
-    core_index = core.reshape(1).astype(jnp.int32)
-    up_parts, down_own, gate_up_grad = tie(
-        exchange(d_up_grad.reshape(by_chip)),
-        weight_grad(act_all, out_all),
-        place_columns(core_index, gate_parts, swap(gate_parts, 4), None, chip_width, 0),
-    )
-    down_grad = place_down(core_index, down_own, swap(down_own, 4), chip_width)
-    qkv_grad = place_qkv(core_index, heads, swap(heads, 4))
     out_grad = out_rows.astype(F32)
     gate_up_grad = place_columns(
         core_index, up_parts, swap(up_parts, 4), gate_up_grad, chip_width, 1

time: 794 us -> 779 us (0.981)
  waiting for transfers between devices: 283 us -> 265 us
  blocking collectives: 15 us -> 0 us
  other arithmetic: 41.1 us -> 51.4 us
    ppermute x49 -> x52, waiting for transfers between devices: 156 us -> 129 us  [swap(): lax.ppermute(value, ('z', 'core', 'fsdp'), [(i, i ^ mask) for i in range(...]
    all_to_all x1 -> x0, blocking collectives: 15 us -> none  [exchange(): return lax.all_to_all(value, axis, split_axis=0, concat_axis=0, tiled=True)]
    all_gather x1, waiting for transfers between devices: 61 us -> 70.8 us  [plane_plan(): lax.all_gather(normed_in.astype(BF), everywhere, axis=0, tiled=True)]
    ppermute x12, waiting for transfers between devices: 17.3 us -> 26.3 us  [shift(): lax.ppermute(value, ('z', 'core', 'fsdp'), [(i, (i + 8 * steps) % 32) for...]
    unnamed x140 -> x130, local copies, waits for them, and re-layouts: 33.2 us -> 39.4 us
    all_to_all x7 -> x8, starting transfers between devices: 31.5 us -> 36.9 us  [exchange(): return lax.all_to_all(value, axis, split_axis=0, concat_axis=0, tiled=True)]
    all_to_all x7 -> x8, waiting for transfers between devices: 44.4 us -> 39.5 us  [exchange(): return lax.all_to_all(value, axis, split_axis=0, concat_axis=0, tiled=True)]
    ppermute x49 -> x52, starting transfers between devices: 38.6 us -> 41 us  [swap(): lax.ppermute(value, ('z', 'core', 'fsdp'), [(i, i ^ mask) for i in range(...]
  transfers between devices with their start and end apart: 73 -> 77, of which waited for: 33 -> 32; matrix products, arithmetic and copies ran while one was open for 12% -> 13% of each run, Pallas kernels for 31% -> 31%
where the time goes in v3:
time: 779 us; the launch traced here: 769 us
  waiting for transfers between devices  265 us (34%)
  Pallas kernels  245 us (31%)
  starting transfers between devices  94.8 us (12%)
  local copies, waits for them, and re-layouts  58.8 us (8%)
  other arithmetic  51.4 us (7%)
  matrix products  38.8 us (5%)
  between operations  15.1 us (2%)
    ppermute x52, waiting for transfers between devices, swap(): lax.ppermute(value, ('z', 'core', 'fsdp'), [(i, i ^ mask) for i in range(...  129 us
    pallas_call x3, Pallas kernels, hidden_layer(): pl.pallas_call(functools.partial(hidden_kernel, steps=steps, own=own), in...  84.4 us
    all_gather x1, waiting for transfers between devices, plane_plan(): lax.all_gather(normed_in.astype(BF), everywhere, axis=0, tiled=True)  70.8 us
    pallas_call x3, Pallas kernels, weight_grad(): pl.pallas_call(weight_grad_kernel, grid=(features // step,), in_specs=[pl...  57.5 us
    ppermute x52, starting transfers between devices, swap(): lax.ppermute(value, ('z', 'core', 'fsdp'), [(i, i ^ mask) for i in range(...  41 us
    all_to_all x8, waiting for transfers between devices, exchange(): return lax.all_to_all(value, axis, split_axis=0, concat_axis=0, tiled=True)  39.5 us
    unnamed x130, local copies, waits for them, and re-layouts  39.4 us
    all_to_all x8, starting transfers between devices, exchange(): return lax.all_to_all(value, axis, split_axis=0, concat_axis=0, tiled=True)  36.9 us
  transfers between devices with their start and end apart: 77, of which 32 were waited for; matrix products, arithmetic and copies ran while one was open for 13% of the time, Pallas kernels for 31%

profile of v3, /device:TPU:0, one launch (start us, length us, event | category | flops | bytes accessed | tf_op | source)
XLA Modules:
  0.0 769.1 jit_solution(5800080735731648981)
XLA Ops:
  20.0 10.2 %collective-permute-done = bf16[128,2048]{1,0:T(8,128)(2,1)S(1)} collective-permute-done((bf16[128,2048]{1,0:T(8,128)(2,1)}, bf16[128,2048]{1,0:T(8,128)(2,1)S(1)}, u32[]{:S(2)}, u32[]{:S(2)}) %collective-permute-start) | collective-permute-done | bytes 524320 | tf_op jit(solution)/shard_map/ppermute | solution.py:343
  63.3 9.1 %all-to-all-done = bf16[4,512,256]{2,1,0:T(8,128)(2,1)} async-done(((bf16[4,512,256]{2,1,0:T(8,128)(2,1)}), bf16[4,512,256]{2,1,0:T(8,128)(2,1)}, u32[]{:S(2)}, u32[]{:S(2)}) %all-to-all-start) | async-done | bytes 1048608 | tf_op jit(solution)/shard_map/all_to_all | solution.py:355
  72.4 70.8 %all-gather.6.cloned.1.call-done = bf16[4096,2048]{1,0:T(8,128)(2,1)} async-done(((bf16[128,2048]{1,0:T(8,128)(2,1)}), bf16[4096,2048]{1,0:T(8,128)(2,1)}) %all-gather.6.cloned.1.call-update) | async-done | bytes 16777232 | tf_op jit(solution)/shard_map/all_gather | solution.py:1160
  152.6 12.6 %convolution_add_fusion = f32[4096,256]{1,0:T(8,128)} fusion(bf16[4096,2048]{1,0:T(8,128)(2,1)} %all-gather.6.cloned.1.call-done, bf16[2048,256]{1,0:T(8,128)(2,1)} %bitcast.16, f32[256]{0:T(256)S(1)} %pad_maximum_fusion.4), kind=kOutput, calls=%fused_computation | convolution fusion | flops 4296015872 | bytes 22021120 | tf_op jit(solution)/shard_map/dot_general | solution.py:383
  165.1 21.3 %attend.1 = (bf16[2048,128]{1,0:T(8,128)(2,1)S(1)}, bf16[2048,128]{1,0:T(8,128)(2,1)S(1)}, bf16[2048,128]{1,0:T(8,128)(2,1)S(1)}, bf16[2048,128]{1,0:T(8,128)(2,...) custom-call(s32[2]{0:T(128)S(1)} %fusion.29.split_ref, ...), custom_call_target="tpu_custom_call" | custom-call | flops 1000 | bytes 1000 | tf_op jit(solution)/shard_map/attend/pallas_call | solution.py:504
  221.6 23.0 %collective-permute-done.12 = bf16[128,2048]{1,0:T(8,128)(2,1)S(1)} collective-permute-done((bf16[128,2048]{1,0:T(8,128)(2,1)S(1)}, bf16[128,2048]{1,0:T(8,128)(2,1)S(1)}, u32[]{:S(2)}, u32[]{:S(2)}) %collective-permute-start.12) | collective-permute-done | bytes 524320 | tf_op jit(solution)/shard_map/ppermute | solution.py:343
  244.6 9.3 %collective-permute-done.11 = bf16[128,2048]{1,0:T(8,128)(2,1)S(1)} collective-permute-done((bf16[128,2048]{1,0:T(8,128)(2,1)S(1)}, bf16[128,2048]{1,0:T(8,128)(2,1)S(1)}, u32[]{:S(2)}, u32[]{:S(2)}) %collective-permute-start.11) | collective-permute-done | bytes 524320 | tf_op jit(solution)/shard_map/ppermute | solution.py:343
  260.8 11.8 %collective-permute-done.14.refs_1_ = bf16[128,2048]{1,0:T(8,128)(2,1)S(1)} collective-permute-done((bf16[128,2048]{1,0:T(8,128)(2,1)}, bf16[128,2048]{1,0:T(8,128)(2,1)S(1)}, u32[]{:S(2)}, u32[]{:S(2)}) %collective-permute-start.14) | collective-permute-done | bytes 524320 | tf_op jit(solution)/shard_map/ppermute | solution.py:343
  298.5 30.7 %hidden.3 = (bf16[4096,768]{1,0:T(8,128)(2,1)}, bf16[4096,768]{1,0:T(8,128)(2,1)}, bf16[4096,768]{1,0:T(8,128)(2,1)}, bf16[4096,2048]{1,0:T(8,128)(2,1)}, bf16[4...) custom-call(s32[2]{0:T(128)S(1)} %pad_add_fusion.where_ref, ...), custom_call_target="tpu_custom_call" | custom-call | flops 1000 | bytes 1000 | tf_op jit(solution)/shard_map/hidden/pallas_call | solution.py:956
  349.0 8.9 %collective-permute-done.28 = bf16[128,2048]{1,0:T(8,128)(2,1)} collective-permute-done((bf16[128,2048]{1,0:T(8,128)(2,1)}, bf16[128,2048]{1,0:T(8,128)(2,1)}, u32[]{:S(2)}, u32[]{:S(2)}) %collective-permute-start.28) | collective-permute-done | bytes 524320 | tf_op jit(solution)/shard_map/ppermute | solution.py:343
  357.9 8.8 %collective-permute-done.27 = bf16[128,2048]{1,0:T(8,128)(2,1)} collective-permute-done((bf16[128,2048]{1,0:T(8,128)(2,1)}, bf16[128,2048]{1,0:T(8,128)(2,1)}, u32[]{:S(2)}, u32[]{:S(2)}) %collective-permute-start.27) | collective-permute-done | bytes 524320 | tf_op jit(solution)/shard_map/ppermute | solution.py:343
  381.5 22.2 %collective-permute-done.30.p1 = bf16[128,2048]{1,0:T(8,128)(2,1)S(1)} collective-permute-done((bf16[128,2048]{1,0:T(8,128)(2,1)S(1)}, bf16[128,2048]{1,0:T(8,128)(2,1)S(1)}, u32[]{:S(2)}, u32[]{:S(2)}) %collective-permute-start.30) | collective-permute-done | bytes 524320 | tf_op jit(solution)/shard_map/ppermute | solution.py:343
  407.3 9.7 %collective-permute-done.32.p3_low = bf16[64,2048]{1,0:T(8,128)(2,1)S(1)} collective-permute-done((bf16[64,2048]{1,0:T(8,128)(2,1)S(1)}, bf16[64,2048]{1,0:T(8,128)(2,1)S(1)}, u32[]{:S(2)}, u32[]{:S(2)}) %collective-permute-start.32) | collective-permute-done | bytes 262176 | tf_op jit(solution)/shard_map/ppermute | solution.py:343
  432.5 22.2 %all-to-all-done.3 = bf16[8,256,128]{2,1,0:T(8,128)(2,1)} async-done(((bf16[8,256,128]{2,1,0:T(8,128)(2,1)}), bf16[8,256,128]{2,1,0:T(8,128)(2,1)}, u32[]{:S(2)}, u32[]{:S(2)}) %all-to-all-start.3) | async-done | bytes 524320 | tf_op jit(solution)/shard_map/all_to_all | solution.py:355
  466.4 28.3 %attend_back.1 = (bf16[32,2,64,256]{3,2,1,0:T(8,128)(2,1)}, bf16[2048,384]{1,0:T(8,128)(2,1)}) custom-call(s32[2]{0:T(128)S(1)} %fusion.29.split_ref, bf16[2048,128]{1,0:T(8,128)(2,1)S(1)} %copy-done.13, bf16[2048,128]{1,0:T(8,128)(2,1)S(1)} %copy-done.15, bf16[2048,128]{1,0:T(8,128)(2,1)S(1)} %copy-done.17, bf16[2048,128]{1,0:T(8,128)(2,1)S(1)} %copy-done.19, ...), custom_call_target="tpu_custom_call" | custom-call | flops 1000 | bytes 1000 | tf_op jit(solution)/shard_map/attend_back/pallas_call | solution.py:642
  500.6 10.9 %fusion.45 = bf16[2048,256]{0,1:T(8,128)(2,1)S(1)} fusion(bf16[4096,2048]{1,0:T(8,128)(2,1)} %all-gather.6.cloned.1.call-done, bf16[4096,256]{1,0:T(8,128)(2,1)} %bitcast.145), kind=kOutput, calls=%fused_computation.160 | convolution fusion | flops 4294967296 | bytes 19922944 | tf_op jit(solution)/shard_map/dot_general | solution.py:391
  518.0 32.4 %hidden.4 = (bf16[4096,768]{1,0:T(8,128)(2,1)}, bf16[4096,768]{1,0:T(8,128)(2,1)}, bf16[4096,768]{1,0:T(8,128)(2,1)}, bf16[4096,2048]{1,0:T(8,128)(2,1)}) custom-call(s32[2]{0:T(128)S(1)} %pad_add_fusion.where_ref, ...), custom_call_target="tpu_custom_call", output_to_operand_aliasing={{0}: (13, {}), {1}: (14, {}), {2}: (15, {}), {3}: (16, {})} | custom-call | flops 1000 | bytes 1000 | tf_op jit(solution)/shard_map/hidden/pallas_call | solution.py:956
  570.2 21.3 %hidden.5 = (bf16[4096,768]{1,0:T(8,128)(2,1)}, bf16[4096,768]{1,0:T(8,128)(2,1)}, bf16[4096,768]{1,0:T(8,128)(2,1)}, bf16[4096,2048]{1,0:T(8,128)(2,1)}) custom-call(s32[2]{0:T(128)S(1)} %pad_add_fusion.where_ref, ...), custom_call_target="tpu_custom_call", output_to_operand_aliasing={{0}: (9, {}), {1}: (10, {}), {2}: (11, {}), {3}: (12, {})} | custom-call | flops 1000 | bytes 1000 | tf_op jit(solution)/shard_map/hidden/pallas_call | solution.py:956
  591.5 19.1 %weight_grad.3 = bf16[2048,768]{1,0:T(8,128)(2,1)} custom-call(bf16[4096,2048]{1,0:T(8,128)(2,1)} %all-gather.8.cloned.1.call-done.refs_0_.left_ref, bf16[4096,768]{1,0:T(8,128)(2,1)} %get-tuple-element.212.right_ref), custom_call_target="tpu_custom_call" | custom-call | flops 1000 | bytes 1000 | tf_op jit(solution)/shard_map/weight_grad/pallas_call | solution.py:985
  625.0 18.4 %weight_grad.4 = bf16[2048,768]{1,0:T(8,128)(2,1)S(1)} custom-call(bf16[4096,2048]{1,0:T(8,128)(2,1)} %all-gather.8.cloned.1.call-done.refs_0_.left_ref, bf16[4096,768]{1,0:T(8,128)(2,1)} %get-tuple-element.220.right_ref), custom_call_target="tpu_custom_call" | custom-call | flops 1000 | bytes 1000 | tf_op jit(solution)/shard_map/weight_grad/pallas_call | solution.py:985
  658.8 20.0 %weight_grad.5.own_ref = bf16[768,2048]{1,0:T(8,128)(2,1)S(1)} custom-call(bf16[4096,768]{1,0:T(8,128)(2,1)} %get-tuple-element.228.left_ref, bf16[4096,2048]{1,0:T(8,128)(2,1)} %get-tuple-element.229.right_ref), custom_call_target="tpu_custom_call" | custom-call | flops 1000 | bytes 1000 | tf_op jit(solution)/shard_map/weight_grad/pallas_call | solution.py:985
  711.1 8.7 %place_columns.2.rest_0_ = f32[512,11264]{1,0:T(8,128)} custom-call(s32[1]{0:T(128)} %bitcast.47.where_ref.core_ref, bf16[4,512,768]{2,1,0:T(8,128)(2,1)} %all-to-all-done.6.own_ref, bf16[4,512,768]{2,1,0:T(8,128)(2,1)} %collective-permute-done.57.other_ref), custom_call_target="tpu_custom_call" | custom-call | flops 1000 | bytes 1000 | tf_op jit(solution)/shard_map/place_columns/pallas_call | solution.py:1020
  719.8 10.0 %place_down.1 = f32[1408,2048]{1,0:T(8,128)} custom-call(s32[1]{0:T(128)} %bitcast.47.where_ref.core_ref, bf16[768,2048]{1,0:T(8,128)(2,1)} %copy-done.1, bf16[768,2048]{1,0:T(8,128)(2,1)} %collective-permute-done.58.other_ref), custom_call_target="tpu_custom_call" | custom-call | flops 1000 | bytes 1000 | tf_op jit(solution)/shard_map/place_down/pallas_call | solution.py:1062
  729.8 11.3 %place_qkv.1 = f32[512,6144]{1,0:T(8,128)} custom-call(s32[2]{0:T(128)} %pad_add_fusion.1.where_ref, bf16[4,4,256,384]{3,2,1,0:T(8,128)(2,1)} %bitcast.144, bf16[4,4,256,384]{3,2,1,0:T(8,128)(2,1)} %collective-permute-done.59.other_ref), custom_call_target="tpu_custom_call" | custom-call | flops 1000 | bytes 1000 | tf_op jit(solution)/shard_map/place_qkv/pallas_call | solution.py:1089
  (365 shorter events, 303.2 us)
Async XLA Ops:
  7.2 136.0 %all-gather.6.cloned.1.call-start = ((), (), s32[]{:S(2)}) async-start(), calls=%async_computation.9 | async-start | bytes 17301504 | tf_op jit(solution)/shard_map/all_gather | solution.py:1160
  143.1 47.2 %all-to-all-start.1 = ((bf16[4,512,768]{2,1,0:T(8,128)(2,1)}), bf16[4,512,768]{2,1,0:T(8,128)(2,1)}, u32[]{:S(2)}, u32[]{:S(2)}) async-start(bf16[4,512,768]{2,1,0:T(8,128)(2,1)} %get-tuple-element.140), calls=%async_computation.1 | async-start | bytes 6291456 | tf_op jit(solution)/shard_map/all_to_all | solution.py:355
  190.3 64.9 %all-to-all-start.2 = ((bf16[4,512,768]{2,1,0:T(8,128)(2,1)}), bf16[4,512,768]{2,1,0:T(8,128)(2,1)}, u32[]{:S(2)}, u32[]{:S(2)}) async-start(bf16[4,512,768]{2,1,0:T(8,128)(2,1)} %get-tuple-element.153), calls=%async_computation.2 | async-start | bytes 6291456 | tf_op jit(solution)/shard_map/all_to_all | solution.py:355
  195.0 299.8 %all-gather.8.cloned.1.call-start = ((), (), s32[]{:S(2)}) async-start(), calls=%async_computation.10 | async-start | bytes 17301504 | tf_op jit(solution)/shard_map/all_gather | solution.py:1203
  221.6 52.7 %collective-permute-start.23 = (bf16[256,2048]{1,0:T(8,128)(2,1)}, bf16[256,2048]{1,0:T(8,128)(2,1)}, u32[]{:S(2)}, u32[]{:S(2)}) collective-permute-start(bf16[256,2048]{1,0:T(8,128)(2,1)} %collective-permute-done.5.refs_1_), channel_id=1, source_target_pairs={{0,8},{1,9},{2,10},{3,11},{4,12},{5,13},{6,14},{7,15},{8,16},{9,17... | collective-permute-start | bytes 3145736 | tf_op jit(solution)/shard_map/ppermute | solution.py:347
  287.5 43.5 %collective-permute-start.24 = (bf16[256,2048]{1,0:T(8,128)(2,1)}, bf16[256,2048]{1,0:T(8,128)(2,1)}, u32[]{:S(2)}, u32[]{:S(2)}) collective-permute-start(bf16[256,2048]{1,0:T(8,128)(2,1)} %collective-permute-done.13.refs_2_), channel_id=1, source_target_pairs={{0,8},{1,9},{2,10},{3,11},{4,12},{5,13},{6,14},{7,15},{8,16},{9,17... | collective-permute-start | bytes 3145736 | tf_op jit(solution)/shard_map/ppermute | solution.py:347
  349.0 105.6 %collective-permute-start.35 = (bf16[4,128,2048]{2,1,0:T(8,128)(2,1)}, bf16[4,128,2048]{2,1,0:T(8,128)(2,1)}, u32[]{:S(2)}, u32[]{:S(2)}) collective-permute-start(bf16[4,128,2048]{2,1,0:T(8,128)(2,1)} %bitcast.26), channel_id=1, source_target_pairs={{0,4},{1,5},{2,6},{3,7},{4,0},{5,1},{6,2},{7,3},{8,12},{9,13},{10,... | collective-permute-start | bytes 6291464 | tf_op jit(solution)/shard_map/ppermute | solution.py:343
  454.6 40.0 %collective-permute-start.34 = (bf16[256,2048]{1,0:T(8,128)(2,1)}, bf16[256,2048]{1,0:T(8,128)(2,1)}, u32[]{:S(2)}, u32[]{:S(2)}) collective-permute-start(bf16[256,2048]{1,0:T(8,128)(2,1)} %collective-permute-done.24.refs_6_), channel_id=1, source_target_pairs={{0,8},{1,9},{2,10},{3,11},{4,12},{5,13},{6,14},{7,15},{8,16},{9,17... | collective-permute-start | bytes 3145736 | tf_op jit(solution)/shard_map/ppermute | solution.py:347
  458.3 41.7 %collective-permute-start.38 = (bf16[128,2048]{1,0:T(8,128)(2,1)}, bf16[128,2048]{1,0:T(8,128)(2,1)}, u32[]{:S(2)}, u32[]{:S(2)}) collective-permute-start(bf16[128,2048]{1,0:T(8,128)(2,1)} %get-tuple-element.265), channel_id=1, source_target_pairs={{0,3},{1,2},{2,1},{3,0},{4,7},{5,6},{6,5},{7,4},{8,11},{9,10},{10,... | collective-permute-start | bytes 1572872 | tf_op jit(solution)/shard_map/ppermute | solution.py:343
  461.4 38.9 %collective-permute-start.37 = (bf16[128,2048]{1,0:T(8,128)(2,1)}, bf16[128,2048]{1,0:T(8,128)(2,1)}, u32[]{:S(2)}, u32[]{:S(2)}) collective-permute-start(bf16[128,2048]{1,0:T(8,128)(2,1)} %get-tuple-element.266), channel_id=1, source_target_pairs={{0,2},{1,3},{2,0},{3,1},{4,6},{5,7},{6,4},{7,5},{8,10},{9,11},{10,... | collective-permute-start | bytes 1572872 | tf_op jit(solution)/shard_map/ppermute | solution.py:343
  461.7 56.2 %collective-permute-start.40 = (bf16[256,2048]{1,0:T(8,128)(2,1)}, bf16[256,2048]{1,0:T(8,128)(2,1)}, u32[]{:S(2)}, u32[]{:S(2)}) collective-permute-start(bf16[256,2048]{1,0:T(8,128)(2,1)} %collective-permute-done.5.refs_1_), channel_id=1, source_target_pairs={{0,4},{1,5},{2,6},{3,7},{4,0},{5,1},{6,2},{7,3},{8,12},{9,13},{10,... | collective-permute-start | bytes 3145736 | tf_op jit(solution)/shard_map/ppermute | solution.py:343
  461.7 56.2 %collective-permute-start.41 = (bf16[256,2048]{1,0:T(8,128)(2,1)}, bf16[256,2048]{1,0:T(8,128)(2,1)}, u32[]{:S(2)}, u32[]{:S(2)}) collective-permute-start(bf16[256,2048]{1,0:T(8,128)(2,1)} %collective-permute-done.13.refs_2_), channel_id=1, source_target_pairs={{0,4},{1,5},{2,6},{3,7},{4,0},{5,1},{6,2},{7,3},{8,12},{9,13},{10,... | collective-permute-start | bytes 3145736 | tf_op jit(solution)/shard_map/ppermute | solution.py:343
  494.8 55.9 %all-to-all-start.4 = ((bf16[4,512,384]{2,1,0:T(8,128)(2,1)}), bf16[4,512,384]{2,1,0:T(8,128)(2,1)S(1)}, u32[]{:S(2)}, u32[]{:S(2)}) async-start(bf16[4,512,384]{2,1,0:T(8,128)(2,1)} %bitcast.146), calls=%async_computation.4 | async-start | bytes 3145728 | tf_op jit(solution)/shard_map/all_to_all | solution.py:355
  499.6 111.2 %reduce-scatter.2.cloned.1.call-start = ((), (), s32[]{:S(2)}) async-start(), calls=%async_computation.11 | async-start | bytes 2359296 | tf_op jit(solution)/shard_map/reduce_scatter | solution.py:1269
  555.7 55.2 %all-to-all-start.5 = ((bf16[4,512,768]{2,1,0:T(8,128)(2,1)}), bf16[4,512,768]{2,1,0:T(8,128)(2,1)}, u32[]{:S(2)}, u32[]{:S(2)}) async-start(bf16[4,512,768]{2,1,0:T(8,128)(2,1)} %pick_heads.1), calls=%async_computation.5 | async-start | bytes 6291456 | tf_op jit(solution)/shard_map/all_to_all | solution.py:355
  560.3 122.8 %all-gather.12.cloned.1.call-start = ((), (), s32[]{:S(2)}) async-start(), calls=%async_computation.13 | async-start | bytes 3932160 | tf_op jit(solution)/shard_map/all_gather | solution.py:1289
  563.2 47.6 %collective-permute-start.46 = (bf16[256,384]{1,0:T(8,128)(2,1)S(1)}, bf16[256,384]{1,0:T(8,128)(2,1)S(1)}, u32[]{:S(2)}, u32[]{:S(2)}) collective-permute-start(bf16[256,384]{1,0:T(8,128)(2,1)S(1)} %bitcast.153), channel_id=1, source_target_pairs={{0,1},{1,0},{2,3},{3,2},{4,5},{5,4},{6,7},{7,6},{8,9},{9,8},{10,11... | collective-permute-start | bytes 589832 | tf_op jit(solution)/shard_map/ppermute | solution.py:343
  566.6 44.2 %collective-permute-start.47 = (bf16[256,384]{1,0:T(8,128)(2,1)}, bf16[256,384]{1,0:T(8,128)(2,1)S(1)}, u32[]{:S(2)}, u32[]{:S(2)}) collective-permute-start(bf16[256,384]{1,0:T(8,128)(2,1)} %bitcast.38), channel_id=1, source_target_pairs={{0,2},{1,3},{2,0},{3,1},{4,6},{5,7},{6,4},{7,5},{8,10},{9,11},{10,... | collective-permute-start | bytes 589832 | tf_op jit(solution)/shard_map/ppermute | solution.py:343
  569.8 41.0 %collective-permute-start.48 = (bf16[256,384]{1,0:T(8,128)(2,1)}, bf16[256,384]{1,0:T(8,128)(2,1)S(1)}, u32[]{:S(2)}, u32[]{:S(2)}) collective-permute-start(bf16[256,384]{1,0:T(8,128)(2,1)} %bitcast.154), channel_id=1, source_target_pairs={{0,3},{1,2},{2,1},{3,0},{4,7},{5,6},{6,5},{7,4},{8,11},{9,10},{10,... | collective-permute-start | bytes 589832 | tf_op jit(solution)/shard_map/ppermute | solution.py:343
  611.9 41.3 %all-to-all-start.6 = ((bf16[4,512,768]{2,1,0:T(8,128)(2,1)}), bf16[4,512,768]{2,1,0:T(8,128)(2,1)}, u32[]{:S(2)}, u32[]{:S(2)}) async-start(bf16[4,512,768]{2,1,0:T(8,128)(2,1)} %bitcast.40), calls=%async_computation.7 | async-start | bytes 6291456 | tf_op jit(solution)/shard_map/all_to_all | solution.py:355
  658.8 52.3 %collective-permute-start.57 = (bf16[4,512,768]{2,1,0:T(8,128)(2,1)}, bf16[4,512,768]{2,1,0:T(8,128)(2,1)}, u32[]{:S(2)}, u32[]{:S(2)}) collective-permute-start(bf16[4,512,768]{2,1,0:T(8,128)(2,1)} %all-to-all-done.6.own_ref), channel_id=1, source_target_pairs={{0,4},{1,5},{2,6},{3,7},{4,0},{5,1},{6,2},{7,3},{8,12},{9,13},{10,... | collective-permute-start | bytes 9437192 | tf_op jit(solution)/shard_map/ppermute | solution.py:343
  683.1 46.7 %collective-permute-start.59 = (bf16[4,4,256,384]{3,2,1,0:T(8,128)(2,1)}, bf16[4,4,256,384]{3,2,1,0:T(8,128)(2,1)}, u32[]{:S(2)}, u32[]{:S(2)}) collective-permute-start(bf16[4,4,256,384]{3,2,1,0:T(8,128)(2,1)} %bitcast.143), channel_id=1, source_target_pairs={{0,4},{1,5},{2,6},{3,7},{4,0},{5,1},{6,2},{7,3},{8,12},{9,13},{10,... | collective-permute-start | bytes 9437192 | tf_op jit(solution)/shard_map/ppermute | solution.py:343
  685.7 55.4 %all-to-all-start.7 = ((bf16[4,512,768]{2,1,0:T(8,128)(2,1)}), bf16[4,512,768]{2,1,0:T(8,128)(2,1)}, u32[]{:S(2)}, u32[]{:S(2)}) async-start(bf16[4,512,768]{2,1,0:T(8,128)(2,1)} %bitcast.136), calls=%async_computation.8 | async-start | bytes 6291456 | tf_op jit(solution)/shard_map/all_to_all | solution.py:355
  690.4 58.7 %all-gather.10.cloned.1.call-start = ((), (), s32[]{:S(2)}) async-start(), calls=%async_computation.12 | async-start | bytes 2359296 | tf_op jit(solution)/shard_map/all_gather | solution.py:1305
  (111 other events, 1260.1 us)
Sparse Core Ops, SparseCore 0:
  12.3 130.7 all-gather.5
  287.6 170.5 all-gather.7
  555.8 36.9 reduce-scatter.1
  612.0 65.1 all-gather.11
  692.5 33.5 all-gather.9

commit v4 on v3

--- a/solution.py
+++ b/solution.py
@@ -508,7 +508,7 @@
         in_specs=[smem, smem, vmem, vmem, vmem, vmem],
         out_specs=(vmem,) * 7,
         scratch_shapes=[pltpu.VMEM((2, row_len, 2 * HD), BF), pltpu.VMEM((2, row_len, 2 * HD), BF)],
-        compiler_params=pltpu.CompilerParams(vmem_limit_bytes=48 * 2**20),
+        compiler_params=pltpu.CompilerParams(vmem_limit_bytes=26 * 2**20),
         cost_estimate=SMALL,
         name="attend",
     )(split, where, mixed, *tables)
@@ -656,7 +656,7 @@
         ]
         + [pltpu.VMEM((row_len, 2 * HD), BF)] * 5
         + [pltpu.SemaphoreType.DMA((5,))],
-        compiler_params=pltpu.CompilerParams(vmem_limit_bytes=48 * 2**20),
+        compiler_params=pltpu.CompilerParams(vmem_limit_bytes=34 * 2**20),
         cost_estimate=SMALL,
         name="attend_back",
     )(split, q, k, v, out, d_out, logs, *tables)
@@ -705,7 +705,7 @@
     )(where, weight, weight, weight)
 
 
-def small_call(kernel, name, out_shape, where, *arrays, flops=0, scratch=(), limit=32):
+def small_call(kernel, name, out_shape, where, *arrays, flops=0, scratch=(), limit=20):
     size = sum(x.size * x.dtype.itemsize for x in arrays)
     vmem = pl.BlockSpec(memory_space=pltpu.VMEM)
     return pl.pallas_call(
@@ -967,7 +967,7 @@
             dma((2, 9)), dma((width // 256, 9)), dma((2, 6, 4)),
         ]
         + ([held] if own else []),
-        compiler_params=pltpu.CompilerParams(vmem_limit_bytes=48 * 2**20),
+        compiler_params=pltpu.CompilerParams(vmem_limit_bytes=(38 if own else 32) * 2**20),
         cost_estimate=SMALL,
         name="hidden",
     )(where, *mids, *outs, *weights, *kept)
@@ -1284,7 +1284,7 @@
             pltpu.VMEM((8 * tokens, 12 * HD), BF),
             pltpu.VMEM((8 * tokens, 512), F32),
         ],
-        limit=48,
+        limit=24,
     )
     heads = lax.all_gather(jnp.stack(pairs), "z", axis=0)
     gate_parts, d_up_grad, near, far, act_all = tie(

time: 779 us -> 796 us (1.022)
  local copies, waits for them, and re-layouts: 58.8 us -> 79.1 us
    unnamed x130 -> x182, local copies, waits for them, and re-layouts: 39.4 us -> 52 us
    pallas_call x4, Pallas kernels: 11.8 us -> 23.1 us  [small_call(): pl.pallas_call(kernel, out_shape=out_shape, in_specs=[pl.BlockSpec(memory...]
  transfers between devices with their start and end apart: 77 -> 77, of which waited for: 32 -> 35; matrix products, arithmetic and copies ran while one was open for 13% -> 14% of each run, Pallas kernels for 31% -> 30%
where the time goes in v4:
time: 796 us; the launch traced here: 785 us
  waiting for transfers between devices  264 us (33%)
  Pallas kernels  245 us (31%)
  starting transfers between devices  92.8 us (12%)
  local copies, waits for them, and re-layouts  79.1 us (10%)
  other arithmetic  52.8 us (7%)
  matrix products  35.5 us (4%)
  between operations  15 us (2%)
    ppermute x52, waiting for transfers between devices, swap(): lax.ppermute(value, ('z', 'core', 'fsdp'), [(i, i ^ mask) for i in range(...  124 us
    pallas_call x3, Pallas kernels, hidden_layer(): pl.pallas_call(functools.partial(hidden_kernel, steps=steps, own=own), in...  79.3 us
    all_gather x1, waiting for transfers between devices, plane_plan(): lax.all_gather(normed_in.astype(BF), everywhere, axis=0, tiled=True)  70.2 us
    pallas_call x3, Pallas kernels, weight_grad(): pl.pallas_call(weight_grad_kernel, grid=(features // step,), in_specs=[pl...  57.4 us
    unnamed x182, local copies, waits for them, and re-layouts  52 us
    ppermute x52, starting transfers between devices, swap(): lax.ppermute(value, ('z', 'core', 'fsdp'), [(i, i ^ mask) for i in range(...  41.7 us
    all_to_all x8, waiting for transfers between devices, exchange(): return lax.all_to_all(value, axis, split_axis=0, concat_axis=0, tiled=True)  37.4 us
    all_to_all x8, starting transfers between devices, exchange(): return lax.all_to_all(value, axis, split_axis=0, concat_axis=0, tiled=True)  35.5 us
  transfers between devices with their start and end apart: 77, of which 35 were waited for; matrix products, arithmetic and copies ran while one was open for 14% of the time, Pallas kernels for 30%

profile of v4, /device:TPU:0, one launch (start us, length us, event | category | flops | bytes accessed | tf_op | source)
XLA Modules:
  0.0 784.6 jit_solution(13799528910844444062)
XLA Ops:
  19.2 11.0 %collective-permute-done = bf16[128,2048]{1,0:T(8,128)(2,1)S(1)} collective-permute-done((bf16[128,2048]{1,0:T(8,128)(2,1)}, bf16[128,2048]{1,0:T(8,128)(2,1)S(1)}, u32[]{:S(2)}, u32[]{:S(2)}) %collective-permute-start) | collective-permute-done | bytes 524320 | tf_op jit(solution)/shard_map/ppermute | solution.py:343
  73.0 70.2 %all-gather.6.cloned.1.call-done = bf16[4096,2048]{1,0:T(8,128)(2,1)} async-done(((bf16[128,2048]{1,0:T(8,128)(2,1)}), bf16[4096,2048]{1,0:T(8,128)(2,1)}) %all-gather.6.cloned.1.call-update) | async-done | bytes 16777232 | tf_op jit(solution)/shard_map/all_gather | solution.py:1160
  151.1 8.9 %convolution_add_fusion = f32[4096,256]{1,0:T(8,128)S(1)} fusion(bf16[4096,2048]{1,0:T(8,128)(2,1)} %all-gather.6.cloned.1.call-done, bf16[2048,256]{1,0:T(8,128)(2,1)} %bitcast.16, f32[256]{0:T(256)S(1)} %pad_maximum_fusion.4), kind=kOutput, calls=%fused_computation | convolution fusion | flops 4296015872 | bytes 22021120 | tf_op jit(solution)/shard_map/dot_general | solution.py:383
  160.0 19.7 %attend.1 = (bf16[2048,128]{1,0:T(8,128)(2,1)S(1)}, bf16[2048,128]{1,0:T(8,128)(2,1)S(1)}, bf16[2048,128]{1,0:T(8,128)(2,1)S(1)}, bf16[2048,128]{1,0:T(8,128)(2,...) custom-call(s32[2]{0:T(128)S(1)} %fusion.29.split_ref, ...), custom_call_target="tpu_custom_call" | custom-call | flops 1000 | bytes 1000 | tf_op jit(solution)/shard_map/attend/pallas_call | solution.py:504
  191.9 11.6 %pair.1 = (bf16[256,256]{1,0:T(8,128)(2,1)S(1)}, bf16[256,256]{1,0:T(8,128)(2,1)S(1)}, bf16[256,256]{1,0:T(8,128)(2,1)S(1)}, bf16[256,256]{1,0:T(8,128)(2,1)S(1)}) custom-call(s32[2]{0:T(128)S(1)} %pad_add_fusion.where_ref, bf16[4,256,128]{2,1,0:T(8,128)(2,1)S(1)} %get-tuple-element.143.mine_ref, bf16[4,256,128]{2,1,0:T(8,128)(2,1)S(1)} %collective-permute-done.6.theirs_ref), custom_call_target="tpu_custom_call" | custom-call | flops 1000 | bytes 1000 | tf_op jit(solution)/shard_map/pair/pallas_call | solution.py:711
  227.1 12.5 %collective-permute-done.12 = bf16[128,2048]{1,0:T(8,128)(2,1)S(1)} collective-permute-done((bf16[128,2048]{1,0:T(8,128)(2,1)S(1)}, bf16[128,2048]{1,0:T(8,128)(2,1)S(1)}, u32[]{:S(2)}, u32[]{:S(2)}) %collective-permute-start.12) | collective-permute-done | bytes 524320 | tf_op jit(solution)/shard_map/ppermute | solution.py:343
  239.7 9.2 %collective-permute-done.11 = bf16[128,2048]{1,0:T(8,128)(2,1)S(1)} collective-permute-done((bf16[128,2048]{1,0:T(8,128)(2,1)S(1)}, bf16[128,2048]{1,0:T(8,128)(2,1)S(1)}, u32[]{:S(2)}, u32[]{:S(2)}) %collective-permute-start.11) | collective-permute-done | bytes 524320 | tf_op jit(solution)/shard_map/ppermute | solution.py:343
  258.1 8.6 %collective-permute-done.14.refs_1_ = bf16[128,2048]{1,0:T(8,128)(2,1)S(1)} collective-permute-done((bf16[128,2048]{1,0:T(8,128)(2,1)S(1)}, bf16[128,2048]{1,0:T(8,128)(2,1)S(1)}, u32[]{:S(2)}, u32[]{:S(2)}) %collective-permute-start.14) | collective-permute-done | bytes 524320 | tf_op jit(solution)/shard_map/ppermute | solution.py:343
  293.9 27.4 %hidden.3 = (bf16[4096,768]{1,0:T(8,128)(2,1)}, bf16[4096,768]{1,0:T(8,128)(2,1)}, bf16[4096,768]{1,0:T(8,128)(2,1)}, bf16[4096,2048]{1,0:T(8,128)(2,1)}, bf16[4...) custom-call(s32[2]{0:T(128)S(1)} %pad_add_fusion.where_ref, ...), custom_call_target="tpu_custom_call" | custom-call | flops 1000 | bytes 1000 | tf_op jit(solution)/shard_map/hidden/pallas_call | solution.py:956
  338.1 15.1 %collective-permute-done.28 = bf16[128,2048]{1,0:T(8,128)(2,1)S(1)} collective-permute-done((bf16[128,2048]{1,0:T(8,128)(2,1)}, bf16[128,2048]{1,0:T(8,128)(2,1)S(1)}, u32[]{:S(2)}, u32[]{:S(2)}) %collective-permute-start.28) | collective-permute-done | bytes 524320 | tf_op jit(solution)/shard_map/ppermute | solution.py:343
  376.8 21.7 %collective-permute-done.30.p1 = bf16[128,2048]{1,0:T(8,128)(2,1)S(1)} collective-permute-done((bf16[128,2048]{1,0:T(8,128)(2,1)S(1)}, bf16[128,2048]{1,0:T(8,128)(2,1)S(1)}, u32[]{:S(2)}, u32[]{:S(2)}) %collective-permute-start.30) | collective-permute-done | bytes 524320 | tf_op jit(solution)/shard_map/ppermute | solution.py:343
  401.9 10.6 %collective-permute-done.32.p3_low = bf16[64,2048]{1,0:T(8,128)(2,1)S(1)} collective-permute-done((bf16[64,2048]{1,0:T(8,128)(2,1)S(1)}, bf16[64,2048]{1,0:T(8,128)(2,1)S(1)}, u32[]{:S(2)}, u32[]{:S(2)}) %collective-permute-start.32) | collective-permute-done | bytes 262176 | tf_op jit(solution)/shard_map/ppermute | solution.py:343
  428.0 22.1 %all-to-all-done.3 = bf16[8,256,128]{2,1,0:T(8,128)(2,1)S(1)} async-done(((bf16[8,256,128]{2,1,0:T(8,128)(2,1)}), bf16[8,256,128]{2,1,0:T(8,128)(2,1)S(1)}, u32[]{:S(2)}, u32[]{:S(2)}) %all-to-all-start.3) | async-done | bytes 524320 | tf_op jit(solution)/shard_map/all_to_all | solution.py:355
  463.0 25.4 %attend_back.1 = (bf16[32,2,64,256]{3,2,1,0:T(8,128)(2,1)S(1)}, bf16[2048,384]{1,0:T(8,128)(2,1)S(1)}) custom-call(s32[2]{0:T(128)S(1)} %fusion.29.split_ref, bf16[2048,128]{1,0:T(8,128)(2,1)S(1)} %copy-done.36, bf16[2048,128]{1,0:T(8,128)(2,1)S(1)} %copy-done.38, bf16[2048,128]{1,0:T(8,128)(2,1)S(1)} %copy-done.40, bf16[2048,128]{1,0:T(8,128)(2,1)S(1)} %copy-done.42, ...), custom_call_target="tpu_custom_call" | custom-call | flops 1000 | bytes 1000 | tf_op jit(solution)/shard_map/attend_back/pallas_call | solution.py:642
  497.4 10.9 %fusion.45 = bf16[2048,256]{0,1:T(8,128)(2,1)S(1)} fusion(bf16[4096,2048]{1,0:T(8,128)(2,1)} %all-gather.6.cloned.1.call-done, bf16[4096,256]{1,0:T(8,128)(2,1)} %bitcast.141), kind=kOutput, calls=%fused_computation.160 | convolution fusion | flops 4294967296 | bytes 19922944 | tf_op jit(solution)/shard_map/dot_general | solution.py:391
  519.2 30.8 %hidden.4 = (bf16[4096,768]{1,0:T(8,128)(2,1)}, bf16[4096,768]{1,0:T(8,128)(2,1)}, bf16[4096,768]{1,0:T(8,128)(2,1)}, bf16[4096,2048]{1,0:T(8,128)(2,1)}) custom-call(s32[2]{0:T(128)S(1)} %pad_add_fusion.where_ref, ...), custom_call_target="tpu_custom_call", output_to_operand_aliasing={{0}: (13, {}), {1}: (14, {}), {2}: (15, {}), {3}: (16, {})} | custom-call | flops 1000 | bytes 1000 | tf_op jit(solution)/shard_map/hidden/pallas_call | solution.py:956
  582.4 21.2 %hidden.5 = (bf16[4096,768]{1,0:T(8,128)(2,1)S(1)}, bf16[4096,768]{1,0:T(8,128)(2,1)}, bf16[4096,768]{1,0:T(8,128)(2,1)}, bf16[4096,2048]{1,0:T(8,128)(2,1)}) custom-call(s32[2]{0:T(128)S(1)} %pad_add_fusion.where_ref, ...), custom_call_target="tpu_custom_call", output_to_operand_aliasing={{0}: (9, {}), {1}: (10, {}), {2}: (11, {}), {3}: (12, {})} | custom-call | flops 1000 | bytes 1000 | tf_op jit(solution)/shard_map/hidden/pallas_call | solution.py:956
  606.3 19.0 %weight_grad.3 = bf16[2048,768]{1,0:T(8,128)(2,1)} custom-call(bf16[4096,2048]{1,0:T(8,128)(2,1)} %all-gather.8.cloned.1.call-done.refs_0_.left_ref, bf16[4096,768]{1,0:T(8,128)(2,1)} %get-tuple-element.212.right_ref), custom_call_target="tpu_custom_call" | custom-call | flops 1000 | bytes 1000 | tf_op jit(solution)/shard_map/weight_grad/pallas_call | solution.py:985
  640.7 18.4 %weight_grad.4 = bf16[2048,768]{1,0:T(8,128)(2,1)S(1)} custom-call(bf16[4096,2048]{1,0:T(8,128)(2,1)} %all-gather.8.cloned.1.call-done.refs_0_.left_ref, bf16[4096,768]{1,0:T(8,128)(2,1)} %get-tuple-element.220.right_ref), custom_call_target="tpu_custom_call" | custom-call | flops 1000 | bytes 1000 | tf_op jit(solution)/shard_map/weight_grad/pallas_call | solution.py:985
  660.8 8.3 %all-to-all-done.6.own_ref = bf16[4,512,768]{2,1,0:T(8,128)(2,1)} async-done(((bf16[4,512,768]{2,1,0:T(8,128)(2,1)}), bf16[4,512,768]{2,1,0:T(8,128)(2,1)}, u32[]{:S(2)}, u32[]{:S(2)}) %all-to-all-start.6) | async-done | bytes 3145760 | tf_op jit(solution)/shard_map/all_to_all | solution.py:355
  674.6 20.0 %weight_grad.5.own_ref = bf16[768,2048]{1,0:T(8,128)(2,1)S(1)} custom-call(bf16[4096,768]{1,0:T(8,128)(2,1)} %copy-done.2, bf16[4096,2048]{1,0:T(8,128)(2,1)} %get-tuple-element.229.right_ref), custom_call_target="tpu_custom_call" | custom-call | flops 1000 | bytes 1000 | tf_op jit(solution)/shard_map/weight_grad/pallas_call | solution.py:985
  726.8 8.7 %place_columns.2.rest_0_ = f32[512,11264]{1,0:T(8,128)} custom-call(s32[1]{0:T(128)} %bitcast.47.where_ref.core_ref, bf16[4,512,768]{2,1,0:T(8,128)(2,1)} %all-to-all-done.6.own_ref, bf16[4,512,768]{2,1,0:T(8,128)(2,1)} %collective-permute-done.57.other_ref), custom_call_target="tpu_custom_call" | custom-call | flops 1000 | bytes 1000 | tf_op jit(solution)/shard_map/place_columns/pallas_call | solution.py:1020
  735.4 10.0 %place_down.1 = f32[1408,2048]{1,0:T(8,128)} custom-call(s32[1]{0:T(128)} %bitcast.47.where_ref.core_ref, bf16[768,2048]{1,0:T(8,128)(2,1)} %copy-done.7, bf16[768,2048]{1,0:T(8,128)(2,1)} %collective-permute-done.58.other_ref), custom_call_target="tpu_custom_call" | custom-call | flops 1000 | bytes 1000 | tf_op jit(solution)/shard_map/place_down/pallas_call | solution.py:1062
  745.5 11.3 %place_qkv.1 = f32[512,6144]{1,0:T(8,128)} custom-call(s32[2]{0:T(128)} %pad_add_fusion.1.where_ref, bf16[4,4,256,384]{3,2,1,0:T(8,128)(2,1)} %bitcast.149, bf16[4,4,256,384]{3,2,1,0:T(8,128)(2,1)} %collective-permute-done.59.other_ref), custom_call_target="tpu_custom_call" | custom-call | flops 1000 | bytes 1000 | tf_op jit(solution)/shard_map/place_qkv/pallas_call | solution.py:1089
  (418 shorter events, 337.2 us)
Async XLA Ops:
  7.2 136.0 %all-gather.6.cloned.1.call-start = ((), (), s32[]{:S(2)}) async-start(), calls=%async_computation.9 | async-start | bytes 17301504 | tf_op jit(solution)/shard_map/all_gather | solution.py:1160
  143.1 40.6 %all-to-all-start.1 = ((bf16[4,512,768]{2,1,0:T(8,128)(2,1)}), bf16[4,512,768]{2,1,0:T(8,128)(2,1)S(1)}, u32[]{:S(2)}, u32[]{:S(2)}) async-start(bf16[4,512,768]{2,1,0:T(8,128)(2,1)} %get-tuple-element.140), calls=%async_computation.1 | async-start | bytes 6291456 | tf_op jit(solution)/shard_map/all_to_all | solution.py:355
  185.4 66.7 %all-to-all-start.2 = ((bf16[4,512,768]{2,1,0:T(8,128)(2,1)}), bf16[4,512,768]{2,1,0:T(8,128)(2,1)}, u32[]{:S(2)}, u32[]{:S(2)}) async-start(bf16[4,512,768]{2,1,0:T(8,128)(2,1)} %get-tuple-element.153), calls=%async_computation.2 | async-start | bytes 6291456 | tf_op jit(solution)/shard_map/all_to_all | solution.py:355
  190.1 300.9 %all-gather.8.cloned.1.call-start = ((), (), s32[]{:S(2)}) async-start(), calls=%async_computation.10 | async-start | bytes 17301504 | tf_op jit(solution)/shard_map/all_gather | solution.py:1203
  227.1 45.8 %collective-permute-start.23 = (bf16[256,2048]{1,0:T(8,128)(2,1)}, bf16[256,2048]{1,0:T(8,128)(2,1)}, u32[]{:S(2)}, u32[]{:S(2)}) collective-permute-start(bf16[256,2048]{1,0:T(8,128)(2,1)} %collective-permute-done.5.refs_1_), channel_id=1, source_target_pairs={{0,8},{1,9},{2,10},{3,11},{4,12},{5,13},{6,14},{7,15},{8,16},{9,17... | collective-permute-start | bytes 3145736 | tf_op jit(solution)/shard_map/ppermute | solution.py:347
  332.4 40.3 %collective-permute-start.29 = (bf16[256,2048]{1,0:T(8,128)(2,1)}, bf16[256,2048]{1,0:T(8,128)(2,1)S(1)}, u32[]{:S(2)}, u32[]{:S(2)}) collective-permute-start(bf16[256,2048]{1,0:T(8,128)(2,1)} %collective-permute-done.23.refs_5_), channel_id=1, source_target_pairs={{0,8},{1,9},{2,10},{3,11},{4,12},{5,13},{6,14},{7,15},{8,16},{9,17... | collective-permute-start | bytes 3145736 | tf_op jit(solution)/shard_map/ppermute | solution.py:347
  338.1 112.9 %collective-permute-start.35 = (bf16[4,128,2048]{2,1,0:T(8,128)(2,1)}, bf16[4,128,2048]{2,1,0:T(8,128)(2,1)}, u32[]{:S(2)}, u32[]{:S(2)}) collective-permute-start(bf16[4,128,2048]{2,1,0:T(8,128)(2,1)} %bitcast.26), channel_id=1, source_target_pairs={{0,4},{1,5},{2,6},{3,7},{4,0},{5,1},{6,2},{7,3},{8,12},{9,13},{10,... | collective-permute-start | bytes 6291464 | tf_op jit(solution)/shard_map/ppermute | solution.py:343
  451.0 39.9 %collective-permute-start.34 = (bf16[256,2048]{1,0:T(8,128)(2,1)}, bf16[256,2048]{1,0:T(8,128)(2,1)}, u32[]{:S(2)}, u32[]{:S(2)}) collective-permute-start(bf16[256,2048]{1,0:T(8,128)(2,1)} %collective-permute-done.24.refs_6_), channel_id=1, source_target_pairs={{0,8},{1,9},{2,10},{3,11},{4,12},{5,13},{6,14},{7,15},{8,16},{9,17... | collective-permute-start | bytes 3145736 | tf_op jit(solution)/shard_map/ppermute | solution.py:347
  455.1 40.7 %collective-permute-start.38 = (bf16[128,2048]{1,0:T(8,128)(2,1)}, bf16[128,2048]{1,0:T(8,128)(2,1)}, u32[]{:S(2)}, u32[]{:S(2)}) collective-permute-start(bf16[128,2048]{1,0:T(8,128)(2,1)} %get-tuple-element.265), channel_id=1, source_target_pairs={{0,3},{1,2},{2,1},{3,0},{4,7},{5,6},{6,5},{7,4},{8,11},{9,10},{10,... | collective-permute-start | bytes 1572872 | tf_op jit(solution)/shard_map/ppermute | solution.py:343
  456.5 39.5 %collective-permute-start.37 = (bf16[128,2048]{1,0:T(8,128)(2,1)}, bf16[128,2048]{1,0:T(8,128)(2,1)}, u32[]{:S(2)}, u32[]{:S(2)}) collective-permute-start(bf16[128,2048]{1,0:T(8,128)(2,1)} %get-tuple-element.266), channel_id=1, source_target_pairs={{0,2},{1,3},{2,0},{3,1},{4,6},{5,7},{6,4},{7,5},{8,10},{9,11},{10,... | collective-permute-start | bytes 1572872 | tf_op jit(solution)/shard_map/ppermute | solution.py:343
  457.2 61.9 %collective-permute-start.40 = (bf16[256,2048]{1,0:T(8,128)(2,1)}, bf16[256,2048]{1,0:T(8,128)(2,1)}, u32[]{:S(2)}, u32[]{:S(2)}) collective-permute-start(bf16[256,2048]{1,0:T(8,128)(2,1)} %collective-permute-done.5.refs_1_), channel_id=1, source_target_pairs={{0,4},{1,5},{2,6},{3,7},{4,0},{5,1},{6,2},{7,3},{8,12},{9,13},{10,... | collective-permute-start | bytes 3145736 | tf_op jit(solution)/shard_map/ppermute | solution.py:343
  457.2 61.9 %collective-permute-start.41 = (bf16[256,2048]{1,0:T(8,128)(2,1)}, bf16[256,2048]{1,0:T(8,128)(2,1)}, u32[]{:S(2)}, u32[]{:S(2)}) collective-permute-start(bf16[256,2048]{1,0:T(8,128)(2,1)} %collective-permute-done.13.refs_2_), channel_id=1, source_target_pairs={{0,4},{1,5},{2,6},{3,7},{4,0},{5,1},{6,2},{7,3},{8,12},{9,13},{10,... | collective-permute-start | bytes 3145736 | tf_op jit(solution)/shard_map/ppermute | solution.py:343
  490.9 63.2 %all-to-all-start.4 = ((bf16[4,512,384]{2,1,0:T(8,128)(2,1)}), bf16[4,512,384]{2,1,0:T(8,128)(2,1)S(1)}, u32[]{:S(2)}, u32[]{:S(2)}) async-start(bf16[4,512,384]{2,1,0:T(8,128)(2,1)} %bitcast.142), calls=%async_computation.4 | async-start | bytes 3145728 | tf_op jit(solution)/shard_map/all_to_all | solution.py:355
  495.6 129.9 %reduce-scatter.2.cloned.1.call-start = ((), (), s32[]{:S(2)}) async-start(), calls=%async_computation.11 | async-start | bytes 2359296 | tf_op jit(solution)/shard_map/reduce_scatter | solution.py:1269
  558.9 66.6 %all-to-all-start.5 = ((bf16[4,512,768]{2,1,0:T(8,128)(2,1)}), bf16[4,512,768]{2,1,0:T(8,128)(2,1)}, u32[]{:S(2)}, u32[]{:S(2)}) async-start(bf16[4,512,768]{2,1,0:T(8,128)(2,1)} %copy-done.8), calls=%async_computation.5 | async-start | bytes 6291456 | tf_op jit(solution)/shard_map/all_to_all | solution.py:355
  563.9 135.0 %all-gather.12.cloned.1.call-start = ((), (), s32[]{:S(2)}) async-start(), calls=%async_computation.13 | async-start | bytes 3932160 | tf_op jit(solution)/shard_map/all_gather | solution.py:1289
  568.7 56.7 %collective-permute-start.46 = (bf16[256,384]{1,0:T(8,128)(2,1)}, bf16[256,384]{1,0:T(8,128)(2,1)}, u32[]{:S(2)}, u32[]{:S(2)}) collective-permute-start(bf16[256,384]{1,0:T(8,128)(2,1)} %bitcast.153), channel_id=1, source_target_pairs={{0,1},{1,0},{2,3},{3,2},{4,5},{5,4},{6,7},{7,6},{8,9},{9,8},{10,11... | collective-permute-start | bytes 589832 | tf_op jit(solution)/shard_map/ppermute | solution.py:343
  571.9 53.5 %collective-permute-start.47 = (bf16[256,384]{1,0:T(8,128)(2,1)}, bf16[256,384]{1,0:T(8,128)(2,1)}, u32[]{:S(2)}, u32[]{:S(2)}) collective-permute-start(bf16[256,384]{1,0:T(8,128)(2,1)} %bitcast.154), channel_id=1, source_target_pairs={{0,2},{1,3},{2,0},{3,1},{4,6},{5,7},{6,4},{7,5},{8,10},{9,11},{10,... | collective-permute-start | bytes 589832 | tf_op jit(solution)/shard_map/ppermute | solution.py:343
  575.1 50.3 %collective-permute-start.48 = (bf16[256,384]{1,0:T(8,128)(2,1)}, bf16[256,384]{1,0:T(8,128)(2,1)}, u32[]{:S(2)}, u32[]{:S(2)}) collective-permute-start(bf16[256,384]{1,0:T(8,128)(2,1)} %bitcast.155), channel_id=1, source_target_pairs={{0,3},{1,2},{2,1},{3,0},{4,7},{5,6},{6,5},{7,4},{8,11},{9,10},{10,... | collective-permute-start | bytes 589832 | tf_op jit(solution)/shard_map/ppermute | solution.py:343
  627.7 41.4 %all-to-all-start.6 = ((bf16[4,512,768]{2,1,0:T(8,128)(2,1)}), bf16[4,512,768]{2,1,0:T(8,128)(2,1)}, u32[]{:S(2)}, u32[]{:S(2)}) async-start(bf16[4,512,768]{2,1,0:T(8,128)(2,1)} %bitcast.40), calls=%async_computation.7 | async-start | bytes 6291456 | tf_op jit(solution)/shard_map/all_to_all | solution.py:355
  674.6 52.2 %collective-permute-start.57 = (bf16[4,512,768]{2,1,0:T(8,128)(2,1)}, bf16[4,512,768]{2,1,0:T(8,128)(2,1)}, u32[]{:S(2)}, u32[]{:S(2)}) collective-permute-start(bf16[4,512,768]{2,1,0:T(8,128)(2,1)} %all-to-all-done.6.own_ref), channel_id=1, source_target_pairs={{0,4},{1,5},{2,6},{3,7},{4,0},{5,1},{6,2},{7,3},{8,12},{9,13},{10,... | collective-permute-start | bytes 9437192 | tf_op jit(solution)/shard_map/ppermute | solution.py:343
  698.9 46.6 %collective-permute-start.59 = (bf16[4,4,256,384]{3,2,1,0:T(8,128)(2,1)}, bf16[4,4,256,384]{3,2,1,0:T(8,128)(2,1)}, u32[]{:S(2)}, u32[]{:S(2)}) collective-permute-start(bf16[4,4,256,384]{3,2,1,0:T(8,128)(2,1)} %bitcast.148), channel_id=1, source_target_pairs={{0,4},{1,5},{2,6},{3,7},{4,0},{5,1},{6,2},{7,3},{8,12},{9,13},{10,... | collective-permute-start | bytes 9437192 | tf_op jit(solution)/shard_map/ppermute | solution.py:343
  701.5 55.3 %all-to-all-start.7 = ((bf16[4,512,768]{2,1,0:T(8,128)(2,1)}), bf16[4,512,768]{2,1,0:T(8,128)(2,1)}, u32[]{:S(2)}, u32[]{:S(2)}) async-start(bf16[4,512,768]{2,1,0:T(8,128)(2,1)} %bitcast.138), calls=%async_computation.8 | async-start | bytes 6291456 | tf_op jit(solution)/shard_map/all_to_all | solution.py:355
  706.2 58.6 %all-gather.10.cloned.1.call-start = ((), (), s32[]{:S(2)}) async-start(), calls=%async_computation.12 | async-start | bytes 2359296 | tf_op jit(solution)/shard_map/all_gather | solution.py:1305
  (137 other events, 1537.0 us)
Sparse Core Ops, SparseCore 0:
  12.3 130.7 all-gather.5
  284.2 169.8 all-gather.7
  559.0 36.5 reduce-scatter.1
  627.8 65.0 all-gather.11
  708.3 33.4 all-gather.9

commit v5 on v4

--- a/solution.py
+++ b/solution.py
@@ -508,7 +508,7 @@
         in_specs=[smem, smem, vmem, vmem, vmem, vmem],
         out_specs=(vmem,) * 7,
         scratch_shapes=[pltpu.VMEM((2, row_len, 2 * HD), BF), pltpu.VMEM((2, row_len, 2 * HD), BF)],
-        compiler_params=pltpu.CompilerParams(vmem_limit_bytes=26 * 2**20),
+        compiler_params=pltpu.CompilerParams(vmem_limit_bytes=56 * 2**20),
         cost_estimate=SMALL,
         name="attend",
     )(split, where, mixed, *tables)
@@ -656,7 +656,7 @@
         ]
         + [pltpu.VMEM((row_len, 2 * HD), BF)] * 5
         + [pltpu.SemaphoreType.DMA((5,))],
-        compiler_params=pltpu.CompilerParams(vmem_limit_bytes=34 * 2**20),
+        compiler_params=pltpu.CompilerParams(vmem_limit_bytes=56 * 2**20),
         cost_estimate=SMALL,
         name="attend_back",
     )(split, q, k, v, out, d_out, logs, *tables)
@@ -699,13 +699,13 @@
             out_specs=pl.BlockSpec((None, rows, 12 * HD), lambda chip, where: (chip, 0, 0)),
         ),
         out_shape=jax.ShapeDtypeStruct((4, rows, 12 * HD), BF),
-        compiler_params=pltpu.CompilerParams(vmem_limit_bytes=32 * 2**20),
+        compiler_params=pltpu.CompilerParams(vmem_limit_bytes=56 * 2**20),
         cost_estimate=SMALL,
         name="pick_heads",
     )(where, weight, weight, weight)
 
 
-def small_call(kernel, name, out_shape, where, *arrays, flops=0, scratch=(), limit=20):
+def small_call(kernel, name, out_shape, where, *arrays, flops=0, scratch=(), limit=56):
     size = sum(x.size * x.dtype.itemsize for x in arrays)
     vmem = pl.BlockSpec(memory_space=pltpu.VMEM)
     return pl.pallas_call(
@@ -967,7 +967,7 @@
             dma((2, 9)), dma((width // 256, 9)), dma((2, 6, 4)),
         ]
         + ([held] if own else []),
-        compiler_params=pltpu.CompilerParams(vmem_limit_bytes=(38 if own else 32) * 2**20),
+        compiler_params=pltpu.CompilerParams(vmem_limit_bytes=56 * 2**20),
         cost_estimate=SMALL,
         name="hidden",
     )(where, *mids, *outs, *weights, *kept)
@@ -991,7 +991,7 @@
         ],
         out_specs=pl.BlockSpec((step, width), lambda i: (i, 0)),
         out_shape=jax.ShapeDtypeStruct((features, width), BF),
-        compiler_params=pltpu.CompilerParams(vmem_limit_bytes=48 * 2**20),
+        compiler_params=pltpu.CompilerParams(vmem_limit_bytes=56 * 2**20),
         cost_estimate=SMALL,
         name="weight_grad",
     )(left, right)
@@ -1027,7 +1027,7 @@
         ),
         out_shape=jax.ShapeDtypeStruct((rows, 2 * chips * chip_width), F32),
         input_output_aliases={} if before is None else {3: 0},
-        compiler_params=pltpu.CompilerParams(vmem_limit_bytes=32 * 2**20),
+        compiler_params=pltpu.CompilerParams(vmem_limit_bytes=56 * 2**20),
         cost_estimate=SMALL,
         name="place_columns",
     )(core, own, other, *([] if before is None else [before]))
@@ -1284,7 +1284,7 @@
             pltpu.VMEM((8 * tokens, 12 * HD), BF),
             pltpu.VMEM((8 * tokens, 512), F32),
         ],
-        limit=24,
+        limit=56,
     )
     heads = lax.all_gather(jnp.stack(pairs), "z", axis=0)
     gate_parts, d_up_grad, near, far, act_all = tie(

time: 796 us -> 781 us (0.981)
  local copies, waits for them, and re-layouts: 79.1 us -> 37.2 us
  Pallas kernels: 245 us -> 271 us
    unnamed x182 -> x108, local copies, waits for them, and re-layouts: 52 us -> 13.2 us
    pallas_call x4, Pallas kernels: 23.1 us -> 31.3 us  [small_call(): pl.pallas_call(kernel, out_shape=out_shape, in_specs=[pl.BlockSpec(memory...]
  transfers between devices with their start and end apart: 77 -> 77, of which waited for: 35 -> 33; matrix products, arithmetic and copies ran while one was open for 14% -> 14% of each run, Pallas kernels for 30% -> 34%
where the time goes in v5:
time: 781 us; the launch traced here: 767 us
  Pallas kernels  271 us (35%)
  waiting for transfers between devices  265 us (34%)
  starting transfers between devices  92.5 us (12%)
  other arithmetic  50.2 us (6%)
  local copies, waits for them, and re-layouts  37.2 us (5%)
  matrix products  36.9 us (5%)
  between operations  14.9 us (2%)
    ppermute x52, waiting for transfers between devices, swap(): lax.ppermute(value, ('z', 'core', 'fsdp'), [(i, i ^ mask) for i in range(...  117 us
    pallas_call x3, Pallas kernels, hidden_layer(): pl.pallas_call(functools.partial(hidden_kernel, steps=steps, own=own), in...  82.5 us
    all_gather x1, waiting for transfers between devices, plane_plan(): lax.all_gather(normed_in.astype(BF), everywhere, axis=0, tiled=True)  70.5 us
    pallas_call x3, Pallas kernels, weight_grad(): pl.pallas_call(weight_grad_kernel, grid=(features // step,), in_specs=[pl...  59.1 us
    ppermute x52, starting transfers between devices, swap(): lax.ppermute(value, ('z', 'core', 'fsdp'), [(i, i ^ mask) for i in range(...  42.5 us
    ppermute x12, waiting for transfers between devices, shift(): lax.ppermute(value, ('z', 'core', 'fsdp'), [(i, (i + 8 * steps) % 32) for...  39.7 us
    all_to_all x8, waiting for transfers between devices, exchange(): return lax.all_to_all(value, axis, split_axis=0, concat_axis=0, tiled=True)  36.8 us
    all_to_all x8, starting transfers between devices, exchange(): return lax.all_to_all(value, axis, split_axis=0, concat_axis=0, tiled=True)  34.5 us
  transfers between devices with their start and end apart: 77, of which 33 were waited for; matrix products, arithmetic and copies ran while one was open for 14% of the time, Pallas kernels for 34%

profile of v5, /device:TPU:0, one launch (start us, length us, event | category | flops | bytes accessed | tf_op | source)
XLA Modules:
  0.0 767.3 jit_solution(652977709173613141)
XLA Ops:
  19.2 11.0 %collective-permute-done = bf16[128,2048]{1,0:T(8,128)(2,1)S(1)} collective-permute-done((bf16[128,2048]{1,0:T(8,128)(2,1)}, bf16[128,2048]{1,0:T(8,128)(2,1)S(1)}, u32[]{:S(2)}, u32[]{:S(2)}) %collective-permute-start) | collective-permute-done | bytes 524320 | tf_op jit(solution)/shard_map/ppermute | solution.py:343
  72.7 70.5 %all-gather.6.cloned.1.call-done = bf16[4096,2048]{1,0:T(8,128)(2,1)} async-done(((bf16[128,2048]{1,0:T(8,128)(2,1)}), bf16[4096,2048]{1,0:T(8,128)(2,1)}) %all-gather.6.cloned.1.call-update) | async-done | bytes 16777232 | tf_op jit(solution)/shard_map/all_gather | solution.py:1160
  151.8 10.4 %convolution_add_fusion = f32[4096,256]{1,0:T(8,128)} fusion(bf16[4096,2048]{1,0:T(8,128)(2,1)} %all-gather.6.cloned.1.call-done, bf16[2048,256]{1,0:T(8,128)(2,1)S(1)} %bitcast.148, f32[256]{0:T(256)S(1)} %pad_maximum_fusion.4), kind=kOutput, calls=%fused_computation | convolution fusion | flops 4296015872 | bytes 22021120 | tf_op jit(solution)/shard_map/dot_general | solution.py:383
  162.2 23.3 %attend.1 = (bf16[2048,128]{1,0:T(8,128)(2,1)}, bf16[2048,128]{1,0:T(8,128)(2,1)}, bf16[2048,128]{1,0:T(8,128)(2,1)}, bf16[2048,128]{1,0:T(8,128)(2,1)}, f32[2,2...) custom-call(s32[2]{0:T(128)} %fusion.29.split_ref, s32[2]{0:T(128)} %pad_add_fusion.where_ref, ...), custom_call_target="tpu_custom_call" | custom-call | flops 1000 | bytes 1000 | tf_op jit(solution)/shard_map/attend/pallas_call | solution.py:504
  194.2 12.6 %pair.1 = (bf16[256,256]{1,0:T(8,128)(2,1)}, bf16[256,256]{1,0:T(8,128)(2,1)}, bf16[256,256]{1,0:T(8,128)(2,1)}, bf16[256,256]{1,0:T(8,128)(2,1)}) custom-call(s32[2]{0:T(128)} %pad_add_fusion.where_ref, bf16[4,256,128]{2,1,0:T(8,128)(2,1)} %get-tuple-element.143.mine_ref, bf16[4,256,128]{2,1,0:T(8,128)(2,1)} %copy-done.30), custom_call_target="tpu_custom_call" | custom-call | flops 1000 | bytes 1000 | tf_op jit(solution)/shard_map/pair/pallas_call | solution.py:711
  232.4 9.2 %collective-permute-done.12 = bf16[128,2048]{1,0:T(8,128)(2,1)S(1)} collective-permute-done((bf16[128,2048]{1,0:T(8,128)(2,1)}, bf16[128,2048]{1,0:T(8,128)(2,1)S(1)}, u32[]{:S(2)}, u32[]{:S(2)}) %collective-permute-start.12) | collective-permute-done | bytes 524320 | tf_op jit(solution)/shard_map/ppermute | solution.py:343
  241.6 10.5 %collective-permute-done.11 = bf16[128,2048]{1,0:T(8,128)(2,1)S(1)} collective-permute-done((bf16[128,2048]{1,0:T(8,128)(2,1)}, bf16[128,2048]{1,0:T(8,128)(2,1)S(1)}, u32[]{:S(2)}, u32[]{:S(2)}) %collective-permute-start.11) | collective-permute-done | bytes 524320 | tf_op jit(solution)/shard_map/ppermute | solution.py:343
  288.9 28.5 %hidden.3 = (bf16[4096,768]{1,0:T(8,128)(2,1)}, bf16[4096,768]{1,0:T(8,128)(2,1)}, bf16[4096,768]{1,0:T(8,128)(2,1)}, bf16[4096,2048]{1,0:T(8,128)(2,1)}, bf16[4...) custom-call(s32[2]{0:T(128)} %pad_add_fusion.where_ref, ...), custom_call_target="tpu_custom_call" | custom-call | flops 1000 | bytes 1000 | tf_op jit(solution)/shard_map/hidden/pallas_call | solution.py:956
  317.3 8.8 %collective-permute-done.24.refs_6_ = bf16[256,2048]{1,0:T(8,128)(2,1)} collective-permute-done((bf16[256,2048]{1,0:T(8,128)(2,1)}, bf16[256,2048]{1,0:T(8,128)(2,1)}, u32[]{:S(2)}, u32[]{:S(2)}) %collective-permute-start.24) | collective-permute-done | bytes 1048608 | tf_op jit(solution)/shard_map/ppermute | solution.py:347
  343.9 12.4 %collective-permute-done.28 = bf16[128,2048]{1,0:T(8,128)(2,1)S(1)} collective-permute-done((bf16[128,2048]{1,0:T(8,128)(2,1)}, bf16[128,2048]{1,0:T(8,128)(2,1)S(1)}, u32[]{:S(2)}, u32[]{:S(2)}) %collective-permute-start.28) | collective-permute-done | bytes 524320 | tf_op jit(solution)/shard_map/ppermute | solution.py:343
  380.8 22.7 %collective-permute-done.30.p1 = bf16[128,2048]{1,0:T(8,128)(2,1)S(1)} collective-permute-done((bf16[128,2048]{1,0:T(8,128)(2,1)S(1)}, bf16[128,2048]{1,0:T(8,128)(2,1)S(1)}, u32[]{:S(2)}, u32[]{:S(2)}) %collective-permute-start.30) | collective-permute-done | bytes 524320 | tf_op jit(solution)/shard_map/ppermute | solution.py:343
  406.5 11.1 %collective-permute-done.32.p3_low = bf16[64,2048]{1,0:T(8,128)(2,1)S(1)} collective-permute-done((bf16[64,2048]{1,0:T(8,128)(2,1)S(1)}, bf16[64,2048]{1,0:T(8,128)(2,1)S(1)}, u32[]{:S(2)}, u32[]{:S(2)}) %collective-permute-start.32) | collective-permute-done | bytes 262176 | tf_op jit(solution)/shard_map/ppermute | solution.py:343
  433.6 21.0 %all-to-all-done.3 = bf16[8,256,128]{2,1,0:T(8,128)(2,1)S(1)} async-done(((bf16[8,256,128]{2,1,0:T(8,128)(2,1)}), bf16[8,256,128]{2,1,0:T(8,128)(2,1)S(1)}, u32[]{:S(2)}, u32[]{:S(2)}) %all-to-all-start.3) | async-done | bytes 524320 | tf_op jit(solution)/shard_map/all_to_all | solution.py:355
  461.9 30.2 %attend_back.1 = (bf16[32,2,64,256]{3,2,1,0:T(8,128)(2,1)}, bf16[2048,384]{1,0:T(8,128)(2,1)}) custom-call(s32[2]{0:T(128)} %fusion.29.split_ref, bf16[2048,128]{1,0:T(8,128)(2,1)} %get-tuple-element.155.q_hbm, bf16[2048,128]{1,0:T(8,128)(2,1)} %get-tuple-element.156.k_hbm, bf16[2048,128]{1,0:T(8,128)(2,1)} %get-tuple-element.157.v_hbm, ...), custom_call_target="tpu_custom_call" | custom-call | flops 1000 | bytes 1000 | tf_op jit(solution)/shard_map/attend_back/pallas_call | solution.py:642
  498.3 10.9 %fusion.45 = bf16[2048,256]{0,1:T(8,128)(2,1)S(1)} fusion(bf16[4096,2048]{1,0:T(8,128)(2,1)} %all-gather.6.cloned.1.call-done, bf16[4096,256]{1,0:T(8,128)(2,1)} %bitcast.145), kind=kOutput, calls=%fused_computation.160 | convolution fusion | flops 4294967296 | bytes 19922944 | tf_op jit(solution)/shard_map/dot_general | solution.py:391
  517.6 32.6 %hidden.4 = (bf16[4096,768]{1,0:T(8,128)(2,1)}, bf16[4096,768]{1,0:T(8,128)(2,1)}, bf16[4096,768]{1,0:T(8,128)(2,1)}, bf16[4096,2048]{1,0:T(8,128)(2,1)}) custom-call(s32[2]{0:T(128)} %pad_add_fusion.where_ref, ...), custom_call_target="tpu_custom_call", output_to_operand_aliasing={{0}: (13, {}), {1}: (14, {}), {2}: (15, {}), {3}: (16, {})} | custom-call | flops 1000 | bytes 1000 | tf_op jit(solution)/shard_map/hidden/pallas_call | solution.py:956
  574.3 21.4 %hidden.5 = (bf16[4096,768]{1,0:T(8,128)(2,1)}, bf16[4096,768]{1,0:T(8,128)(2,1)}, bf16[4096,768]{1,0:T(8,128)(2,1)}, bf16[4096,2048]{1,0:T(8,128)(2,1)}) custom-call(s32[2]{0:T(128)} %pad_add_fusion.where_ref, ...), custom_call_target="tpu_custom_call", output_to_operand_aliasing={{0}: (9, {}), {1}: (10, {}), {2}: (11, {}), {3}: (12, {})} | custom-call | flops 1000 | bytes 1000 | tf_op jit(solution)/shard_map/hidden/pallas_call | solution.py:956
  595.8 19.0 %weight_grad.3 = bf16[2048,768]{1,0:T(8,128)(2,1)} custom-call(bf16[4096,2048]{1,0:T(8,128)(2,1)} %all-gather.8.cloned.1.call-done.refs_0_.left_ref, bf16[4096,768]{1,0:T(8,128)(2,1)} %get-tuple-element.212.right_ref), custom_call_target="tpu_custom_call" | custom-call | flops 1000 | bytes 1000 | tf_op jit(solution)/shard_map/weight_grad/pallas_call | solution.py:985
  622.0 9.2 %d_in.1 = (bf16[4,128,2048]{2,1,0:T(8,128)(2,1)}, bf16[4,128,2048]{2,1,0:T(8,128)(2,1)}) custom-call(s32[2]{0:T(128)} %pad_add_fusion.where_ref, bf16[4,512,384]{2,1,0:T(8,128)(2,1)} %all-to-all-done.4.in_ref, bf16[2048,768]{1,0:T(8,128)(2,1)} %bitcast.35.weight_ref), custom_call_target="tpu_custom_call" | custom-call | flops 1000 | bytes 1000 | tf_op jit(solution)/shard_map/d_in/pallas_call | solution.py:711
  631.2 19.0 %weight_grad.4 = bf16[2048,768]{1,0:T(8,128)(2,1)} custom-call(bf16[4096,2048]{1,0:T(8,128)(2,1)} %all-gather.8.cloned.1.call-done.refs_0_.left_ref, bf16[4096,768]{1,0:T(8,128)(2,1)} %get-tuple-element.220.right_ref), custom_call_target="tpu_custom_call" | custom-call | flops 1000 | bytes 1000 | tf_op jit(solution)/shard_map/weight_grad/pallas_call | solution.py:985
  664.4 21.0 %weight_grad.5.own_ref = bf16[768,2048]{1,0:T(8,128)(2,1)} custom-call(bf16[4096,768]{1,0:T(8,128)(2,1)} %get-tuple-element.228.left_ref, bf16[4096,2048]{1,0:T(8,128)(2,1)} %get-tuple-element.229.right_ref), custom_call_target="tpu_custom_call" | custom-call | flops 1000 | bytes 1000 | tf_op jit(solution)/shard_map/weight_grad/pallas_call | solution.py:985
  709.0 8.7 %place_columns.2.rest_0_ = f32[512,11264]{1,0:T(8,128)} custom-call(s32[1]{0:T(128)} %bitcast.47.where_ref.core_ref, bf16[4,512,768]{2,1,0:T(8,128)(2,1)} %all-to-all-done.6.own_ref, bf16[4,512,768]{2,1,0:T(8,128)(2,1)} %collective-permute-done.57.other_ref), custom_call_target="tpu_custom_call" | custom-call | flops 1000 | bytes 1000 | tf_op jit(solution)/shard_map/place_columns/pallas_call | solution.py:1020
  717.7 10.1 %place_down.1 = f32[1408,2048]{1,0:T(8,128)} custom-call(s32[1]{0:T(128)} %bitcast.47.where_ref.core_ref, bf16[768,2048]{1,0:T(8,128)(2,1)} %weight_grad.5.own_ref, bf16[768,2048]{1,0:T(8,128)(2,1)} %collective-permute-done.58.other_ref), custom_call_target="tpu_custom_call" | custom-call | flops 1000 | bytes 1000 | tf_op jit(solution)/shard_map/place_down/pallas_call | solution.py:1062
  727.7 11.3 %place_qkv.1 = f32[512,6144]{1,0:T(8,128)} custom-call(s32[2]{0:T(128)} %pad_add_fusion.1.where_ref, bf16[4,4,256,384]{3,2,1,0:T(8,128)(2,1)} %bitcast.143, bf16[4,4,256,384]{3,2,1,0:T(8,128)(2,1)} %collective-permute-done.59.other_ref), custom_call_target="tpu_custom_call" | custom-call | flops 1000 | bytes 1000 | tf_op jit(solution)/shard_map/place_qkv/pallas_call | solution.py:1089
  (343 shorter events, 307.2 us)
Async XLA Ops:
  7.2 136.0 %all-gather.6.cloned.1.call-start = ((), (), s32[]{:S(2)}) async-start(), calls=%async_computation.9 | async-start | bytes 17301504 | tf_op jit(solution)/shard_map/all_gather | solution.py:1160
  143.1 42.3 %all-to-all-start.1 = ((bf16[4,512,768]{2,1,0:T(8,128)(2,1)}), bf16[4,512,768]{2,1,0:T(8,128)(2,1)S(1)}, u32[]{:S(2)}, u32[]{:S(2)}) async-start(bf16[4,512,768]{2,1,0:T(8,128)(2,1)} %get-tuple-element.140), calls=%async_computation.1 | async-start | bytes 6291456 | tf_op jit(solution)/shard_map/all_to_all | solution.py:355
  187.1 70.0 %all-to-all-start.2 = ((bf16[4,512,768]{2,1,0:T(8,128)(2,1)}), bf16[4,512,768]{2,1,0:T(8,128)(2,1)}, u32[]{:S(2)}, u32[]{:S(2)}) async-start(bf16[4,512,768]{2,1,0:T(8,128)(2,1)} %get-tuple-element.153), calls=%async_computation.2 | async-start | bytes 6291456 | tf_op jit(solution)/shard_map/all_to_all | solution.py:355
  191.8 300.4 %all-gather.8.cloned.1.call-start = ((), (), s32[]{:S(2)}) async-start(), calls=%async_computation.10 | async-start | bytes 17301504 | tf_op jit(solution)/shard_map/all_gather | solution.py:1203
  232.4 45.6 %collective-permute-start.23 = (bf16[256,2048]{1,0:T(8,128)(2,1)}, bf16[256,2048]{1,0:T(8,128)(2,1)}, u32[]{:S(2)}, u32[]{:S(2)}) collective-permute-start(bf16[256,2048]{1,0:T(8,128)(2,1)} %collective-permute-done.5.refs_1_), channel_id=1, source_target_pairs={{0,8},{1,9},{2,10},{3,11},{4,12},{5,13},{6,14},{7,15},{8,16},{9,17... | collective-permute-start | bytes 3145736 | tf_op jit(solution)/shard_map/ppermute | solution.py:347
  287.2 39.0 %collective-permute-start.24 = (bf16[256,2048]{1,0:T(8,128)(2,1)}, bf16[256,2048]{1,0:T(8,128)(2,1)}, u32[]{:S(2)}, u32[]{:S(2)}) collective-permute-start(bf16[256,2048]{1,0:T(8,128)(2,1)} %collective-permute-done.13.refs_2_), channel_id=1, source_target_pairs={{0,8},{1,9},{2,10},{3,11},{4,12},{5,13},{6,14},{7,15},{8,16},{9,17... | collective-permute-start | bytes 3145736 | tf_op jit(solution)/shard_map/ppermute | solution.py:347
  338.3 37.7 %collective-permute-start.29 = (bf16[256,2048]{1,0:T(8,128)(2,1)}, bf16[256,2048]{1,0:T(8,128)(2,1)S(1)}, u32[]{:S(2)}, u32[]{:S(2)}) collective-permute-start(bf16[256,2048]{1,0:T(8,128)(2,1)} %collective-permute-done.23.refs_5_), channel_id=1, source_target_pairs={{0,8},{1,9},{2,10},{3,11},{4,12},{5,13},{6,14},{7,15},{8,16},{9,17... | collective-permute-start | bytes 3145736 | tf_op jit(solution)/shard_map/ppermute | solution.py:347
  343.9 110.8 %collective-permute-start.35 = (bf16[4,128,2048]{2,1,0:T(8,128)(2,1)}, bf16[4,128,2048]{2,1,0:T(8,128)(2,1)}, u32[]{:S(2)}, u32[]{:S(2)}) collective-permute-start(bf16[4,128,2048]{2,1,0:T(8,128)(2,1)} %bitcast.26), channel_id=1, source_target_pairs={{0,4},{1,5},{2,6},{3,7},{4,0},{5,1},{6,2},{7,3},{8,12},{9,13},{10,... | collective-permute-start | bytes 6291464 | tf_op jit(solution)/shard_map/ppermute | solution.py:343
  454.7 37.5 %collective-permute-start.34 = (bf16[256,2048]{1,0:T(8,128)(2,1)}, bf16[256,2048]{1,0:T(8,128)(2,1)}, u32[]{:S(2)}, u32[]{:S(2)}) collective-permute-start(bf16[256,2048]{1,0:T(8,128)(2,1)} %collective-permute-done.24.refs_6_), channel_id=1, source_target_pairs={{0,8},{1,9},{2,10},{3,11},{4,12},{5,13},{6,14},{7,15},{8,16},{9,17... | collective-permute-start | bytes 3145736 | tf_op jit(solution)/shard_map/ppermute | solution.py:347
  458.9 38.2 %collective-permute-start.38 = (bf16[128,2048]{1,0:T(8,128)(2,1)}, bf16[128,2048]{1,0:T(8,128)(2,1)S(1)}, u32[]{:S(2)}, u32[]{:S(2)}) collective-permute-start(bf16[128,2048]{1,0:T(8,128)(2,1)} %get-tuple-element.265), channel_id=1, source_target_pairs={{0,3},{1,2},{2,1},{3,0},{4,7},{5,6},{6,5},{7,4},{8,11},{9,10},{10,... | collective-permute-start | bytes 1572872 | tf_op jit(solution)/shard_map/ppermute | solution.py:343
  461.4 56.2 %collective-permute-start.40 = (bf16[256,2048]{1,0:T(8,128)(2,1)}, bf16[256,2048]{1,0:T(8,128)(2,1)}, u32[]{:S(2)}, u32[]{:S(2)}) collective-permute-start(bf16[256,2048]{1,0:T(8,128)(2,1)} %collective-permute-done.5.refs_1_), channel_id=1, source_target_pairs={{0,4},{1,5},{2,6},{3,7},{4,0},{5,1},{6,2},{7,3},{8,12},{9,13},{10,... | collective-permute-start | bytes 3145736 | tf_op jit(solution)/shard_map/ppermute | solution.py:343
  461.4 56.2 %collective-permute-start.41 = (bf16[256,2048]{1,0:T(8,128)(2,1)}, bf16[256,2048]{1,0:T(8,128)(2,1)}, u32[]{:S(2)}, u32[]{:S(2)}) collective-permute-start(bf16[256,2048]{1,0:T(8,128)(2,1)} %collective-permute-done.13.refs_2_), channel_id=1, source_target_pairs={{0,4},{1,5},{2,6},{3,7},{4,0},{5,1},{6,2},{7,3},{8,12},{9,13},{10,... | collective-permute-start | bytes 3145736 | tf_op jit(solution)/shard_map/ppermute | solution.py:343
  492.2 62.2 %all-to-all-start.4 = ((bf16[4,512,384]{2,1,0:T(8,128)(2,1)}), bf16[4,512,384]{2,1,0:T(8,128)(2,1)}, u32[]{:S(2)}, u32[]{:S(2)}) async-start(bf16[4,512,384]{2,1,0:T(8,128)(2,1)} %bitcast.146), calls=%async_computation.4 | async-start | bytes 3145728 | tf_op jit(solution)/shard_map/all_to_all | solution.py:355
  496.9 118.1 %reduce-scatter.2.cloned.1.call-start = ((), (), s32[]{:S(2)}) async-start(), calls=%async_computation.11 | async-start | bytes 2359296 | tf_op jit(solution)/shard_map/reduce_scatter | solution.py:1269
  558.8 56.2 %all-to-all-start.5 = ((bf16[4,512,768]{2,1,0:T(8,128)(2,1)}), bf16[4,512,768]{2,1,0:T(8,128)(2,1)}, u32[]{:S(2)}, u32[]{:S(2)}) async-start(bf16[4,512,768]{2,1,0:T(8,128)(2,1)} %pick_heads.1), calls=%async_computation.5 | async-start | bytes 6291456 | tf_op jit(solution)/shard_map/all_to_all | solution.py:355
  563.6 124.1 %all-gather.12.cloned.1.call-start = ((), (), s32[]{:S(2)}) async-start(), calls=%async_computation.13 | async-start | bytes 3932160 | tf_op jit(solution)/shard_map/all_gather | solution.py:1289
  568.3 46.7 %collective-permute-start.46 = (bf16[256,384]{1,0:T(8,128)(2,1)}, bf16[256,384]{1,0:T(8,128)(2,1)}, u32[]{:S(2)}, u32[]{:S(2)}) collective-permute-start(bf16[256,384]{1,0:T(8,128)(2,1)} %bitcast.152), channel_id=1, source_target_pairs={{0,1},{1,0},{2,3},{3,2},{4,5},{5,4},{6,7},{7,6},{8,9},{9,8},{10,11... | collective-permute-start | bytes 589832 | tf_op jit(solution)/shard_map/ppermute | solution.py:343
  571.6 43.3 %collective-permute-start.47 = (bf16[256,384]{1,0:T(8,128)(2,1)}, bf16[256,384]{1,0:T(8,128)(2,1)}, u32[]{:S(2)}, u32[]{:S(2)}) collective-permute-start(bf16[256,384]{1,0:T(8,128)(2,1)} %bitcast.153), channel_id=1, source_target_pairs={{0,2},{1,3},{2,0},{3,1},{4,6},{5,7},{6,4},{7,5},{8,10},{9,11},{10,... | collective-permute-start | bytes 589832 | tf_op jit(solution)/shard_map/ppermute | solution.py:343
  573.9 41.1 %collective-permute-start.48 = (bf16[256,384]{1,0:T(8,128)(2,1)}, bf16[256,384]{1,0:T(8,128)(2,1)S(1)}, u32[]{:S(2)}, u32[]{:S(2)}) collective-permute-start(bf16[256,384]{1,0:T(8,128)(2,1)} %bitcast.154), channel_id=1, source_target_pairs={{0,3},{1,2},{2,1},{3,0},{4,7},{5,6},{6,5},{7,4},{8,11},{9,10},{10,... | collective-permute-start | bytes 589832 | tf_op jit(solution)/shard_map/ppermute | solution.py:343
  617.1 41.3 %all-to-all-start.6 = ((bf16[4,512,768]{2,1,0:T(8,128)(2,1)}), bf16[4,512,768]{2,1,0:T(8,128)(2,1)}, u32[]{:S(2)}, u32[]{:S(2)}) async-start(bf16[4,512,768]{2,1,0:T(8,128)(2,1)} %bitcast.137), calls=%async_computation.7 | async-start | bytes 6291456 | tf_op jit(solution)/shard_map/all_to_all | solution.py:355
  664.4 44.6 %collective-permute-start.57 = (bf16[4,512,768]{2,1,0:T(8,128)(2,1)}, bf16[4,512,768]{2,1,0:T(8,128)(2,1)}, u32[]{:S(2)}, u32[]{:S(2)}) collective-permute-start(bf16[4,512,768]{2,1,0:T(8,128)(2,1)} %all-to-all-done.6.own_ref), channel_id=1, source_target_pairs={{0,4},{1,5},{2,6},{3,7},{4,0},{5,1},{6,2},{7,3},{8,12},{9,13},{10,... | collective-permute-start | bytes 9437192 | tf_op jit(solution)/shard_map/ppermute | solution.py:343
  687.7 40.0 %collective-permute-start.59 = (bf16[4,4,256,384]{3,2,1,0:T(8,128)(2,1)}, bf16[4,4,256,384]{3,2,1,0:T(8,128)(2,1)}, u32[]{:S(2)}, u32[]{:S(2)}) collective-permute-start(bf16[4,4,256,384]{3,2,1,0:T(8,128)(2,1)} %bitcast.142), channel_id=1, source_target_pairs={{0,4},{1,5},{2,6},{3,7},{4,0},{5,1},{6,2},{7,3},{8,12},{9,13},{10,... | collective-permute-start | bytes 9437192 | tf_op jit(solution)/shard_map/ppermute | solution.py:343
  690.4 48.7 %all-to-all-start.7 = ((bf16[4,512,768]{2,1,0:T(8,128)(2,1)}), bf16[4,512,768]{2,1,0:T(8,128)(2,1)}, u32[]{:S(2)}, u32[]{:S(2)}) async-start(bf16[4,512,768]{2,1,0:T(8,128)(2,1)} %bitcast.136), calls=%async_computation.8 | async-start | bytes 6291456 | tf_op jit(solution)/shard_map/all_to_all | solution.py:355
  695.1 51.5 %all-gather.10.cloned.1.call-start = ((), (), s32[]{:S(2)}) async-start(), calls=%async_computation.12 | async-start | bytes 2359296 | tf_op jit(solution)/shard_map/all_gather | solution.py:1305
  (100 other events, 1369.8 us)
Sparse Core Ops, SparseCore 0:
  12.3 130.7 all-gather.5
  287.3 170.6 all-gather.7
  558.9 36.3 reduce-scatter.1
  617.2 65.2 all-gather.11
  697.2 30.8 all-gather.9

commit v6 on v3

--- a/solution.py
+++ b/solution.py
@@ -967,7 +967,7 @@
             dma((2, 9)), dma((width // 256, 9)), dma((2, 6, 4)),
         ]
         + ([held] if own else []),
-        compiler_params=pltpu.CompilerParams(vmem_limit_bytes=48 * 2**20),
+        compiler_params=pltpu.CompilerParams(vmem_limit_bytes=(38 if own else 32) * 2**20),
         cost_estimate=SMALL,
         name="hidden",
     )(where, *mids, *outs, *weights, *kept)

time: 779 us -> 796 us (1.022)
  local copies, waits for them, and re-layouts: 58.8 us -> 76.7 us
  waiting for transfers between devices: 265 us -> 275 us
    ppermute x52, waiting for transfers between devices: 129 us -> 139 us  [swap(): lax.ppermute(value, ('z', 'core', 'fsdp'), [(i, i ^ mask) for i in range(...]
    unnamed x130 -> x178, local copies, waits for them, and re-layouts: 39.4 us -> 49.5 us
  transfers between devices with their start and end apart: 77 -> 77, of which waited for: 32 -> 33; matrix products, arithmetic and copies ran while one was open for 13% -> 14% of each run, Pallas kernels for 31% -> 29%
where the time goes in v6:
time: 796 us; the launch traced here: 789 us
  waiting for transfers between devices  275 us (35%)
  Pallas kernels  238 us (30%)
  starting transfers between devices  92.1 us (12%)
  local copies, waits for them, and re-layouts  76.7 us (10%)
  other arithmetic  53 us (7%)
  matrix products  39.2 us (5%)
  between operations  15.2 us (2%)
    ppermute x52, waiting for transfers between devices, swap(): lax.ppermute(value, ('z', 'core', 'fsdp'), [(i, i ^ mask) for i in range(...  139 us
    pallas_call x3, Pallas kernels, hidden_layer(): pl.pallas_call(functools.partial(hidden_kernel, steps=steps, own=own), in...  79.1 us
    all_gather x1, waiting for transfers between devices, plane_plan(): lax.all_gather(normed_in.astype(BF), everywhere, axis=0, tiled=True)  70.2 us
    pallas_call x3, Pallas kernels, weight_grad(): pl.pallas_call(weight_grad_kernel, grid=(features // step,), in_specs=[pl...  57.5 us
    unnamed x178, local copies, waits for them, and re-layouts  49.5 us
    ppermute x52, starting transfers between devices, swap(): lax.ppermute(value, ('z', 'core', 'fsdp'), [(i, i ^ mask) for i in range(...  40.6 us
    all_to_all x8, waiting for transfers between devices, exchange(): return lax.all_to_all(value, axis, split_axis=0, concat_axis=0, tiled=True)  37.4 us
    all_to_all x8, starting transfers between devices, exchange(): return lax.all_to_all(value, axis, split_axis=0, concat_axis=0, tiled=True)  35.6 us
  transfers between devices with their start and end apart: 77, of which 33 were waited for; matrix products, arithmetic and copies ran while one was open for 14% of the time, Pallas kernels for 29%

profile of v6, /device:TPU:0, one launch (start us, length us, event | category | flops | bytes accessed | tf_op | source)
XLA Modules:
  0.0 788.9 jit_solution(10655349455677304405)
XLA Ops:
  19.2 11.0 %collective-permute-done = bf16[128,2048]{1,0:T(8,128)(2,1)S(1)} collective-permute-done((bf16[128,2048]{1,0:T(8,128)(2,1)}, bf16[128,2048]{1,0:T(8,128)(2,1)S(1)}, u32[]{:S(2)}, u32[]{:S(2)}) %collective-permute-start) | collective-permute-done | bytes 524320 | tf_op jit(solution)/shard_map/ppermute | solution.py:343
  73.0 70.2 %all-gather.6.cloned.1.call-done = bf16[4096,2048]{1,0:T(8,128)(2,1)} async-done(((bf16[128,2048]{1,0:T(8,128)(2,1)}), bf16[4096,2048]{1,0:T(8,128)(2,1)}) %all-gather.6.cloned.1.call-update) | async-done | bytes 16777232 | tf_op jit(solution)/shard_map/all_gather | solution.py:1160
  151.6 12.6 %convolution_add_fusion = f32[4096,256]{1,0:T(8,128)} fusion(bf16[4096,2048]{1,0:T(8,128)(2,1)} %all-gather.6.cloned.1.call-done, bf16[2048,256]{1,0:T(8,128)(2,1)} %bitcast.16, f32[256]{0:T(256)S(1)} %pad_maximum_fusion.4), kind=kOutput, calls=%fused_computation | convolution fusion | flops 4296015872 | bytes 22021120 | tf_op jit(solution)/shard_map/dot_general | solution.py:383
  164.3 21.3 %attend.1 = (bf16[2048,128]{1,0:T(8,128)(2,1)S(1)}, bf16[2048,128]{1,0:T(8,128)(2,1)S(1)}, bf16[2048,128]{1,0:T(8,128)(2,1)S(1)}, bf16[2048,128]{1,0:T(8,128)(2,...) custom-call(s32[2]{0:T(128)S(1)} %fusion.29.split_ref, ...), custom_call_target="tpu_custom_call" | custom-call | flops 1000 | bytes 1000 | tf_op jit(solution)/shard_map/attend/pallas_call | solution.py:504
  222.4 23.1 %collective-permute-done.12 = bf16[128,2048]{1,0:T(8,128)(2,1)S(1)} collective-permute-done((bf16[128,2048]{1,0:T(8,128)(2,1)S(1)}, bf16[128,2048]{1,0:T(8,128)(2,1)S(1)}, u32[]{:S(2)}, u32[]{:S(2)}) %collective-permute-start.12) | collective-permute-done | bytes 524320 | tf_op jit(solution)/shard_map/ppermute | solution.py:343
  245.5 9.5 %collective-permute-done.11 = bf16[128,2048]{1,0:T(8,128)(2,1)S(1)} collective-permute-done((bf16[128,2048]{1,0:T(8,128)(2,1)S(1)}, bf16[128,2048]{1,0:T(8,128)(2,1)S(1)}, u32[]{:S(2)}, u32[]{:S(2)}) %collective-permute-start.11) | collective-permute-done | bytes 524320 | tf_op jit(solution)/shard_map/ppermute | solution.py:343
  261.1 11.6 %collective-permute-done.14.refs_1_ = bf16[128,2048]{1,0:T(8,128)(2,1)S(1)} collective-permute-done((bf16[128,2048]{1,0:T(8,128)(2,1)S(1)}, bf16[128,2048]{1,0:T(8,128)(2,1)S(1)}, u32[]{:S(2)}, u32[]{:S(2)}) %collective-permute-start.14) | collective-permute-done | bytes 524320 | tf_op jit(solution)/shard_map/ppermute | solution.py:343
  297.4 27.3 %hidden.3 = (bf16[4096,768]{1,0:T(8,128)(2,1)}, bf16[4096,768]{1,0:T(8,128)(2,1)}, bf16[4096,768]{1,0:T(8,128)(2,1)}, bf16[4096,2048]{1,0:T(8,128)(2,1)}, bf16[4...) custom-call(s32[2]{0:T(128)S(1)} %pad_add_fusion.where_ref, ...), custom_call_target="tpu_custom_call" | custom-call | flops 1000 | bytes 1000 | tf_op jit(solution)/shard_map/hidden/pallas_call | solution.py:956
  341.6 16.2 %collective-permute-done.28 = bf16[128,2048]{1,0:T(8,128)(2,1)S(1)} collective-permute-done((bf16[128,2048]{1,0:T(8,128)(2,1)}, bf16[128,2048]{1,0:T(8,128)(2,1)S(1)}, u32[]{:S(2)}, u32[]{:S(2)}) %collective-permute-start.28) | collective-permute-done | bytes 524320 | tf_op jit(solution)/shard_map/ppermute | solution.py:343
  381.3 21.6 %collective-permute-done.30.p1 = bf16[128,2048]{1,0:T(8,128)(2,1)S(1)} collective-permute-done((bf16[128,2048]{1,0:T(8,128)(2,1)S(1)}, bf16[128,2048]{1,0:T(8,128)(2,1)S(1)}, u32[]{:S(2)}, u32[]{:S(2)}) %collective-permute-start.30) | collective-permute-done | bytes 524320 | tf_op jit(solution)/shard_map/ppermute | solution.py:343
  406.3 10.6 %collective-permute-done.32.p3_low = bf16[64,2048]{1,0:T(8,128)(2,1)S(1)} collective-permute-done((bf16[64,2048]{1,0:T(8,128)(2,1)S(1)}, bf16[64,2048]{1,0:T(8,128)(2,1)S(1)}, u32[]{:S(2)}, u32[]{:S(2)}) %collective-permute-start.32) | collective-permute-done | bytes 262176 | tf_op jit(solution)/shard_map/ppermute | solution.py:343
  432.4 22.3 %all-to-all-done.3 = bf16[8,256,128]{2,1,0:T(8,128)(2,1)S(1)} async-done(((bf16[8,256,128]{2,1,0:T(8,128)(2,1)}), bf16[8,256,128]{2,1,0:T(8,128)(2,1)S(1)}, u32[]{:S(2)}, u32[]{:S(2)}) %all-to-all-start.3) | async-done | bytes 524320 | tf_op jit(solution)/shard_map/all_to_all | solution.py:355
  467.5 27.2 %attend_back.1 = (bf16[32,2,64,256]{3,2,1,0:T(8,128)(2,1)}, bf16[2048,384]{1,0:T(8,128)(2,1)}) custom-call(s32[2]{0:T(128)S(1)} %fusion.29.split_ref, bf16[2048,128]{1,0:T(8,128)(2,1)S(1)} %copy-done.34, bf16[2048,128]{1,0:T(8,128)(2,1)S(1)} %copy-done.36, bf16[2048,128]{1,0:T(8,128)(2,1)S(1)} %copy-done.38, bf16[2048,128]{1,0:T(8,128)(2,1)S(1)} %copy-done.40, ...), custom_call_target="tpu_custom_call" | custom-call | flops 1000 | bytes 1000 | tf_op jit(solution)/shard_map/attend_back/pallas_call | solution.py:642
  501.6 10.9 %fusion.45 = bf16[2048,256]{0,1:T(8,128)(2,1)S(1)} fusion(bf16[4096,2048]{1,0:T(8,128)(2,1)} %all-gather.6.cloned.1.call-done, bf16[4096,256]{1,0:T(8,128)(2,1)} %bitcast.148), kind=kOutput, calls=%fused_computation.160 | convolution fusion | flops 4294967296 | bytes 19922944 | tf_op jit(solution)/shard_map/dot_general | solution.py:391
  523.4 30.8 %hidden.4 = (bf16[4096,768]{1,0:T(8,128)(2,1)}, bf16[4096,768]{1,0:T(8,128)(2,1)}, bf16[4096,768]{1,0:T(8,128)(2,1)}, bf16[4096,2048]{1,0:T(8,128)(2,1)}) custom-call(s32[2]{0:T(128)S(1)} %pad_add_fusion.where_ref, ...), custom_call_target="tpu_custom_call", output_to_operand_aliasing={{0}: (13, {}), {1}: (14, {}), {2}: (15, {}), {3}: (16, {})} | custom-call | flops 1000 | bytes 1000 | tf_op jit(solution)/shard_map/hidden/pallas_call | solution.py:956
  586.5 21.0 %hidden.5 = (bf16[4096,768]{1,0:T(8,128)(2,1)S(1)}, bf16[4096,768]{1,0:T(8,128)(2,1)}, bf16[4096,768]{1,0:T(8,128)(2,1)}, bf16[4096,2048]{1,0:T(8,128)(2,1)}) custom-call(s32[2]{0:T(128)S(1)} %pad_add_fusion.where_ref, ...), custom_call_target="tpu_custom_call", output_to_operand_aliasing={{0}: (9, {}), {1}: (10, {}), {2}: (11, {}), {3}: (12, {})} | custom-call | flops 1000 | bytes 1000 | tf_op jit(solution)/shard_map/hidden/pallas_call | solution.py:956
  610.2 19.0 %weight_grad.3 = bf16[2048,768]{1,0:T(8,128)(2,1)} custom-call(bf16[4096,2048]{1,0:T(8,128)(2,1)} %all-gather.8.cloned.1.call-done.refs_0_.left_ref, bf16[4096,768]{1,0:T(8,128)(2,1)} %get-tuple-element.212.right_ref), custom_call_target="tpu_custom_call" | custom-call | flops 1000 | bytes 1000 | tf_op jit(solution)/shard_map/weight_grad/pallas_call | solution.py:985
  644.8 18.4 %weight_grad.4 = bf16[2048,768]{1,0:T(8,128)(2,1)S(1)} custom-call(bf16[4096,2048]{1,0:T(8,128)(2,1)} %all-gather.8.cloned.1.call-done.refs_0_.left_ref, bf16[4096,768]{1,0:T(8,128)(2,1)} %get-tuple-element.220.right_ref), custom_call_target="tpu_custom_call" | custom-call | flops 1000 | bytes 1000 | tf_op jit(solution)/shard_map/weight_grad/pallas_call | solution.py:985
  664.9 8.3 %all-to-all-done.6.own_ref = bf16[4,512,768]{2,1,0:T(8,128)(2,1)} async-done(((bf16[4,512,768]{2,1,0:T(8,128)(2,1)}), bf16[4,512,768]{2,1,0:T(8,128)(2,1)}, u32[]{:S(2)}, u32[]{:S(2)}) %all-to-all-start.6) | async-done | bytes 3145760 | tf_op jit(solution)/shard_map/all_to_all | solution.py:355
  678.7 20.1 %weight_grad.5.own_ref = bf16[768,2048]{1,0:T(8,128)(2,1)S(1)} custom-call(bf16[4096,768]{1,0:T(8,128)(2,1)} %copy-done.2, bf16[4096,2048]{1,0:T(8,128)(2,1)} %get-tuple-element.229.right_ref), custom_call_target="tpu_custom_call" | custom-call | flops 1000 | bytes 1000 | tf_op jit(solution)/shard_map/weight_grad/pallas_call | solution.py:985
  730.9 8.7 %place_columns.2.rest_0_ = f32[512,11264]{1,0:T(8,128)} custom-call(s32[1]{0:T(128)} %bitcast.47.where_ref.core_ref, bf16[4,512,768]{2,1,0:T(8,128)(2,1)} %all-to-all-done.6.own_ref, bf16[4,512,768]{2,1,0:T(8,128)(2,1)} %collective-permute-done.57.other_ref), custom_call_target="tpu_custom_call" | custom-call | flops 1000 | bytes 1000 | tf_op jit(solution)/shard_map/place_columns/pallas_call | solution.py:1020
  739.5 10.0 %place_down.1 = f32[1408,2048]{1,0:T(8,128)} custom-call(s32[1]{0:T(128)} %bitcast.47.where_ref.core_ref, bf16[768,2048]{1,0:T(8,128)(2,1)} %copy-done.7, bf16[768,2048]{1,0:T(8,128)(2,1)} %collective-permute-done.58.other_ref), custom_call_target="tpu_custom_call" | custom-call | flops 1000 | bytes 1000 | tf_op jit(solution)/shard_map/place_down/pallas_call | solution.py:1062
  749.5 11.3 %place_qkv.1 = f32[512,6144]{1,0:T(8,128)} custom-call(s32[2]{0:T(128)} %pad_add_fusion.1.where_ref, bf16[4,4,256,384]{3,2,1,0:T(8,128)(2,1)} %bitcast.147, bf16[4,4,256,384]{3,2,1,0:T(8,128)(2,1)} %collective-permute-done.59.other_ref), custom_call_target="tpu_custom_call" | custom-call | flops 1000 | bytes 1000 | tf_op jit(solution)/shard_map/place_qkv/pallas_call | solution.py:1089
  774.3 7.6 place_columns.3
  (414 shorter events, 323.2 us)
Async XLA Ops:
  7.2 136.0 %all-gather.6.cloned.1.call-start = ((), (), s32[]{:S(2)}) async-start(), calls=%async_computation.9 | async-start | bytes 17301504 | tf_op jit(solution)/shard_map/all_gather | solution.py:1160
  143.1 46.4 %all-to-all-start.1 = ((bf16[4,512,768]{2,1,0:T(8,128)(2,1)}), bf16[4,512,768]{2,1,0:T(8,128)(2,1)S(1)}, u32[]{:S(2)}, u32[]{:S(2)}) async-start(bf16[4,512,768]{2,1,0:T(8,128)(2,1)} %get-tuple-element.140), calls=%async_computation.1 | async-start | bytes 6291456 | tf_op jit(solution)/shard_map/all_to_all | solution.py:355
  191.2 65.1 %all-to-all-start.2 = ((bf16[4,512,768]{2,1,0:T(8,128)(2,1)}), bf16[4,512,768]{2,1,0:T(8,128)(2,1)}, u32[]{:S(2)}, u32[]{:S(2)}) async-start(bf16[4,512,768]{2,1,0:T(8,128)(2,1)} %get-tuple-element.153), calls=%async_computation.2 | async-start | bytes 6291456 | tf_op jit(solution)/shard_map/all_to_all | solution.py:355
  195.9 299.0 %all-gather.8.cloned.1.call-start = ((), (), s32[]{:S(2)}) async-start(), calls=%async_computation.10 | async-start | bytes 17301504 | tf_op jit(solution)/shard_map/all_gather | solution.py:1203
  222.4 52.2 %collective-permute-start.23 = (bf16[256,2048]{1,0:T(8,128)(2,1)}, bf16[256,2048]{1,0:T(8,128)(2,1)}, u32[]{:S(2)}, u32[]{:S(2)}) collective-permute-start(bf16[256,2048]{1,0:T(8,128)(2,1)} %collective-permute-done.5.refs_1_), channel_id=1, source_target_pairs={{0,8},{1,9},{2,10},{3,11},{4,12},{5,13},{6,14},{7,15},{8,16},{9,17... | collective-permute-start | bytes 3145736 | tf_op jit(solution)/shard_map/ppermute | solution.py:347
  287.6 39.2 %collective-permute-start.24 = (bf16[256,2048]{1,0:T(8,128)(2,1)}, bf16[256,2048]{1,0:T(8,128)(2,1)}, u32[]{:S(2)}, u32[]{:S(2)}) collective-permute-start(bf16[256,2048]{1,0:T(8,128)(2,1)} %collective-permute-done.13.refs_2_), channel_id=1, source_target_pairs={{0,8},{1,9},{2,10},{3,11},{4,12},{5,13},{6,14},{7,15},{8,16},{9,17... | collective-permute-start | bytes 3145736 | tf_op jit(solution)/shard_map/ppermute | solution.py:347
  336.1 41.1 %collective-permute-start.29 = (bf16[256,2048]{1,0:T(8,128)(2,1)}, bf16[256,2048]{1,0:T(8,128)(2,1)S(1)}, u32[]{:S(2)}, u32[]{:S(2)}) collective-permute-start(bf16[256,2048]{1,0:T(8,128)(2,1)} %collective-permute-done.23.refs_5_), channel_id=1, source_target_pairs={{0,8},{1,9},{2,10},{3,11},{4,12},{5,13},{6,14},{7,15},{8,16},{9,17... | collective-permute-start | bytes 3145736 | tf_op jit(solution)/shard_map/ppermute | solution.py:347
  341.6 114.0 %collective-permute-start.35 = (bf16[4,128,2048]{2,1,0:T(8,128)(2,1)}, bf16[4,128,2048]{2,1,0:T(8,128)(2,1)}, u32[]{:S(2)}, u32[]{:S(2)}) collective-permute-start(bf16[4,128,2048]{2,1,0:T(8,128)(2,1)} %bitcast.26), channel_id=1, source_target_pairs={{0,4},{1,5},{2,6},{3,7},{4,0},{5,1},{6,2},{7,3},{8,12},{9,13},{10,... | collective-permute-start | bytes 6291464 | tf_op jit(solution)/shard_map/ppermute | solution.py:343
  455.6 39.2 %collective-permute-start.34 = (bf16[256,2048]{1,0:T(8,128)(2,1)}, bf16[256,2048]{1,0:T(8,128)(2,1)}, u32[]{:S(2)}, u32[]{:S(2)}) collective-permute-start(bf16[256,2048]{1,0:T(8,128)(2,1)} %collective-permute-done.24.refs_6_), channel_id=1, source_target_pairs={{0,8},{1,9},{2,10},{3,11},{4,12},{5,13},{6,14},{7,15},{8,16},{9,17... | collective-permute-start | bytes 3145736 | tf_op jit(solution)/shard_map/ppermute | solution.py:347
  459.6 40.3 %collective-permute-start.38 = (bf16[128,2048]{1,0:T(8,128)(2,1)}, bf16[128,2048]{1,0:T(8,128)(2,1)}, u32[]{:S(2)}, u32[]{:S(2)}) collective-permute-start(bf16[128,2048]{1,0:T(8,128)(2,1)} %get-tuple-element.265), channel_id=1, source_target_pairs={{0,3},{1,2},{2,1},{3,0},{4,7},{5,6},{6,5},{7,4},{8,11},{9,10},{10,... | collective-permute-start | bytes 1572872 | tf_op jit(solution)/shard_map/ppermute | solution.py:343
  461.7 61.6 %collective-permute-start.40 = (bf16[256,2048]{1,0:T(8,128)(2,1)}, bf16[256,2048]{1,0:T(8,128)(2,1)}, u32[]{:S(2)}, u32[]{:S(2)}) collective-permute-start(bf16[256,2048]{1,0:T(8,128)(2,1)} %collective-permute-done.5.refs_1_), channel_id=1, source_target_pairs={{0,4},{1,5},{2,6},{3,7},{4,0},{5,1},{6,2},{7,3},{8,12},{9,13},{10,... | collective-permute-start | bytes 3145736 | tf_op jit(solution)/shard_map/ppermute | solution.py:343
  461.7 61.6 %collective-permute-start.41 = (bf16[256,2048]{1,0:T(8,128)(2,1)}, bf16[256,2048]{1,0:T(8,128)(2,1)}, u32[]{:S(2)}, u32[]{:S(2)}) collective-permute-start(bf16[256,2048]{1,0:T(8,128)(2,1)} %collective-permute-done.13.refs_2_), channel_id=1, source_target_pairs={{0,4},{1,5},{2,6},{3,7},{4,0},{5,1},{6,2},{7,3},{8,12},{9,13},{10,... | collective-permute-start | bytes 3145736 | tf_op jit(solution)/shard_map/ppermute | solution.py:343
  494.8 63.5 %all-to-all-start.4 = ((bf16[4,512,384]{2,1,0:T(8,128)(2,1)}), bf16[4,512,384]{2,1,0:T(8,128)(2,1)S(1)}, u32[]{:S(2)}, u32[]{:S(2)}) async-start(bf16[4,512,384]{2,1,0:T(8,128)(2,1)} %bitcast.149), calls=%async_computation.4 | async-start | bytes 3145728 | tf_op jit(solution)/shard_map/all_to_all | solution.py:355
  499.5 129.9 %reduce-scatter.2.cloned.1.call-start = ((), (), s32[]{:S(2)}) async-start(), calls=%async_computation.11 | async-start | bytes 2359296 | tf_op jit(solution)/shard_map/reduce_scatter | solution.py:1269
  563.1 66.3 %all-to-all-start.5 = ((bf16[4,512,768]{2,1,0:T(8,128)(2,1)}), bf16[4,512,768]{2,1,0:T(8,128)(2,1)}, u32[]{:S(2)}, u32[]{:S(2)}) async-start(bf16[4,512,768]{2,1,0:T(8,128)(2,1)} %copy-done.8), calls=%async_computation.5 | async-start | bytes 6291456 | tf_op jit(solution)/shard_map/all_to_all | solution.py:355
  568.0 134.9 %all-gather.12.cloned.1.call-start = ((), (), s32[]{:S(2)}) async-start(), calls=%async_computation.13 | async-start | bytes 3932160 | tf_op jit(solution)/shard_map/all_gather | solution.py:1289
  572.8 56.6 %collective-permute-start.46 = (bf16[256,384]{1,0:T(8,128)(2,1)}, bf16[256,384]{1,0:T(8,128)(2,1)}, u32[]{:S(2)}, u32[]{:S(2)}) collective-permute-start(bf16[256,384]{1,0:T(8,128)(2,1)} %bitcast.153), channel_id=1, source_target_pairs={{0,1},{1,0},{2,3},{3,2},{4,5},{5,4},{6,7},{7,6},{8,9},{9,8},{10,11... | collective-permute-start | bytes 589832 | tf_op jit(solution)/shard_map/ppermute | solution.py:343
  576.0 53.4 %collective-permute-start.47 = (bf16[256,384]{1,0:T(8,128)(2,1)}, bf16[256,384]{1,0:T(8,128)(2,1)}, u32[]{:S(2)}, u32[]{:S(2)}) collective-permute-start(bf16[256,384]{1,0:T(8,128)(2,1)} %bitcast.154), channel_id=1, source_target_pairs={{0,2},{1,3},{2,0},{3,1},{4,6},{5,7},{6,4},{7,5},{8,10},{9,11},{10,... | collective-permute-start | bytes 589832 | tf_op jit(solution)/shard_map/ppermute | solution.py:343
  579.3 50.1 %collective-permute-start.48 = (bf16[256,384]{1,0:T(8,128)(2,1)}, bf16[256,384]{1,0:T(8,128)(2,1)}, u32[]{:S(2)}, u32[]{:S(2)}) collective-permute-start(bf16[256,384]{1,0:T(8,128)(2,1)} %bitcast.155), channel_id=1, source_target_pairs={{0,3},{1,2},{2,1},{3,0},{4,7},{5,6},{6,5},{7,4},{8,11},{9,10},{10,... | collective-permute-start | bytes 589832 | tf_op jit(solution)/shard_map/ppermute | solution.py:343
  631.6 41.5 %all-to-all-start.6 = ((bf16[4,512,768]{2,1,0:T(8,128)(2,1)}), bf16[4,512,768]{2,1,0:T(8,128)(2,1)}, u32[]{:S(2)}, u32[]{:S(2)}) async-start(bf16[4,512,768]{2,1,0:T(8,128)(2,1)} %bitcast.40), calls=%async_computation.7 | async-start | bytes 6291456 | tf_op jit(solution)/shard_map/all_to_all | solution.py:355
  678.7 52.2 %collective-permute-start.57 = (bf16[4,512,768]{2,1,0:T(8,128)(2,1)}, bf16[4,512,768]{2,1,0:T(8,128)(2,1)}, u32[]{:S(2)}, u32[]{:S(2)}) collective-permute-start(bf16[4,512,768]{2,1,0:T(8,128)(2,1)} %all-to-all-done.6.own_ref), channel_id=1, source_target_pairs={{0,4},{1,5},{2,6},{3,7},{4,0},{5,1},{6,2},{7,3},{8,12},{9,13},{10,... | collective-permute-start | bytes 9437192 | tf_op jit(solution)/shard_map/ppermute | solution.py:343
  702.9 46.6 %collective-permute-start.59 = (bf16[4,4,256,384]{3,2,1,0:T(8,128)(2,1)}, bf16[4,4,256,384]{3,2,1,0:T(8,128)(2,1)}, u32[]{:S(2)}, u32[]{:S(2)}) collective-permute-start(bf16[4,4,256,384]{3,2,1,0:T(8,128)(2,1)} %bitcast.146), channel_id=1, source_target_pairs={{0,4},{1,5},{2,6},{3,7},{4,0},{5,1},{6,2},{7,3},{8,12},{9,13},{10,... | collective-permute-start | bytes 9437192 | tf_op jit(solution)/shard_map/ppermute | solution.py:343
  705.6 55.3 %all-to-all-start.7 = ((bf16[4,512,768]{2,1,0:T(8,128)(2,1)}), bf16[4,512,768]{2,1,0:T(8,128)(2,1)}, u32[]{:S(2)}, u32[]{:S(2)}) async-start(bf16[4,512,768]{2,1,0:T(8,128)(2,1)} %bitcast.138), calls=%async_computation.8 | async-start | bytes 6291456 | tf_op jit(solution)/shard_map/all_to_all | solution.py:355
  710.2 58.6 %all-gather.10.cloned.1.call-start = ((), (), s32[]{:S(2)}) async-start(), calls=%async_computation.12 | async-start | bytes 2359296 | tf_op jit(solution)/shard_map/all_gather | solution.py:1305
  (135 other events, 1608.0 us)
Sparse Core Ops, SparseCore 0:
  12.3 130.7 all-gather.5
  287.7 170.7 all-gather.7
  563.2 36.5 reduce-scatter.1
  631.7 65.1 all-gather.11
  712.4 33.4 all-gather.9
